TPU v7x, 256 devices: a whole 4x4x8 slice. The times are simulated.
256 devices in a mesh: row: 4 (over x_hi, core), col: 8 (over z), depth: 8 (over y, x_lo).
Axes of the slice: x: 4 (x_hi: 2, x_lo: 2; x = x_hi * 2 + x_lo), y: 4, z: 8, core: 2. Of those that a mesh axis runs over, the one named last changes fastest.
Arguments:
- block_values: bfloat16 [192, 16, 128, 128], P(('row', 'depth'), 'col'), may hold values from -1.1953125 to 1.1953125
- block_columns: int32 [192, 16], P(('row', 'depth'), 'col'), may hold values from -1 to 23, as said below
- pattern_columns: int32 [192, 24], P('row', 'col'), may hold values from 0 to 23, as said below
Outputs:
- next_values: bfloat16 [192, 24, 128, 128], P(('row', 'depth'), 'col')
Inputs may be any that keep to these rules, and one draw needn't show every extreme that they name: `block_columns`: in each block row and panel the 2 slots first list distinct block columns of that panel, numbered from 0 within it, then hold -1; at least one slot is used; the listed columns are the first entries of pattern_columns in that block row and panel, in the same order. `pattern_columns`: in each block row and panel the 3 entries are distinct block columns of that panel, numbered from 0 within it.
All inputs are finite; a program needn't handle non-finite values.
Results may differ from a plain program's by a relative error of at most 0.012.
Values may be sent and summed in bfloat16 or wider, within the bound.
No kernel may reach another device: no remote copies, remote signals or barrier semaphores. Data moves between devices by JAX's collectives and lax.ppermute only.
A program may use at most 128 MiB of HBM per device.

v0:
```python
import math

import jax
import jax.numpy as jnp
from jax import lax
from jax.sharding import PartitionSpec as P

NB = 192
KA = 2
KC = 3


def spread(array, axis, root):
    mine = lax.axis_index(axis) == root
    return lax.psum(jnp.where(mine, array, jnp.zeros_like(array)), axis)


def panel_product(left_values, left_columns, right_values, right_columns, pattern, right_slots):
    total_rows = left_values.shape[0]
    batch_rows = math.gcd(total_rows, 8)
    batches = total_rows // batch_rows
    right_panel = jnp.arange(right_columns.shape[1], dtype=jnp.int32) // right_slots
    out_panel = jnp.arange(pattern.shape[1], dtype=jnp.int32) // KC
    same_panel = right_panel[None, :] == out_panel[:, None]

    def one_batch(pieces):
        values, columns, wanted = pieces
        present = columns >= 0
        source_rows = jnp.maximum(columns, 0)
        chosen_values = jnp.take(right_values, source_rows, axis=0)
        chosen_columns = jnp.take(right_columns, source_rows, axis=0)
        matches = (
            (chosen_columns[:, :, None, :] == wanted[:, None, :, None])
            & same_panel[None, None, :, :]
            & present[:, :, None, None]
        )
        combined = jnp.einsum(
            "isut,istxy->isuxy",
            matches.astype(jnp.bfloat16),
            chosen_values,
            preferred_element_type=jnp.bfloat16,
        )
        return jnp.einsum("isxy,isuyz->iuxz", values, combined, preferred_element_type=jnp.float32)

    result = lax.map(
        one_batch,
        (
            left_values.reshape((batches, batch_rows) + left_values.shape[1:]),
            left_columns.reshape((batches, batch_rows, left_columns.shape[1])),
            pattern.reshape((batches, batch_rows, pattern.shape[1])),
        ),
    )
    return result.reshape((total_rows,) + result.shape[2:])


def local(block_values, block_columns, pattern_columns):
    row_devices = lax.axis_size("row")
    col_devices = lax.axis_size("col")
    depth_devices = lax.axis_size("depth")
    panel_total = max(row_devices, col_devices, depth_devices)
    panel_span = NB // panel_total
    panels_per_col = panel_total // col_devices
    panels_per_row = panel_total // row_devices
    panels_per_layer = panel_total // depth_devices
    depth_index = lax.axis_index("depth")
    col_index = lax.axis_index("col")
    gathered_values, gathered_columns = (
        lax.all_gather(block_values, ("col", "depth"), axis=0, tiled=True),
        lax.all_gather(block_columns, ("col", "depth"), axis=0, tiled=True),
    )
    group_rows = gathered_values.shape[0] // col_devices
    stacked_values = gathered_values.reshape((col_devices, group_rows) + gathered_values.shape[1:])
    stacked_columns = gathered_columns.reshape((col_devices, group_rows, gathered_columns.shape[1]))
    tile_values = lax.dynamic_index_in_dim(stacked_values, col_index, 0, keepdims=False)
    tile_columns = lax.dynamic_index_in_dim(stacked_columns, col_index, 0, keepdims=False)

    def fetch_left(panel_index):
        owner_col = panel_index // panels_per_col
        owner_values = lax.dynamic_index_in_dim(stacked_values, owner_col, 0, keepdims=False)
        owner_columns = lax.dynamic_index_in_dim(stacked_columns, owner_col, 0, keepdims=False)
        return (owner_values, owner_columns)

    def fetch_right(values, columns, panel_index):
        first_row = panel_index % panels_per_row * panel_span
        return (
            spread(
                lax.dynamic_slice_in_dim(values, first_row, panel_span, 0),
                "row",
                panel_index // panels_per_row,
            ),
            spread(
                lax.dynamic_slice_in_dim(columns, first_row, panel_span, 0),
                "row",
                panel_index // panels_per_row,
            ),
        )

    panel_list = [depth_index * panels_per_layer + 0]
    left_list = [fetch_left(panel_index) for panel_index in panel_list]
    term_shape = pattern_columns.shape + block_values.shape[2:]
    square_terms = jnp.zeros(term_shape, jnp.float32)
    for panel_index, left_pair in zip(panel_list, left_list):
        right_values, right_columns = fetch_right(tile_values, tile_columns, panel_index)
        square_terms = panel_product(
            left_pair[0], left_pair[1], right_values, right_columns, pattern_columns, KA
        )
    square = lax.psum(square_terms.astype(jnp.bfloat16), "depth")
    cube_terms = jnp.zeros(term_shape, jnp.float32)
    for panel_index, left_pair in zip(panel_list, left_list):
        right_values, right_columns = fetch_right(square, pattern_columns, panel_index)
        cube_terms = panel_product(
            left_pair[0], left_pair[1], right_values, right_columns, pattern_columns, KC
        )
    cube_sum = lax.psum_scatter(
        cube_terms.astype(jnp.bfloat16), "depth", scatter_dimension=0, tiled=True
    ).astype(jnp.float32)
    own_rows = block_values.shape[0]
    own_pattern = lax.dynamic_slice_in_dim(pattern_columns, depth_index * own_rows, own_rows, 0)
    slot_panel = jnp.arange(block_columns.shape[1], dtype=jnp.int32) // KA
    out_panel = jnp.arange(own_pattern.shape[1], dtype=jnp.int32) // KC
    matched = (
        (block_columns[:, None, :] == own_pattern[:, :, None])
        & (slot_panel[None, None, :] == out_panel[None, :, None])
        & (block_columns >= 0)[:, None, :]
    )
    mapped = jnp.einsum(
        "ius,isxy->iuxy",
        matched.astype(jnp.bfloat16),
        block_values,
        preferred_element_type=jnp.float32,
    )
    return (1.5 * mapped - 0.5 * cube_sum).astype(jnp.bfloat16)


def solution(mesh):
    placed = (P(("row", "depth"), "col", None, None), P(("row", "depth"), "col"), P("row", "col"))
    return jax.shard_map(
        local,
        mesh=mesh,
        in_specs=placed,
        out_specs=P(("row", "depth"), "col", None, None),
        check_vma=False,
    )
```

profile of v0, /device:TPU:1, one launch (start us, length us, event | category | flops | bytes accessed | tf_op | source)
XLA Modules:
  0.0 1233.9 jit_solution(7291518584452857572)
XLA Ops:
  7.3 552.3 %all-gather.3.cloned.1.call-done = bf16[384,2,128,128]{3,2,1,0:T(8,128)(2,1)} async-done(((bf16[6,2,128,128]{3,2,1,0:T(8,128)(2,1)}), bf16[384,2,128,128]{3,2,1,0:T(8,128)(2,1)}) %all-gather.3.cloned.1.call-update) | async-done | bytes 25165840 | tf_op jit(solution)/shard_map/all_gather | solution.py:68
  559.6 2.7 select_bitcast_fusion
  562.4 126.6 %all-gather = s32[64,6,2]{1,2,0:T(2,128)S(1)} all-gather(s32[1,6,2]{1,2,0:T(2,128)S(1)} %bitcast.108), channel_id=1, replica_groups=mesh['row'=4,'col'=8,'depth'=8] {'col','depth'}, dimensions={0}, use_global_device_ids=true | all-gather | bytes 3120 | tf_op jit(solution)/shard_map/all_gather | solution.py:69
  689.4 41.8 %all-reduce = (s32[24,3]{1,0:T(8,128)S(1)}, s32[24,2]{0,1:T(2,128)S(1)}) all-reduce(s32[24,3]{1,0:T(8,128)S(1)} %broadcast_select_fusion.4, s32[24,2]{0,1:T(2,128)S(1)} %bitcast.109), channel_id=1, replica_groups=mesh['row'=4,'col'=8,'depth'=8] {'row'}, use_global_device_ids=true, to_apply=%region_6.7 | all-reduce | flops 120 | bytes 960 | tf_op jit(solution)/shard_map/psum | solution.py:15
  731.4 4.0 constant_dynamic-slice_fusion.2
  735.5 3.3 broadcast.279.clone
  738.8 41.5 %while.22 = (s32[]{:T(128)}, bf16[6,8,3,128,128]{3,4,2,1,0:T(8,128)(2,1)}, s32[6,8,2]{1,2,0:T(2,128)S(1)}, s32[24,2]{1,0:T(8,128)S(1)}, s32[6,8,3]{1,2,0:T(4,128...) while((s32[]{:T(128)}, ...), condition=%wide.region_3.4_spmd.clone, body=%wide.region_2.3_spmd.clone.sunk | while | flops 204998000 | bytes 8396221 | solution.py:45
  743.0 2.6 bitcast_dynamic-update-slice_fusion.4
  750.0 2.6 bitcast_dynamic-update-slice_fusion.4
  756.9 2.6 bitcast_dynamic-update-slice_fusion.4
  763.8 2.6 bitcast_dynamic-update-slice_fusion.4
  770.7 2.6 bitcast_dynamic-update-slice_fusion.4
  777.6 2.6 bitcast_dynamic-update-slice_fusion.4
  780.2 6.7 copy.118
  787.0 203.9 %all-reduce.7.cloned.1.call-done = bf16[48,3,128,128]{3,2,1,0:T(8,128)(2,1)} async-done(((bf16[48,3,128,128]{3,2,1,0:T(8,128)(2,1)}), bf16[48,3,128,128]{3,2,1,0:T(8,128)(2,1)}) %all-reduce.7.cloned.1.call-update) | async-done | bytes 4718608 | tf_op jit(solution)/shard_map/psum | solution.py:107
  990.9 3.2 dynamic-slice_select_fusion
  994.2 69.2 %all-reduce.9.cloned.1.call-done = bf16[24,3,128,128]{3,2,1,0:T(8,128)(2,1)} async-done(((bf16[24,3,128,128]{3,2,1,0:T(8,128)(2,1)}), bf16[24,3,128,128]{3,2,1,0:T(8,128)(2,1)}) %all-reduce.9.cloned.1.call-update) | async-done | bytes 2359312 | tf_op jit(solution)/shard_map/psum | solution.py:15
  1063.4 3.4 broadcast.279
  1066.7 49.3 %while.23 = (s32[]{:T(128)}, bf16[6,8,3,128,128]{3,4,2,1,0:T(8,128)(2,1)}, s32[6,8,2]{1,2,0:T(2,128)S(1)}, s32[24,3]{1,0:T(8,128)S(1)}, s32[6,8,3]{1,2,0:T(4,128...) while((s32[]{:T(128)}, ...), condition=%wide.region_8.9_spmd.clone, body=%wide.region_7.8_spmd.clone.sunk | while | flops 206833184 | bytes 9969651 | solution.py:45
  1067.8 2.5 gather_fusion.2
  1072.3 2.6 bitcast_dynamic-update-slice_fusion.5
  1076.0 2.5 gather_fusion.2
  1080.5 2.6 bitcast_dynamic-update-slice_fusion.5
  1084.2 2.5 gather_fusion.2
  1088.7 2.6 bitcast_dynamic-update-slice_fusion.5
  1092.4 2.5 gather_fusion.2
  1096.9 2.6 bitcast_dynamic-update-slice_fusion.5
  1100.6 2.5 gather_fusion.2
  1105.0 2.7 bitcast_dynamic-update-slice_fusion.5
  1113.3 2.7 bitcast_dynamic-update-slice_fusion.5
  1116.0 6.6 copy.121
  1124.4 100.8 %reduce-scatter.2.cloned.1.call-done = bf16[6,3,128,128]{3,2,1,0:T(8,128)(2,1)} async-done(((bf16[48,3,128,128]{3,2,1,0:T(8,128)(2,1)}), bf16[6,3,128,128]{3,2,1,0:T(8,128)(2,1)}) %reduce-scatter.2.cloned.1.call-update) | async-done | bytes 589840 | tf_op jit(solution)/shard_map/reduce_scatter | solution.py:114
  (216 shorter events, 51.6 us)
Async XLA Ops:
  6.5 553.1 %all-gather.3.cloned.1.call-start = ((), (), s32[]{:S(2)}) async-start(), calls=%async_computation.1 | async-start | bytes 25559040 | tf_op jit(solution)/shard_map/all_gather | solution.py:68
  7.3 728.2 %all-reduce.5.cloned.1.call-start = ((), (), s32[]{:S(2)}) async-start(), calls=%async_computation.2 | async-start | bytes 3145728 | tf_op jit(solution)/shard_map/psum | solution.py:15
  559.6 2.8 copy-start.3
  559.6 129.4 %copy-start.2 = (s32[48,3]{0,1:T(4,128)S(1)}, s32[48,3]{0,1:T(4,128)}, u32[]{:S(2)}) copy-start(s32[48,3]{0,1:T(4,128)} %param.9) | copy-start | bytes 1732
  562.3 428.5 %all-reduce.7.cloned.1.call-start = ((), (), s32[]{:S(2)}) async-start(), calls=%async_computation.3 | async-start | bytes 9437184 | tf_op jit(solution)/shard_map/psum | solution.py:107
  735.5 3.3 copy-start
  787.0 276.4 %all-reduce.9.cloned.1.call-start = ((), (), s32[]{:S(2)}) async-start(), calls=%async_computation.4 | async-start | bytes 4718592 | tf_op jit(solution)/shard_map/psum | solution.py:15
  994.2 231.1 %reduce-scatter.2.cloned.1.call-start = ((), (), s32[]{:S(2)}) async-start(), calls=%async_computation.5 | async-start | bytes 5308416 | tf_op jit(solution)/shard_map/reduce_scatter | solution.py:114
  1122.6 1.0 copy-start.1
Sparse Core Ops, SparseCore 0:
  9.1 550.4 all-gather.2
  562.5 58.8 all-reduce.4
  787.1 203.7 all-reduce.6
  994.3 69.0 all-reduce.8
  1122.8 102.4 reduce-scatter.1
where the time goes:
time: 1240 us; the launch traced here: 1230 us
  waiting for transfers between devices  927 us (75%)
  blocking collectives  168 us (14%)
  local copies, waits for them, and re-layouts  60.4 us (5%)
  matrix products  55.2 us (4%)
  between operations  13.2 us (1%)
    all_gather x1, waiting for transfers between devices, local(): lax.all_gather(block_values, ('col', 'depth'), axis=0, tiled=True)  552 us
    psum x1, waiting for transfers between devices, local(): square = lax.psum(square_terms.astype(jnp.bfloat16), 'depth')  204 us
    all_gather x1, blocking collectives, local(): lax.all_gather(block_columns, ('col', 'depth'), axis=0, tiled=True)  127 us
    reduce_scatter x1, waiting for transfers between devices, local(): lax.psum_scatter(cube_terms.astype(jnp.bfloat16), 'depth', scatter_dimens...  101 us
    psum x2, waiting for transfers between devices, spread(): return lax.psum(jnp.where(mine, array, jnp.zeros_like(array)), axis)  69.2 us
    psum x1, blocking collectives, spread(): return lax.psum(jnp.where(mine, array, jnp.zeros_like(array)), axis)  41.8 us
    dot_general x12, matrix products, one_batch(): jnp.einsum('isxy,isuyz->iuxz', values, combined, preferred_element_type=j...  31.7 us
  transfers between devices with their start and end apart: 5, of which 4 were waited for; matrix products, arithmetic and copies ran while one was open for 0% of the time, Pallas kernels for 0%

commit v1 on v0

v1 whole, which is shorter than its diff:
```python
import functools

import jax
import jax.numpy as jnp
from jax import lax
from jax.experimental import pallas as pl
from jax.experimental.pallas import tpu as pltpu
from jax.sharding import PartitionSpec as P

BLK = 128
KA = 2
KC = 3
TP = 24
ROWS = 6
PAY = ROWS * KA * BLK + 16
SROWS = ROWS * KC * BLK
HELD = 96
SLOTS = 48
ALL = ("row", "col", "depth")


def chip_of(device):
    row, col, depth = device // 64, device // 8 % 8, device % 8
    return row // 2 * 2 + depth % 2, depth // 2, col, row % 2


def device_of(x, y, z, core):
    return (x // 2 * 2 + core) * 64 + z * 8 + y * 2 + x % 2


def moves(rule):
    pairs = []
    for device in range(256):
        x, y, z, core = rule(*chip_of(device))
        pairs.append((device, device_of(x % 4, y % 4, z, core)))
    return pairs


def first_ring(step):
    return moves(lambda x, y, z, core: (x + step * (1 - core), y + step * core, z, core))


def second_ring(step):
    return moves(lambda x, y, z, core: (x + step * core, y + step * (1 - core), z, core))


def swap(array):
    return lax.ppermute(array, ALL, moves(lambda x, y, z, core: (x, y, z, 1 - core)))


def plane_gather(piece):
    ring = [piece] + [lax.ppermute(piece, ALL, first_ring(step)) for step in (1, -1, 2)]
    near = jnp.concatenate(ring, axis=0)
    half = near.shape[0] // 2
    plus = lax.ppermute(near, ALL, second_ring(1))
    minus = lax.ppermute(near, ALL, second_ring(-1))
    far_a = lax.ppermute(plus[:half], ALL, second_ring(1))
    far_b = lax.ppermute(minus[half:], ALL, second_ring(-1))
    return near, plus, minus, far_a, far_b


def product_kernel(
    slots, piece_rows, core_ref, place_ref, have_ref, want_ref, right_ref, find_ref,
    own_ref, other_ref, near_ref, plus_ref, minus_ref, fara_ref, farb_ref,
    mine_out, theirs_out, total, left_buf, right_buf, todo, count, sems,
):
    core = core_ref[0]
    count[0] = 0

    def wait(n):
        slot = lax.rem(n, SLOTS)
        pltpu.make_async_copy(own_ref.at[pl.ds(0, BLK)], left_buf.at[slot], sems.at[0, slot]).wait()
        pltpu.make_async_copy(own_ref.at[pl.ds(0, BLK)], right_buf.at[slot], sems.at[1, slot]).wait()

    def start(n):
        slot = lax.rem(n, SLOTS)
        entry = todo[0, n]
        row, spot = entry // 8, lax.rem(entry, 8)
        panel, side = spot // 2, lax.rem(spot, 2)

        def left(ref, offset):
            offset = pl.multiple_of(offset, 16)
            pltpu.make_async_copy(ref.at[pl.ds(offset, BLK)], left_buf.at[slot], sems.at[0, slot]).start()

        @pl.when(row < ROWS)
        def _():
            whole = panel // 2 * 4 + 2 * core + lax.rem(panel, 2)
            left(own_ref, whole * PAY + (row * KA + side) * BLK)

        @pl.when(row >= ROWS)
        def _():
            left(other_ref, panel * PAY + ((row - ROWS) * KA + side) * BLK)

        place = todo[1, n]
        group, line = place // ROWS, lax.rem(place, ROWS)
        outer, inner = group // 4, lax.rem(group, 4)
        block = (line * slots + todo[2, n]) * BLK

        def right(ref, offset):
            offset = pl.multiple_of(offset, 16)
            pltpu.make_async_copy(ref.at[pl.ds(offset, BLK)], right_buf.at[slot], sems.at[1, slot]).start()

        for index, ref in enumerate((near_ref, plus_ref, minus_ref)):
            pl.when(outer == index)(functools.partial(right, ref, inner * piece_rows + block))
        pl.when((outer == 3) & (inner < 2))(functools.partial(right, fara_ref, inner * piece_rows + block))
        pl.when((outer == 3) & (inner >= 2))(functools.partial(right, farb_ref, (inner - 2) * piece_rows + block))

    def scan_row(row, carry):
        for spot in range(8):
            entry = row * 8 + spot
            place = place_ref[entry]

            @pl.when((have_ref[place] & want_ref[row]) != 0)
            def _():
                for slot in range(slots):
                    column = right_ref[place * slots + slot]
                    found = find_ref[row * TP + jnp.maximum(column, 0)]

                    @pl.when((column >= 0) & (found >= 0))
                    def _():
                        n = count[0]
                        todo[0, n] = entry
                        todo[1, n] = place
                        todo[2, n] = slot
                        todo[3, n] = row * KC + found
                        count[0] = n + 1
                        pl.when(n < SLOTS)(functools.partial(start, n))

        return carry

    lax.fori_loop(0, 2 * ROWS, scan_row, 0)
    total[...] = jnp.zeros_like(total)
    found = count[0]

    def multiply(n, carry):
        wait(n)
        slot = lax.rem(n, SLOTS)
        out = todo[3, n]
        total[out] += jnp.dot(left_buf[slot], right_buf[slot], preferred_element_type=jnp.float32)
        pl.when(n + SLOTS < found)(functools.partial(start, n + SLOTS))
        return carry

    lax.fori_loop(0, found, multiply, 0)
    for block in range(ROWS * KC):
        mine_out[pl.ds(block * BLK, BLK), :] = total[block]
        theirs_out[pl.ds(block * BLK, BLK), :] = total[ROWS * KC + block].astype(jnp.bfloat16)


def product(slots, piece_rows, tables, arrays):
    smem = pl.BlockSpec(memory_space=pltpu.SMEM)
    hbm = pl.BlockSpec(memory_space=pl.ANY)
    vmem = pl.BlockSpec(memory_space=pltpu.VMEM)
    return pl.pallas_call(
        functools.partial(product_kernel, slots, piece_rows),
        out_shape=(
            jax.ShapeDtypeStruct((SROWS, BLK), jnp.float32),
            jax.ShapeDtypeStruct((SROWS, BLK), jnp.bfloat16),
        ),
        in_specs=[smem] * len(tables) + [hbm] * len(arrays),
        out_specs=(vmem, vmem),
        scratch_shapes=[
            pltpu.VMEM((2 * ROWS * KC, BLK, BLK), jnp.float32),
            pltpu.VMEM((SLOTS, BLK, BLK), jnp.bfloat16),
            pltpu.VMEM((SLOTS, BLK, BLK), jnp.bfloat16),
            pltpu.SMEM((4, 2 * ROWS * 8 * KC), jnp.int32),
            pltpu.SMEM((1,), jnp.int32),
            pltpu.SemaphoreType.DMA((2, SLOTS)),
        ],
        compiler_params=pltpu.CompilerParams(vmem_limit_bytes=24 * 1024 * 1024),
    )(*tables, *arrays)


def bits(columns):
    return jnp.sum(jnp.where(columns >= 0, 1 << jnp.maximum(columns, 0), 0), axis=-1, dtype=jnp.int32)


def local(block_values, block_columns, pattern_columns):
    row, depth = lax.axis_index("row"), lax.axis_index("depth")
    core, x, y = row % 2, row // 2 * 2 + depth % 2, depth // 2
    own_pattern = lax.dynamic_slice_in_dim(pattern_columns, depth * ROWS, ROWS, 0)

    marks = jnp.concatenate([block_columns.reshape(1, -1), own_pattern.reshape(1, -1)], axis=1)
    marks = jnp.pad(marks.astype(jnp.bfloat16), ((0, 15), (0, BLK - marks.shape[1])))
    piece = jnp.concatenate([block_values.reshape(ROWS * KA * BLK, BLK), marks], axis=0)

    left = lax.all_gather(piece, "col", axis=0, tiled=True)
    right = plane_gather(piece)
    wanted = jnp.concatenate([own_pattern, swap(own_pattern)], axis=0)

    by_core = left.reshape(2, 2, 2, PAY, BLK)
    left_other = swap(lax.dynamic_index_in_dim(by_core, 1 - core, 1, keepdims=False).reshape(4 * PAY, BLK))

    def marks_of(array):
        return array.reshape(-1, PAY, BLK)[:, ROWS * KA * BLK, :].astype(jnp.int32)

    own_marks = lax.dynamic_index_in_dim(marks_of(left).reshape(2, 2, 2, BLK), core, 1, keepdims=False)
    left_marks = jnp.stack([own_marks.reshape(4, BLK), marks_of(left_other)])[:, :, : ROWS * KA]
    left_columns = left_marks.reshape(2, 4, ROWS, KA).transpose(0, 2, 1, 3).reshape(2 * ROWS, 4, KA)

    panel, column = jnp.arange(4)[:, None], jnp.arange(TP)[None, :]
    away_x = (x - (panel // 2 * 2 + column // ROWS % 2)) % 4
    away_y = (y - (panel % 2 * 2 + column // 12)) % 4
    order = lambda away: jnp.where(away == 2, 3, jnp.where(away == 3, 2, away))
    away_x, away_y = order(away_x), order(away_y)
    group = jnp.where(core == 0, away_y * 4 + away_x, away_x * 4 + away_y)
    held_at = (group * ROWS + column % ROWS).astype(jnp.int32)
    hit = left_columns[:, :, :, None] == jnp.arange(TP)
    place = jnp.sum(jnp.where(hit, held_at[None, :, None, :], 0), axis=-1)
    place = jnp.where(left_columns >= 0, place, HELD).reshape(-1).astype(jnp.int32)

    right_marks = jnp.concatenate([marks_of(part) for part in right], axis=0)
    x_columns = right_marks[:, : ROWS * KA].reshape(HELD, KA)
    s_columns = right_marks[:, ROWS * KA : ROWS * (KA + KC)].reshape(HELD, KC)
    find = sum(jnp.where(wanted[:, u : u + 1] == jnp.arange(TP), u + 1, 0) for u in range(KC)) - 1
    want = bits(wanted)
    core_table = core.reshape(1).astype(jnp.int32)

    def tables(columns):
        have = jnp.pad(bits(columns), (0, 1))
        return core_table, place, have, want, columns.reshape(-1), find.reshape(-1).astype(jnp.int32)

    mine, theirs = product(KA, PAY, tables(x_columns), (left, left_other) + right)
    square = (mine + swap(theirs).astype(jnp.float32)).astype(jnp.bfloat16)
    mine, theirs = product(KC, SROWS, tables(s_columns), (left, left_other) + plane_gather(square))
    cube = (mine + swap(theirs).astype(jnp.float32)).reshape(ROWS, KC, BLK, BLK)
    stored = jnp.where((block_columns >= 0)[:, :, None, None], block_values, 0).astype(jnp.float32)
    mapped = jnp.pad(stored, ((0, 0), (0, KC - KA), (0, 0), (0, 0)))
    return (1.5 * mapped - 0.5 * cube).astype(jnp.bfloat16)


def solution(mesh):
    placed = (P(("row", "depth"), "col", None, None), P(("row", "depth"), "col"), P("row", "col"))
    return jax.shard_map(
        local,
        mesh=mesh,
        in_specs=placed,
        out_specs=P(("row", "depth"), "col", None, None),
        check_vma=False,
    )
```

time: 1240 us -> 214 us (0.17)
  waiting for transfers between devices: 927 us -> 95.7 us
  blocking collectives: 168 us -> 0 us
  matrix products: 55.2 us -> 0 us
  starting transfers between devices: 0.17 us -> 33.8 us
  local copies, waits for them, and re-layouts: 60.4 us -> 27 us
  Pallas kernels: 0 us -> 21.8 us
  other arithmetic: 9.33 us -> 21.8 us
    all_gather x1, waiting for transfers between devices: 552 us -> 26.7 us  [local(): left = lax.all_gather(piece, 'col', axis=0, tiled=True)]
    psum x3 -> x0, waiting for transfers between devices: 273 us -> none  [the longest x1 204 us: local(): square = lax.psum(square_terms.astype(jnp.bfloat16), 'depth')]
    all_gather x1 -> x0, blocking collectives: 127 us -> none  [local(): lax.all_gather(block_columns, ('col', 'depth'), axis=0, tiled=True)]
    reduce_scatter x1 -> x0, waiting for transfers between devices: 101 us -> none  [local(): lax.psum_scatter(cube_terms.astype(jnp.bfloat16), 'depth', scatter_dimens...]
    ppermute x0 -> x18, waiting for transfers between devices: none -> 69 us  [the longest x2 26.4 us: plane_gather(): plus = lax.ppermute(near, ALL, second_ring(1))]
    dot_general x25 -> x0, matrix products: 55.2 us -> none  [the longest x12 31.7 us: one_batch(): jnp.einsum('isxy,isuyz->iuxz', values, combined, preferred_element_type=j...]
    psum x1 -> x0, blocking collectives: 41.8 us -> none  [spread(): return lax.psum(jnp.where(mine, array, jnp.zeros_like(array)), axis)]
    ppermute x0 -> x18, starting transfers between devices: none -> 33.8 us  [the longest x4 12.3 us: swap(): lax.ppermute(array, ALL, moves(lambda x, y, z, core: (x, y, z, 1 - core)))]
  transfers between devices with their start and end apart: 5 -> 19, of which waited for: 4 -> 14; matrix products, arithmetic and copies ran while one was open for 0% -> 8% of each run, Pallas kernels for 0% -> 0%
where the time goes in v1:
time: 214 us
  waiting for transfers between devices  95.7 us (45%)
  starting transfers between devices  33.8 us (16%)
  local copies, waits for them, and re-layouts  27 us (13%)
  other arithmetic  21.8 us (10%)
  Pallas kernels  21.8 us (10%)
  between operations  13.6 us (6%)
    all_gather x1, waiting for transfers between devices, local(): left = lax.all_gather(piece, 'col', axis=0, tiled=True)  26.7 us
    ppermute x2, waiting for transfers between devices, plane_gather(): plus = lax.ppermute(near, ALL, second_ring(1))  26.4 us
    pallas_call x2, Pallas kernels, product(): pl.pallas_call(functools.partial(product_kernel, slots, piece_rows), out_...  21.8 us
    ppermute x6, waiting for transfers between devices, plane_gather(): lax.ppermute(piece, ALL, first_ring(step))  20.4 us
    ppermute x2, waiting for transfers between devices, plane_gather(): far_a = lax.ppermute(plus[:half], ALL, second_ring(1))  16.7 us
    concatenate x1, other arithmetic, plane_gather(): near = jnp.concatenate(ring, axis=0)  13.1 us
    ppermute x4, starting transfers between devices, swap(): lax.ppermute(array, ALL, moves(lambda x, y, z, core: (x, y, z, 1 - core)))  12.3 us
    unnamed x23, local copies, waits for them, and re-layouts  10.8 us
  transfers between devices with their start and end apart: 19, of which 14 were waited for; matrix products, arithmetic and copies ran while one was open for 8% of the time, Pallas kernels for 0%

profile of v1, /device:TPU:1, one launch (start us, length us, event | category | flops | bytes accessed | tf_op | source)
XLA Modules:
  0.0 213.7 jit_solution(18337060852029482464)
XLA Ops:
  7.5 1.8 constant_dynamic-update-slice_fusion.4
  10.8 1.8 pad_maximum_fusion.1
  12.6 2.2 %collective-permute-start.1 = (bf16[1552,128]{1,0:T(8,128)(2,1)}, bf16[1552,128]{1,0:T(8,128)(2,1)S(1)}, u32[]{:S(2)}, u32[]{:S(2)}) collective-permute-start(bf16[1552,128]{1,0:T(8,128)(2,1)} %pad_maximum_fusion.1), channel_id=1, source_target_pairs={{0,1},{1,128},{2,3},{3,130},{4,5},{5,132},{6,7},{7,134},{8,9},{9,1... | collective-permute-start | bytes 1191944 | tf_op jit(solution)/shard_map/ppermute | solution.py:52
  14.8 1.5 collective-permute-start.2
  16.3 1.6 collective-permute-start.3
  17.9 4.1 %collective-permute-done.1 = bf16[1552,128]{1,0:T(8,128)(2,1)S(1)} collective-permute-done((bf16[1552,128]{1,0:T(8,128)(2,1)}, bf16[1552,128]{1,0:T(8,128)(2,1)S(1)}, u32[]{:S(2)}, u32[]{:S(2)}) %collective-permute-start.1) | collective-permute-done | bytes 397344 | tf_op jit(solution)/shard_map/ppermute | solution.py:52
  22.8 3.0 %collective-permute-done.2 = bf16[1552,128]{1,0:T(8,128)(2,1)S(1)} collective-permute-done((bf16[1552,128]{1,0:T(8,128)(2,1)}, bf16[1552,128]{1,0:T(8,128)(2,1)S(1)}, u32[]{:S(2)}, u32[]{:S(2)}) %collective-permute-start.2) | collective-permute-done | bytes 397344 | tf_op jit(solution)/shard_map/ppermute | solution.py:52
  29.1 1.8 collective-permute-start.5
  30.9 4.2 %collective-permute-start.8 = (s32[6,3]{0,1:T(4,128)S(1)}, s32[6,3]{0,1:T(4,128)S(1)}, u32[]{:S(2)}, u32[]{:S(2)}) collective-permute-start(s32[6,3]{0,1:T(4,128)S(1)} %get-tuple-element.16), channel_id=1, source_target_pairs={{0,64},{1,65},{2,66},{3,67},{4,68},{5,69},{6,70},{7,71},{8,72},{9,... | collective-permute-start | bytes 224 | tf_op jit(solution)/shard_map/ppermute | solution.py:48
  35.0 26.7 %all-gather.2.cloned.1.call-done.own_ref = bf16[12416,128]{1,0:T(8,128)(2,1)} async-done(((bf16[1552,128]{1,0:T(8,128)(2,1)}), bf16[12416,128]{1,0:T(8,128)(2,1)}) %all-gather.2.cloned.1.call-update) | async-done | bytes 3178512 | tf_op jit(solution)/shard_map/all_gather | solution.py:186
  61.7 2.6 %constant_dynamic-slice_fusion = bf16[2,1,2,1552,128]{4,3,2,1,0:T(8,128)(2,1)} fusion(bf16[2,2,2,1552,128]{4,3,2,1,0:T(8,128)(2,1)} %bitcast.43, s32[]{:T(128)S(6)} %select_n.198), kind=kLoop, calls=%fused_computation.65 | loop fusion | bytes 3178500 | tf_op jit(solution)/shard_map/jit(dynamic_index_in_dim)/dynamic_slice | solution.py:191
  65.2 2.2 %slice.73 = bf16[3104,128]{1,0:T(8,128)(2,1)} slice(bf16[6208,128]{1,0:T(8,128)(2,1)} %collective-permute-done.4.plus_ref), slice={[0:3104], [0:128]} | slice | bytes 1589248 | tf_op jit(solution)/shard_map/slice | solution.py:57
  68.7 2.1 slice.75
  74.7 5.5 %collective-permute-done.6.fara_ref = bf16[3104,128]{1,0:T(8,128)(2,1)} collective-permute-done((bf16[3104,128]{1,0:T(8,128)(2,1)}, bf16[3104,128]{1,0:T(8,128)(2,1)}, u32[]{:S(2)}, u32[]{:S(2)}) %collective-permute-start.6) | collective-permute-done | bytes 794656 | tf_op jit(solution)/shard_map/ppermute | solution.py:57
  85.6 8.6 %shard_map.37 = (f32[2304,128]{1,0:T(8,128)S(1)}, bf16[2304,128]{1,0:T(8,128)(2,1)S(1)}) custom-call(s32[1]{0:T(128)} %bitcast.core_ref, s32[96]{0:T(128)S(1)} %broadcast_select_fusion.1.place_ref, s32[97]{0:T(128)S(1)} %pad.22.have_ref, s32[12]{0:T(128)S(1)} %get-tuple-element.13.want_ref, s32[192]{0:T(256)S(1)} %reshape_reshape.7.right_ref, ...), custom_call_target="tpu_custom_call" | custom-call | tf_op jit(solution)/shard_map/pallas_call | solution.py:153
  95.3 1.6 collective-permute-done.9
  97.9 1.9 collective-permute-start.11
  99.8 2.2 %collective-permute-start.12 = (bf16[2304,128]{1,0:T(8,128)(2,1)S(1)}, bf16[2304,128]{1,0:T(8,128)(2,1)S(1)}, u32[]{:S(2)}, u32[]{:S(2)}) collective-permute-start(bf16[2304,128]{1,0:T(8,128)(2,1)S(1)} %add_convert_fusion), channel_id=1, source_target_pairs={{0,128},{1,129},{2,130},{3,131},{4,132},{5,133},{6,134},{7,135},{8... | collective-permute-start | bytes 1769480 | tf_op jit(solution)/shard_map/ppermute | solution.py:52
  101.9 5.4 %collective-permute-done.10 = bf16[2304,128]{1,0:T(8,128)(2,1)S(1)} collective-permute-done((bf16[2304,128]{1,0:T(8,128)(2,1)S(1)}, bf16[2304,128]{1,0:T(8,128)(2,1)S(1)}, u32[]{:S(2)}, u32[]{:S(2)}) %collective-permute-start.10) | collective-permute-done | bytes 589856 | tf_op jit(solution)/shard_map/ppermute | solution.py:52
  107.7 6.6 %collective-permute-done.12 = bf16[2304,128]{1,0:T(8,128)(2,1)S(1)} collective-permute-done((bf16[2304,128]{1,0:T(8,128)(2,1)S(1)}, bf16[2304,128]{1,0:T(8,128)(2,1)S(1)}, u32[]{:S(2)}, u32[]{:S(2)}) %collective-permute-start.12) | collective-permute-done | bytes 589856 | tf_op jit(solution)/shard_map/ppermute | solution.py:52
  114.3 13.1 %pad_maximum_fusion.near_ref = bf16[9216,128]{1,0:T(8,128)(2,1)S(1)} fusion(bf16[2304,128]{1,0:T(8,128)(2,1)S(1)} %collective-permute-done.12, bf16[2304,128]{1,0:T(8,128)(2,1)S(1)} %collective-permute-done.11, bf16[2304,128]{1,0:T(8,128)(2,1)S(1)} %collective-permute-done.10, bf16[2304,128]{1,0:T(8,128)(2,1)S(1)} %add_convert_fusion), kind=kLoop, calls=%fused_computation | loop fusion | flops 9437184 | bytes 4718592 | tf_op jit(solution)/shard_map/concatenate | solution.py:53
  127.5 1.5 collective-permute-start.13
  129.0 1.7 collective-permute-start.14
  130.7 26.4 %collective-permute-done.13.plus_ref = bf16[9216,128]{1,0:T(8,128)(2,1)S(1)} collective-permute-done((bf16[9216,128]{1,0:T(8,128)(2,1)S(1)}, bf16[9216,128]{1,0:T(8,128)(2,1)S(1)}, u32[]{:S(2)}, u32[]{:S(2)}) %collective-permute-start.13) | collective-permute-done | bytes 2359328 | tf_op jit(solution)/shard_map/ppermute | solution.py:55
  160.9 2.7 %collective-permute-start.16 = (bf16[4608,128]{1,0:T(8,128)(2,1)}, bf16[4608,128]{1,0:T(8,128)(2,1)}, u32[]{:S(2)}, u32[]{:S(2)}) collective-permute-start(bf16[4608,128]{1,0:T(8,128)(2,1)} %slice.80), channel_id=1, source_target_pairs={{0,6},{1,7},{2,0},{3,1},{4,2},{5,3},{6,4},{7,5},{8,14},{9,15},{10,... | collective-permute-start | bytes 3538952 | tf_op jit(solution)/shard_map/ppermute | solution.py:58
  164.0 11.2 %collective-permute-done.15.fara_ref = bf16[4608,128]{1,0:T(8,128)(2,1)} collective-permute-done((bf16[4608,128]{1,0:T(8,128)(2,1)}, bf16[4608,128]{1,0:T(8,128)(2,1)}, u32[]{:S(2)}, u32[]{:S(2)}) %collective-permute-start.15) | collective-permute-done | bytes 1179680 | tf_op jit(solution)/shard_map/ppermute | solution.py:57
  175.2 1.9 collective-permute-done.16.farb_ref
  177.1 1.7 copy-done.2
  178.7 1.7 copy-done.4
  180.4 1.7 copy-done.6
  182.1 13.2 %shard_map.38 = (f32[2304,128]{1,0:T(8,128)S(1)}, bf16[2304,128]{1,0:T(8,128)(2,1)}) custom-call(s32[1]{0:T(128)} %bitcast.core_ref, s32[96]{0:T(128)S(1)} %broadcast_select_fusion.1.place_ref, s32[97]{0:T(128)S(1)} %pad.21.have_ref, s32[12]{0:T(128)S(1)} %get-tuple-element.13.want_ref, s32[288]{0:T(512)S(1)} %reshape_reshape.6.right_ref, ...), custom_call_target="tpu_custom_call" | custom-call | tf_op jit(solution)/shard_map/pallas_call | solution.py:153
  196.3 6.4 %collective-permute-start.17 = (bf16[2304,128]{1,0:T(8,128)(2,1)}, bf16[2304,128]{1,0:T(8,128)(2,1)S(1)}, u32[]{:S(2)}, u32[]{:S(2)}) collective-permute-start(bf16[2304,128]{1,0:T(8,128)(2,1)} %get-tuple-element.12), channel_id=1, source_target_pairs={{0,64},{1,65},{2,66},{3,67},{4,68},{5,69},{6,70},{7,71},{8,72},{9,... | collective-permute-start | bytes 1769480 | tf_op jit(solution)/shard_map/ppermute | solution.py:48
  (95 shorter events, 29.7 us)
Async XLA Ops:
  6.5 55.2 %all-gather.2.cloned.1.call-start = ((), (), s32[]{:S(2)}) async-start(), calls=%async_computation | async-start | bytes 3575808 | tf_op jit(solution)/shard_map/all_gather | solution.py:186
  12.6 9.4 %collective-permute-start.1 = (bf16[1552,128]{1,0:T(8,128)(2,1)}, bf16[1552,128]{1,0:T(8,128)(2,1)S(1)}, u32[]{:S(2)}, u32[]{:S(2)}) collective-permute-start(bf16[1552,128]{1,0:T(8,128)(2,1)} %pad_maximum_fusion.1), channel_id=1, source_target_pairs={{0,1},{1,128},{2,3},{3,130},{4,5},{5,132},{6,7},{7,134},{8,9},{9,1... | collective-permute-start | bytes 1191944 | tf_op jit(solution)/shard_map/ppermute | solution.py:52
  14.8 10.9 %collective-permute-start.2 = (bf16[1552,128]{1,0:T(8,128)(2,1)}, bf16[1552,128]{1,0:T(8,128)(2,1)S(1)}, u32[]{:S(2)}, u32[]{:S(2)}) collective-permute-start(bf16[1552,128]{1,0:T(8,128)(2,1)} %pad_maximum_fusion.1), channel_id=1, source_target_pairs={{0,129},{1,0},{2,131},{3,2},{4,133},{5,4},{6,135},{7,6},{8,137},{9... | collective-permute-start | bytes 1191944 | tf_op jit(solution)/shard_map/ppermute | solution.py:52
  16.3 11.1 %collective-permute-start.3 = (bf16[1552,128]{1,0:T(8,128)(2,1)}, bf16[1552,128]{1,0:T(8,128)(2,1)S(1)}, u32[]{:S(2)}, u32[]{:S(2)}) collective-permute-start(bf16[1552,128]{1,0:T(8,128)(2,1)} %pad_maximum_fusion.1), channel_id=1, source_target_pairs={{0,128},{1,129},{2,130},{3,131},{4,132},{5,133},{6,134},{7,135},{8... | collective-permute-start | bytes 1191944 | tf_op jit(solution)/shard_map/ppermute | solution.py:52
  28.2 37.0 %collective-permute-start.4 = (bf16[6208,128]{1,0:T(8,128)(2,1)}, bf16[6208,128]{1,0:T(8,128)(2,1)}, u32[]{:S(2)}, u32[]{:S(2)}) collective-permute-start(bf16[6208,128]{1,0:T(8,128)(2,1)} %constant_dynamic-update-slice_fusion.near_ref), channel_id=1, source_target_pairs={{0,2},{1,3},{2,4},{3,5},{4,6},{5,7},{6,0},{7,1},{8,10},{9,11},{10,... | collective-permute-start | bytes 4767752 | tf_op jit(solution)/shard_map/ppermute | solution.py:55
  29.1 39.6 %collective-permute-start.5 = (bf16[6208,128]{1,0:T(8,128)(2,1)}, bf16[6208,128]{1,0:T(8,128)(2,1)}, u32[]{:S(2)}, u32[]{:S(2)}) collective-permute-start(bf16[6208,128]{1,0:T(8,128)(2,1)} %constant_dynamic-update-slice_fusion.near_ref), channel_id=1, source_target_pairs={{0,6},{1,7},{2,0},{3,1},{4,2},{5,3},{6,4},{7,5},{8,14},{9,15},{10,... | collective-permute-start | bytes 4767752 | tf_op jit(solution)/shard_map/ppermute | solution.py:56
  30.9 41.5 %collective-permute-start.8 = (s32[6,3]{0,1:T(4,128)S(1)}, s32[6,3]{0,1:T(4,128)S(1)}, u32[]{:S(2)}, u32[]{:S(2)}) collective-permute-start(s32[6,3]{0,1:T(4,128)S(1)} %get-tuple-element.16), channel_id=1, source_target_pairs={{0,64},{1,65},{2,66},{3,67},{4,68},{5,69},{6,70},{7,71},{8,72},{9,... | collective-permute-start | bytes 224 | tf_op jit(solution)/shard_map/ppermute | solution.py:48
  64.4 19.0 %collective-permute-start = (bf16[6208,128]{1,0:T(8,128)(2,1)}, bf16[6208,128]{1,0:T(8,128)(2,1)}, u32[]{:S(2)}, u32[]{:S(2)}) collective-permute-start(bf16[6208,128]{1,0:T(8,128)(2,1)} %bitcast.6), channel_id=1, source_target_pairs={{0,64},{1,65},{2,66},{3,67},{4,68},{5,69},{6,70},{7,71},{8,72},{9,... | collective-permute-start | bytes 4767752 | tf_op jit(solution)/shard_map/ppermute | solution.py:48
  65.2 18.1 %copy-start = (bf16[12416,128]{1,0:T(8,128)(2,1)S(1)}, bf16[12416,128]{1,0:T(8,128)(2,1)}, u32[]{:S(2)}) copy-start(bf16[12416,128]{1,0:T(8,128)(2,1)} %all-gather.2.cloned.1.call-done.own_ref) | copy-start | bytes 9535492
  67.5 12.7 %collective-permute-start.6 = (bf16[3104,128]{1,0:T(8,128)(2,1)}, bf16[3104,128]{1,0:T(8,128)(2,1)}, u32[]{:S(2)}, u32[]{:S(2)}) collective-permute-start(bf16[3104,128]{1,0:T(8,128)(2,1)} %slice.73), channel_id=1, source_target_pairs={{0,2},{1,3},{2,4},{3,5},{4,6},{5,7},{6,0},{7,1},{8,10},{9,11},{10,... | collective-permute-start | bytes 2383880 | tf_op jit(solution)/shard_map/ppermute | solution.py:57
  70.7 11.5 %collective-permute-start.7 = (bf16[3104,128]{1,0:T(8,128)(2,1)}, bf16[3104,128]{1,0:T(8,128)(2,1)}, u32[]{:S(2)}, u32[]{:S(2)}) collective-permute-start(bf16[3104,128]{1,0:T(8,128)(2,1)} %slice.75), channel_id=1, source_target_pairs={{0,6},{1,7},{2,0},{3,1},{4,2},{5,3},{6,4},{7,5},{8,14},{9,15},{10,... | collective-permute-start | bytes 2383880 | tf_op jit(solution)/shard_map/ppermute | solution.py:58
  94.3 2.6 %collective-permute-start.9 = (bf16[2304,128]{1,0:T(8,128)(2,1)S(1)}, bf16[2304,128]{1,0:T(8,128)(2,1)S(1)}, u32[]{:S(2)}, u32[]{:S(2)}) collective-permute-start(bf16[2304,128]{1,0:T(8,128)(2,1)S(1)} %get-tuple-element.10), channel_id=1, source_target_pairs={{0,64},{1,65},{2,66},{3,67},{4,68},{5,69},{6,70},{7,71},{8,72},{9,... | collective-permute-start | bytes 1769480 | tf_op jit(solution)/shard_map/ppermute | solution.py:48
  97.0 10.3 %collective-permute-start.10 = (bf16[2304,128]{1,0:T(8,128)(2,1)S(1)}, bf16[2304,128]{1,0:T(8,128)(2,1)S(1)}, u32[]{:S(2)}, u32[]{:S(2)}) collective-permute-start(bf16[2304,128]{1,0:T(8,128)(2,1)S(1)} %add_convert_fusion), channel_id=1, source_target_pairs={{0,1},{1,128},{2,3},{3,130},{4,5},{5,132},{6,7},{7,134},{8,9},{9,1... | collective-permute-start | bytes 1769480 | tf_op jit(solution)/shard_map/ppermute | solution.py:52
  97.9 9.8 %collective-permute-start.11 = (bf16[2304,128]{1,0:T(8,128)(2,1)S(1)}, bf16[2304,128]{1,0:T(8,128)(2,1)S(1)}, u32[]{:S(2)}, u32[]{:S(2)}) collective-permute-start(bf16[2304,128]{1,0:T(8,128)(2,1)S(1)} %add_convert_fusion), channel_id=1, source_target_pairs={{0,129},{1,0},{2,131},{3,2},{4,133},{5,4},{6,135},{7,6},{8,137},{9... | collective-permute-start | bytes 1769480 | tf_op jit(solution)/shard_map/ppermute | solution.py:52
  99.8 14.6 %collective-permute-start.12 = (bf16[2304,128]{1,0:T(8,128)(2,1)S(1)}, bf16[2304,128]{1,0:T(8,128)(2,1)S(1)}, u32[]{:S(2)}, u32[]{:S(2)}) collective-permute-start(bf16[2304,128]{1,0:T(8,128)(2,1)S(1)} %add_convert_fusion), channel_id=1, source_target_pairs={{0,128},{1,129},{2,130},{3,131},{4,132},{5,133},{6,134},{7,135},{8... | collective-permute-start | bytes 1769480 | tf_op jit(solution)/shard_map/ppermute | solution.py:52
  127.4 32.0 %copy-start.1 = (bf16[9216,128]{1,0:T(8,128)(2,1)}, bf16[9216,128]{1,0:T(8,128)(2,1)S(1)}, u32[]{:S(2)}) copy-start(bf16[9216,128]{1,0:T(8,128)(2,1)S(1)} %pad_maximum_fusion.near_ref) | copy-start | bytes 7077892
  127.5 29.7 %collective-permute-start.13 = (bf16[9216,128]{1,0:T(8,128)(2,1)S(1)}, bf16[9216,128]{1,0:T(8,128)(2,1)S(1)}, u32[]{:S(2)}, u32[]{:S(2)}) collective-permute-start(bf16[9216,128]{1,0:T(8,128)(2,1)S(1)} %pad_maximum_fusion.near_ref), channel_id=1, source_target_pairs={{0,2},{1,3},{2,4},{3,5},{4,6},{5,7},{6,0},{7,1},{8,10},{9,11},{10,... | collective-permute-start | bytes 7077896 | tf_op jit(solution)/shard_map/ppermute | solution.py:55
  129.0 29.4 %collective-permute-start.14 = (bf16[9216,128]{1,0:T(8,128)(2,1)S(1)}, bf16[9216,128]{1,0:T(8,128)(2,1)S(1)}, u32[]{:S(2)}, u32[]{:S(2)}) collective-permute-start(bf16[9216,128]{1,0:T(8,128)(2,1)S(1)} %pad_maximum_fusion.near_ref), channel_id=1, source_target_pairs={{0,6},{1,7},{2,0},{3,1},{4,2},{5,3},{6,4},{7,5},{8,14},{9,15},{10,... | collective-permute-start | bytes 7077896 | tf_op jit(solution)/shard_map/ppermute | solution.py:56
  157.1 2.3 %copy-start.3 = (bf16[9216,128]{1,0:T(8,128)(2,1)}, bf16[9216,128]{1,0:T(8,128)(2,1)S(1)}, u32[]{:S(2)}) copy-start(bf16[9216,128]{1,0:T(8,128)(2,1)S(1)} %collective-permute-done.13.plus_ref) | copy-start | bytes 7077892
  158.3 16.9 %collective-permute-start.15 = (bf16[4608,128]{1,0:T(8,128)(2,1)}, bf16[4608,128]{1,0:T(8,128)(2,1)}, u32[]{:S(2)}, u32[]{:S(2)}) collective-permute-start(bf16[4608,128]{1,0:T(8,128)(2,1)} %slice.79), channel_id=1, source_target_pairs={{0,2},{1,3},{2,4},{3,5},{4,6},{5,7},{6,0},{7,1},{8,10},{9,11},{10,... | collective-permute-start | bytes 3538952 | tf_op jit(solution)/shard_map/ppermute | solution.py:57
  159.5 1.4 copy-start.5
  160.9 16.1 %collective-permute-start.16 = (bf16[4608,128]{1,0:T(8,128)(2,1)}, bf16[4608,128]{1,0:T(8,128)(2,1)}, u32[]{:S(2)}, u32[]{:S(2)}) collective-permute-start(bf16[4608,128]{1,0:T(8,128)(2,1)} %slice.80), channel_id=1, source_target_pairs={{0,6},{1,7},{2,0},{3,1},{4,2},{5,3},{6,4},{7,5},{8,14},{9,15},{10,... | collective-permute-start | bytes 3538952 | tf_op jit(solution)/shard_map/ppermute | solution.py:58
  163.9 38.8 %copy-start.8 = (s32[6,2]{0,1:T(2,128)S(1)}, s32[6,2]{0,1:T(2,128)}, u32[]{:S(2)}) copy-start(s32[6,2]{0,1:T(2,128)} %param.4) | copy-start | bytes 148
  177.1 1.7 copy-start.2
  178.7 1.7 copy-start.4
  180.4 1.7 copy-start.6
  195.3 1.0 copy-start.7
  196.3 8.2 %collective-permute-start.17 = (bf16[2304,128]{1,0:T(8,128)(2,1)}, bf16[2304,128]{1,0:T(8,128)(2,1)S(1)}, u32[]{:S(2)}, u32[]{:S(2)}) collective-permute-start(bf16[2304,128]{1,0:T(8,128)(2,1)} %get-tuple-element.12), channel_id=1, source_target_pairs={{0,64},{1,65},{2,66},{3,67},{4,68},{5,69},{6,70},{7,71},{8,72},{9,... | collective-permute-start | bytes 1769480 | tf_op jit(solution)/shard_map/ppermute | solution.py:48
Sparse Core Ops, SparseCore 0:
  12.7 48.9 all-gather.1

commit v2 on v1

v2 whole, which is shorter than its diff:
```python
import functools

import jax
import jax.numpy as jnp
from jax import lax
from jax.experimental import pallas as pl
from jax.experimental.pallas import tpu as pltpu
from jax.sharding import PartitionSpec as P

BLK = 128
KA = 2
KC = 3
TP = 24
ROWS = 6
OUTS = ROWS * KC
LEFT = ROWS * KA
ROOM = 24
SLOTS = 64
JOBS = 2 * ROWS * 8 * KC
ALL = ("row", "col", "depth")


def chip_of(device):
    row, col, depth = device // 64, device // 8 % 8, device % 8
    return row // 2 * 2 + depth % 2, depth // 2, col, row % 2


def device_of(x, y, z, core):
    return (x // 2 * 2 + core) * 64 + z * 8 + y * 2 + x % 2


def move(array, rule):
    pairs = []
    for device in range(256):
        x, y, z, core = rule(*chip_of(device))
        pairs.append((device, device_of(x % 4, y % 4, z % 8, core)))
    return lax.ppermute(array, ALL, pairs)


def first_ring(array, step):
    return move(array, lambda x, y, z, core: (x + step * (1 - core), y + step * core, z, core))


def second_ring(array, step):
    return move(array, lambda x, y, z, core: (x + step * core, y + step * (1 - core), z, core))


def swap(array):
    return move(array, lambda x, y, z, core: (x, y, z, 1 - core))


def ring_order(away):
    away = away & 3
    return jnp.where(away == 2, 3, jnp.where(away == 3, 2, away))


def first_pieces(piece):
    return tuple([piece] + [first_ring(piece, step) for step in (1, -1, 2)])


def far_pieces(plus, minus):
    half = plus.shape[0] // 2
    return second_ring(plus[:half], 1), second_ring(minus[half:], -1)


def doubled(array, count, rule):
    return jnp.concatenate([array, move(array, functools.partial(rule, count))], axis=0)


def along_z(n, x, y, z, core):
    return x, y, z - n, core


def along_x(n, x, y, z, core):
    return x - n, y, z, core


def along_y(n, x, y, z, core):
    return x, y - n, z, core


def block_copy(ref, block, target, sem):
    offset = pl.multiple_of(block * BLK, BLK)
    return pltpu.make_async_copy(ref.at[pl.ds(offset, BLK)], target, sem)


def plan_kernel(here_ref, own_ref, other_ref, plane_ref, x_jobs, s_jobs, takes, seen, group_code):
    core, x, y, z = here_ref[0], here_ref[1], here_ref[2], here_ref[3]
    first, second = jnp.where(core == 0, x, y), jnp.where(core == 0, y, x)

    for group in range(16):
        at_x, at_y = group // 8 * 2 + group % 2, group // 4 % 2 * 2 + group // 2 % 2
        far = jnp.where(core == 0, at_x, at_y)
        inner = ring_order(first - far)
        outer = ring_order(second - jnp.where(core == 0, at_y, at_x))
        group_code[0, group] = inner
        group_code[1, group] = outer
        group_code[2, group] = far
        group_code[3, group] = ((at_y - y) & 3) * 4 + ((at_x - x) & 3)

    def clear(n, carry):
        seen[n] = -1
        return carry

    lax.fori_loop(0, 16 * OUTS, clear, 0)
    x_jobs[0] = 0
    s_jobs[0] = 0
    for outer in range(4):
        takes[outer, ROOM] = 0

    def scan(marks_ref, half):
        def scan_row(row, carry):
            wanted = [marks_ref[0, LEFT + row * KC + u] for u in range(KC)]
            for panel in range(4):
                whole = panel // 2 * 4 + 2 * core + panel % 2
                line = (whole - z) & 7
                for side in range(KA):
                    column = marks_ref[line, row * KA + side]

                    @pl.when(column >= 0)
                    def _(panel=panel, whole=whole, side=side, column=column):
                        quarter = column // ROWS
                        place = column - quarter * ROWS
                        group = panel * 4 + quarter
                        table = group_code[3, group]
                        founds = []
                        for slot in range(KC):
                            have = plane_ref[table, LEFT + place * KC + slot]
                            found = jnp.where(have == wanted[0], 0, jnp.where(have == wanted[1], 1, 2))
                            founds.append(jnp.where((found < 2) | (have == wanted[2]), found, -1))

                        @pl.when((founds[0] >= 0) | (founds[1] >= 0) | (founds[2] >= 0))
                        def _():
                            inner, outer = group_code[0, group], group_code[1, group]
                            left = half * 8 * LEFT + whole * LEFT + row * KA + side
                            source = jnp.where(outer < 3, outer, 3 + (inner >> 1))
                            within = jnp.where(outer < 3, inner, inner & 1) * ROWS + place
                            for slot, found in enumerate(founds):
                                out = half * OUTS + row * KC + found

                                if slot < KA:

                                    @pl.when((found >= 0) & (plane_ref[table, place * KA + slot] >= 0))
                                    def _(slot=slot, out=out):
                                        count = x_jobs[0]
                                        x_jobs[0] = count + 1
                                        block = within * KA + slot
                                        x_jobs[1 + count] = (source << 21) | (block << 14) | (left << 6) | out

                                @pl.when(found >= 0)
                                def _(slot=slot, out=out):
                                    mark = group * OUTS + place * KC + slot

                                    @pl.when((outer > 0) & (seen[mark] < 0))
                                    def _():
                                        rank = takes[outer, ROOM]
                                        takes[outer, ROOM] = rank + 1
                                        seen[mark] = rank

                                        @pl.when(rank < ROOM)
                                        def _():
                                            takes[outer, rank] = (group_code[2, group] << 5) | (place * KC + slot)

                                    count = s_jobs[0]
                                    s_jobs[0] = count + 1
                                    s_jobs[1 + count] = (source << 21) | ((within * KC + slot) << 14) | (left << 6) | out
                                    s_jobs[1 + JOBS + count] = jnp.where(
                                        outer == 0, (inner << 5) | (place * KC + slot), ((3 + outer) << 5) | (seen[mark] & 31)
                                    )

            return carry

        lax.fori_loop(0, ROWS, scan_row, 0)

    scan(own_ref, 0)
    scan(other_ref, 1)
    most = jnp.maximum(takes[1, ROOM], jnp.maximum(takes[2, ROOM], takes[3, ROOM]))
    for outer in range(4):
        takes[outer, ROOM + 1] = most


SMEM = pl.BlockSpec(memory_space=pltpu.SMEM)
VMEM = pl.BlockSpec(memory_space=pltpu.VMEM)
ANY = pl.BlockSpec(memory_space=pl.ANY)


def plan(here, own, other, plane):
    return pl.pallas_call(
        plan_kernel,
        out_shape=(
            jax.ShapeDtypeStruct((1 + JOBS,), jnp.int32),
            jax.ShapeDtypeStruct((1 + 2 * JOBS,), jnp.int32),
            jax.ShapeDtypeStruct((4, BLK), jnp.int32),
        ),
        in_specs=[SMEM] * 4,
        out_specs=(SMEM,) * 3,
        scratch_shapes=[pltpu.SMEM((16 * OUTS,), jnp.int32), pltpu.SMEM((4, 16), jnp.int32)],
    )(here, own, other, plane)


def product_kernel(rights, packed, jobs_ref, own_ref, other_ref, *refs):
    right_refs, (mine_out, theirs_out, total, left_buf, right_buf, sems) = refs[:rights], refs[rights:]
    count = jobs_ref[0]

    def start(n):
        slot = lax.rem(n, SLOTS)
        job = jobs_ref[1 + n]
        left = (job >> 6) & 255
        if packed:
            code = jobs_ref[1 + JOBS + n]
            source, block = code >> 5, code & 31
        else:
            source, block = job >> 21, (job >> 14) & 127

        @pl.when(left < 8 * LEFT)
        def _():
            block_copy(own_ref, left, left_buf.at[slot], sems.at[0, slot]).start()

        @pl.when(left >= 8 * LEFT)
        def _():
            block_copy(other_ref, left - 8 * LEFT, left_buf.at[slot], sems.at[0, slot]).start()

        for index, ref in enumerate(right_refs):

            @pl.when(source == index)
            def _(ref=ref):
                block_copy(ref, block, right_buf.at[slot], sems.at[1, slot]).start()

    def wait(n):
        slot = lax.rem(n, SLOTS)
        block_copy(own_ref, 0, left_buf.at[slot], sems.at[0, slot]).wait()
        block_copy(own_ref, 0, right_buf.at[slot], sems.at[1, slot]).wait()

    def first(n, carry):
        start(n)
        return carry

    lax.fori_loop(0, jnp.minimum(count, SLOTS), first, 0)
    total[...] = jnp.zeros_like(total)

    def multiply(group, carry):
        at = [group * 4 + index for index in range(4)]
        for n in at:
            pl.when(n < count)(functools.partial(wait, n))
        outs = [jnp.where(n < count, jobs_ref[jnp.minimum(1 + n, JOBS)] & 63, 2 * OUTS) for n in at]
        slots = [lax.rem(n, SLOTS) for n in at]
        dots = [jnp.dot(left_buf[slot], right_buf[slot], preferred_element_type=jnp.float32) for slot in slots]
        for out, dot in zip(outs, dots):
            total[out] += dot
        for n in at:
            pl.when(n + SLOTS < count)(functools.partial(start, n + SLOTS))
        return carry

    lax.fori_loop(0, (count + 3) // 4, multiply, 0)
    for block in range(OUTS):
        mine_out[pl.ds(block * BLK, BLK), :] = total[block]
        theirs_out[pl.ds(block * BLK, BLK), :] = total[OUTS + block].astype(jnp.bfloat16)


def product(jobs, left, left_other, rights, packed):
    return pl.pallas_call(
        functools.partial(product_kernel, len(rights), packed),
        out_shape=(
            jax.ShapeDtypeStruct((OUTS * BLK, BLK), jnp.float32),
            jax.ShapeDtypeStruct((OUTS * BLK, BLK), jnp.bfloat16),
        ),
        in_specs=[SMEM] + [ANY] * (2 + len(rights)),
        out_specs=(VMEM, VMEM),
        scratch_shapes=[
            pltpu.VMEM((2 * OUTS + 1, BLK, BLK), jnp.float32),
            pltpu.VMEM((SLOTS, BLK, BLK), jnp.bfloat16),
            pltpu.VMEM((SLOTS, BLK, BLK), jnp.bfloat16),
            pltpu.SemaphoreType.DMA((2, SLOTS)),
        ],
        compiler_params=pltpu.CompilerParams(vmem_limit_bytes=24 * 1024 * 1024),
    )(jobs, left, left_other, *rights)


def pack_kernel(here_ref, *refs):
    lists, pieces, outs, sems = refs[:3], refs[3:7], refs[7:10], refs[10]
    first = jnp.where(here_ref[0] == 0, here_ref[1], here_ref[2])

    for target, out in enumerate(outs):
        asked = lists[target]

        def start(n, carry, target=target, out=out, asked=asked):
            code = asked[0, n]
            inner = ring_order(first - (code >> 5))
            offset = pl.multiple_of(n * BLK, BLK)
            for index, ref in enumerate(pieces):

                @pl.when(inner == index)
                def _(ref=ref):
                    block_copy(ref, code & 31, out.at[pl.ds(offset, BLK)], sems.at[target, n]).start()

            return carry

        lax.fori_loop(0, jnp.minimum(asked[0, ROOM], ROOM), start, 0)

    for target, out in enumerate(outs):
        asked = lists[target]

        def wait(n, carry, target=target, out=out):
            block_copy(pieces[0], 0, out.at[pl.ds(0, BLK)], sems.at[target, n]).wait()
            return carry

        lax.fori_loop(0, jnp.minimum(asked[0, ROOM], ROOM), wait, 0)


def pack(here, lists, pieces):
    shape = jax.ShapeDtypeStruct((ROOM * BLK, BLK), jnp.bfloat16)
    return pl.pallas_call(
        pack_kernel,
        out_shape=(shape,) * 3,
        in_specs=[SMEM] * 4 + [ANY] * 4,
        out_specs=(ANY,) * 3,
        scratch_shapes=[pltpu.SemaphoreType.DMA((3, ROOM))],
    )(here, *lists, *pieces)


def local(block_values, block_columns, pattern_columns):
    row, depth, z = lax.axis_index("row"), lax.axis_index("depth"), lax.axis_index("col")
    here = jnp.stack([row % 2, row // 2 * 2 + depth % 2, depth // 2, z]).astype(jnp.int32)
    own_pattern = lax.dynamic_slice_in_dim(pattern_columns, depth * ROWS, ROWS, 0)

    piece = block_values.reshape(LEFT * BLK, BLK)
    left = lax.all_gather(piece, "col", axis=0, tiled=True)
    near = jnp.concatenate(first_pieces(piece), axis=0)

    marks = jnp.concatenate([block_columns.reshape(1, -1), own_pattern.reshape(1, -1)], axis=1)
    marks = jnp.pad(marks, ((0, 0), (0, BLK - marks.shape[1])))
    row_marks, plane_marks = doubled(marks, 1, along_z), doubled(marks, 1, along_x)
    row_marks, plane_marks = doubled(row_marks, 2, along_z), doubled(plane_marks, 2, along_x)
    row_marks, plane_marks, near = lax.optimization_barrier((row_marks, plane_marks, near))
    row_marks, plane_marks = doubled(row_marks, 4, along_z), doubled(plane_marks, 1, along_y)
    plane_marks = doubled(plane_marks, 2, along_y)
    plus, minus, other_marks = second_ring(near, 1), second_ring(near, -1), swap(row_marks)
    plus, minus, row_marks, other_marks, plane_marks = lax.optimization_barrier(
        (plus, minus, row_marks, other_marks, plane_marks)
    )
    far = far_pieces(plus, minus)
    left, near, plus, minus = lax.optimization_barrier((left, near, plus, minus))
    right = (near, plus, minus) + far
    x_jobs, s_jobs, takes = plan(here, row_marks, other_marks, plane_marks)
    left_other = swap(left)

    add = lambda mine, theirs: mine + swap(theirs).astype(jnp.float32)
    square = add(*product(x_jobs, left, left_other, right, False)).astype(jnp.bfloat16)
    square, takes = lax.optimization_barrier((square, takes))
    pieces = first_pieces(square)
    asked = tuple(second_ring(takes[index : index + 1], step) for index, step in ((1, -1), (2, 1), (3, 2)))
    most = functools.reduce(jnp.maximum, asked, takes[:1])[0, ROOM + 1]

    def packed(pieces):
        sent = pack(here, asked, pieces)
        got = tuple(second_ring(part, step) for part, step in zip(sent, (1, -1, 2)))
        return tuple(product(s_jobs, left, left_other, pieces + got, True))

    def dense(pieces):
        near = jnp.concatenate(pieces, axis=0)
        plus, minus = second_ring(near, 1), second_ring(near, -1)
        return tuple(product(s_jobs, left, left_other, (near, plus, minus) + far_pieces(plus, minus), False))

    cube = add(*lax.cond(most <= ROOM, packed, dense, pieces)).reshape(ROWS, KC, BLK, BLK)
    stored = jnp.where((block_columns >= 0)[:, :, None, None], block_values, 0).astype(jnp.float32)
    mapped = jnp.pad(stored, ((0, 0), (0, KC - KA), (0, 0), (0, 0)))
    return (1.5 * mapped - 0.5 * cube).astype(jnp.bfloat16)


def solution(mesh):
    placed = (P(("row", "depth"), "col", None, None), P(("row", "depth"), "col"), P("row", "col"))
    return jax.shard_map(
        local,
        mesh=mesh,
        in_specs=placed,
        out_specs=P(("row", "depth"), "col", None, None),
        check_vma=False,
    )
```

time: 214 us -> 151 us (0.71)
  the two profiles are of different devices: /device:TPU:1 before, /device:TPU:5 now
where the time goes in v2:
time: 151 us; the launch traced here: 152 us
  starting transfers between devices  68.6 us (45%)
  waiting for transfers between devices  37.1 us (25%)
  Pallas kernels  21.6 us (14%)
  between operations  14.2 us (9%)
  local copies, waits for them, and re-layouts  5.54 us (4%)
  other arithmetic  4.55 us (3%)
    ppermute x27, starting transfers between devices, move(): return lax.ppermute(array, ALL, pairs)  68.6 us
    ppermute x27, waiting for transfers between devices, move(): return lax.ppermute(array, ALL, pairs)  36.4 us
    pallas_call x2, Pallas kernels, product(): pl.pallas_call(functools.partial(product_kernel, len(rights), packed), ou...  10.5 us
    pallas_call x1, Pallas kernels, plan(): pl.pallas_call(plan_kernel, out_shape=(jax.ShapeDtypeStruct((1 + JOBS,),...  9.06 us
    slice x2, local copies, waits for them, and re-layouts, far_pieces(): return (second_ring(plus[:half], 1), second_ring(minus[half:], -1))  3.03 us
  transfers between devices with their start and end apart: 28, of which 16 were waited for; matrix products, arithmetic and copies ran while one was open for 5% of the time, Pallas kernels for 6%

profile of v2, /device:TPU:5, one launch (start us, length us, event | category | flops | bytes accessed | tf_op | source)
XLA Modules:
  0.0 151.6 jit_solution(12476686347293112598)
XLA Ops:
  7.3 1.4 collective-permute-start.11
  8.6 1.5 %collective-permute-start.12 = (bf16[1536,128]{1,0:T(8,128)(2,1)}, bf16[1536,128]{1,0:T(8,128)(2,1)S(1)}, u32[]{:S(2)}, u32[]{:S(2)}) collective-permute-start(bf16[1536,128]{1,0:T(8,128)(2,1)} %bitcast.10), channel_id=1, source_target_pairs={{0,129},{1,0},{2,131},{3,2},{4,133},{5,4},{6,135},{7,6},{8,137},{9... | collective-permute-start | bytes 1179656 | tf_op jit(solution)/shard_map/ppermute | solution.py:37
  10.2 1.6 %collective-permute-start.13 = (bf16[1536,128]{1,0:T(8,128)(2,1)}, bf16[1536,128]{1,0:T(8,128)(2,1)S(1)}, u32[]{:S(2)}, u32[]{:S(2)}) collective-permute-start(bf16[1536,128]{1,0:T(8,128)(2,1)} %bitcast.11), channel_id=1, source_target_pairs={{0,128},{1,129},{2,130},{3,131},{4,132},{5,133},{6,134},{7,135},{8... | collective-permute-start | bytes 1179656 | tf_op jit(solution)/shard_map/ppermute | solution.py:37
  12.9 5.6 %collective-permute-start.7 = (s32[1,128]{1,0:T(1,128)S(1)}, s32[1,128]{1,0:T(1,128)S(1)}, u32[]{:S(2)}, u32[]{:S(2)}) collective-permute-start(s32[1,128]{1,0:T(1,128)S(1)} %pad.13), channel_id=1, source_target_pairs={{0,56},{1,57},{2,58},{3,59},{4,60},{5,61},{6,62},{7,63},{8,0},{9,1... | collective-permute-start | bytes 1544 | tf_op jit(solution)/shard_map/ppermute | solution.py:37
  19.2 1.7 %collective-permute-done.9 = s32[1,128]{1,0:T(1,128)S(1)} collective-permute-done((s32[1,128]{1,0:T(1,128)S(1)}, s32[1,128]{1,0:T(1,128)S(1)}, u32[]{:S(2)}, u32[]{:S(2)}) %collective-permute-start.9) | collective-permute-done | bytes 544 | tf_op jit(solution)/shard_map/ppermute | solution.py:37
  21.9 4.9 %collective-permute-start.8 = (s32[2,128]{1,0:T(2,128)S(1)}, s32[2,128]{1,0:T(2,128)S(1)}, u32[]{:S(2)}, u32[]{:S(2)}) collective-permute-start(s32[2,128]{1,0:T(2,128)S(1)} %get-tuple-element.110), channel_id=1, source_target_pairs={{0,48},{1,49},{2,50},{3,51},{4,52},{5,53},{6,54},{7,55},{8,56},{9,... | collective-permute-start | bytes 3080 | tf_op jit(solution)/shard_map/ppermute | solution.py:37
  28.7 1.6 %collective-permute-start.14 = (bf16[6144,128]{1,0:T(8,128)(2,1)S(1)}, bf16[6144,128]{1,0:T(8,128)(2,1)S(1)}, u32[]{:S(2)}, u32[]{:S(2)}) collective-permute-start(bf16[6144,128]{1,0:T(8,128)(2,1)S(1)} %pad_maximum_fusion.refs_0_), channel_id=1, source_target_pairs={{0,2},{1,3},{2,4},{3,5},{4,6},{5,7},{6,0},{7,1},{8,10},{9,11},{10,... | collective-permute-start | bytes 4718600 | tf_op jit(solution)/shard_map/ppermute | solution.py:37
  31.5 2.7 %collective-permute-start.16 = (s32[4,128]{1,0:T(4,128)S(1)}, s32[4,128]{1,0:T(4,128)S(1)}, u32[]{:S(2)}, u32[]{:S(2)}) collective-permute-start(s32[4,128]{1,0:T(4,128)S(1)} %get-tuple-element.84), channel_id=1, source_target_pairs={{0,32},{1,33},{2,34},{3,35},{4,36},{5,37},{6,38},{7,39},{8,40},{9,... | collective-permute-start | bytes 6152 | tf_op jit(solution)/shard_map/ppermute | solution.py:37
  34.4 3.6 %collective-permute-done.16 = s32[4,128]{1,0:T(4,128)S(1)} collective-permute-done((s32[4,128]{1,0:T(4,128)S(1)}, s32[4,128]{1,0:T(4,128)S(1)}, u32[]{:S(2)}, u32[]{:S(2)}) %collective-permute-start.16) | collective-permute-done | bytes 2080 | tf_op jit(solution)/shard_map/ppermute | solution.py:37
  38.0 18.2 %collective-permute-start.17 = (s32[8,128]{1,0:T(8,128)S(1)}, s32[8,128]{1,0:T(8,128)S(1)}, u32[]{:S(2)}, u32[]{:S(2)}) collective-permute-start(s32[8,128]{1,0:T(8,128)S(1)} %pad_add_fusion.1.own_ref), channel_id=1, source_target_pairs={{0,64},{1,65},{2,66},{3,67},{4,68},{5,69},{6,70},{7,71},{8,72},{9,... | collective-permute-start | bytes 12296 | tf_op jit(solution)/shard_map/ppermute | solution.py:37
  57.1 2.0 %collective-permute-start.20 = (bf16[12288,128]{1,0:T(8,128)(2,1)}, bf16[12288,128]{1,0:T(8,128)(2,1)}, u32[]{:S(2)}, u32[]{:S(2)}) collective-permute-start(bf16[12288,128]{1,0:T(8,128)(2,1)} %all-gather.2.cloned.1.call-done.own_ref), channel_id=1, source_target_pairs={{0,64},{1,65},{2,66},{3,67},{4,68},{5,69},{6,70},{7,71},{8,72},{9,... | collective-permute-start | bytes 9437192 | tf_op jit(solution)/shard_map/ppermute | solution.py:37
  60.0 2.1 %slice.28 = bf16[3072,128]{1,0:T(8,128)(2,1)} slice(bf16[6144,128]{1,0:T(8,128)(2,1)} %collective-permute-done.15.refs_2_), slice={[3072:6144], [0:128]} | slice | bytes 1572864 | tf_op jit(solution)/shard_map/slice | solution.py:63
  62.9 1.6 %collective-permute-start.22 = (bf16[3072,128]{1,0:T(8,128)(2,1)}, bf16[3072,128]{1,0:T(8,128)(2,1)}, u32[]{:S(2)}, u32[]{:S(2)}) collective-permute-start(bf16[3072,128]{1,0:T(8,128)(2,1)} %slice.28), channel_id=1, source_target_pairs={{0,6},{1,7},{2,0},{3,1},{4,2},{5,3},{6,4},{7,5},{8,14},{9,15},{10,... | collective-permute-start | bytes 2359304 | tf_op jit(solution)/shard_map/ppermute | solution.py:37
  64.6 9.1 %shard_map.37 = (s32[289]{0:T(512)}, s32[577]{0:T(1024)S(1)}, s32[4,128]{1,0:T(4,128)}) custom-call(s32[4]{0:T(128)S(1)} %pad_add_fusion.7.here_ref, s32[8,128]{1,0:T(8,128)} %copy-done.3, s32[8,128]{1,0:T(8,128)} %copy-done.4, s32[16,128]{1,0:T(8,128)} %pad_add_fusion.plane_ref), custom_call_target="tpu_custom_call" | custom-call | tf_op jit(solution)/shard_map/pallas_call | solution.py:188
  76.1 3.6 %shard_map.38 = (f32[2304,128]{1,0:T(8,128)S(1)}, bf16[2304,128]{1,0:T(8,128)(2,1)S(1)}) custom-call(s32[289]{0:T(512)S(1)} %copy-done.1, bf16[12288,128]{1,0:T(8,128)(2,1)} %all-gather.2.cloned.1.call-done.own_ref, bf16[12288,128]{1,0:T(8,128)(2,1)} %collective-permute-done.20.other_ref, bf16[6144,128]{1,0:T(8,128)(2,1)S(1)} %pad_maximum_fusion.refs_0_, ...), custom_call_target="tpu_custom_call" | custom-call | tf_op jit(solution)/shard_map/pallas_call | solution.py:261
  80.9 1.6 %collective-permute-done.23 = bf16[2304,128]{1,0:T(8,128)(2,1)S(1)} collective-permute-done((bf16[2304,128]{1,0:T(8,128)(2,1)S(1)}, bf16[2304,128]{1,0:T(8,128)(2,1)S(1)}, u32[]{:S(2)}, u32[]{:S(2)}) %collective-permute-start.23) | collective-permute-done | bytes 589856 | tf_op jit(solution)/shard_map/ppermute | solution.py:37
  82.7 1.4 collective-permute-start.27
  84.1 1.4 collective-permute-start.28
  86.6 1.9 %collective-permute-start.24 = (s32[1,128]{1,0:T(1,128)S(1)}, s32[1,128]{1,0:T(1,128)S(1)}, u32[]{:S(2)}, u32[]{:S(2)}) collective-permute-start(s32[1,128]{1,0:T(1,128)S(1)} %get-tuple-element.104), channel_id=1, source_target_pairs={{0,6},{1,7},{2,0},{3,1},{4,2},{5,3},{6,4},{7,5},{8,14},{9,15},{10,... | collective-permute-start | bytes 1544 | tf_op jit(solution)/shard_map/ppermute | solution.py:37
  91.8 3.0 %collective-permute-done.26 = s32[1,128]{1,0:T(1,128)S(1)} collective-permute-done((s32[1,128]{1,0:T(1,128)S(1)}, s32[1,128]{1,0:T(1,128)S(1)}, u32[]{:S(2)}, u32[]{:S(2)}) %collective-permute-start.26) | collective-permute-done | bytes 544 | tf_op jit(solution)/shard_map/ppermute | solution.py:37
  96.1 4.1 %collective-permute-done.29 = bf16[2304,128]{1,0:T(8,128)(2,1)S(1)} collective-permute-done((bf16[2304,128]{1,0:T(8,128)(2,1)S(1)}, bf16[2304,128]{1,0:T(8,128)(2,1)S(1)}, u32[]{:S(2)}, u32[]{:S(2)}) %collective-permute-start.29) | collective-permute-done | bytes 589856 | tf_op jit(solution)/shard_map/ppermute | solution.py:37
  100.2 30.6 %conditional.1 = ((f32[2304,128]{1,0:T(8,128)}, bf16[2304,128]{1,0:T(8,128)(2,1)S(1)})) conditional(s32[]{:T(128)} %bitcast.5, (bf16[2304,128]{1,0:T(8,128)(2,1)S(1)}, bf16[2304,128]{1,0:T(8,128)(2,1)S(1)}, bf16[2304,128]{1,0:T(8,128)(2,1)S(1)}, bf16[2304,128]{1,0:T(8,128)(2,1)S(1)}, s32[577]{0:T(1024)S(1)}, /*index=5*/bf16[12288,128]{1,0:T(8,128)(2,1)}, ...), branch_computations={%region_0.1_spmd, %region_1.2_spmd} | conditional | bytes 37748904 | solution.py:364
  100.2 2.1 %branch_1_fun.2 = (bf16[3072,128]{1,0:T(8,128)(2,1)}, bf16[3072,128]{1,0:T(8,128)(2,1)}, bf16[3072,128]{1,0:T(8,128)(2,1)}) custom-call(s32[4]{0:T(128)S(1)} %get-tuple-element.55.here_ref, s32[1,128]{1,0:T(1,128)S(1)} %get-tuple-element.56.refs_0_, s32[1,128]{1,0:T(1,128)S(1)} %get-tuple-element.57.refs_1_, s32[1,128]{1,0:T(1,128)S(1)} %get-tuple-element.58.refs_2_, ...), custom_call_target="tpu_custom_call" | custom-call | tf_op jit(solution)/shard_map/cond/branch_1_fun/pallas_call | solution.py:312
  102.3 2.8 %collective-permute-start = (bf16[3072,128]{1,0:T(8,128)(2,1)}, bf16[3072,128]{1,0:T(8,128)(2,1)S(1)}, u32[]{:S(2)}, u32[]{:S(2)}) collective-permute-start(bf16[3072,128]{1,0:T(8,128)(2,1)} %get-tuple-element.59), channel_id=1, source_target_pairs={{0,2},{1,3},{2,4},{3,5},{4,6},{5,7},{6,0},{7,1},{8,10},{9,11},{10,... | collective-permute-start | bytes 2359304 | tf_op jit(solution)/shard_map/cond/branch_1_fun/ppermute | solution.py:37
  105.1 2.4 %collective-permute-start.2 = (bf16[3072,128]{1,0:T(8,128)(2,1)}, bf16[3072,128]{1,0:T(8,128)(2,1)S(1)}, u32[]{:S(2)}, u32[]{:S(2)}) collective-permute-start(bf16[3072,128]{1,0:T(8,128)(2,1)} %get-tuple-element.61), channel_id=1, source_target_pairs={{0,4},{1,5},{2,6},{3,7},{4,0},{5,1},{6,2},{7,3},{8,12},{9,13},{10,... | collective-permute-start | bytes 2359304 | tf_op jit(solution)/shard_map/cond/branch_1_fun/ppermute | solution.py:37
  107.4 6.9 %collective-permute-done.refs_4_ = bf16[3072,128]{1,0:T(8,128)(2,1)S(1)} collective-permute-done((bf16[3072,128]{1,0:T(8,128)(2,1)}, bf16[3072,128]{1,0:T(8,128)(2,1)S(1)}, u32[]{:S(2)}, u32[]{:S(2)}) %collective-permute-start) | collective-permute-done | bytes 786464 | tf_op jit(solution)/shard_map/cond/branch_1_fun/ppermute | solution.py:37
  114.3 2.1 %collective-permute-done.1.refs_5_ = bf16[3072,128]{1,0:T(8,128)(2,1)S(1)} collective-permute-done((bf16[3072,128]{1,0:T(8,128)(2,1)}, bf16[3072,128]{1,0:T(8,128)(2,1)S(1)}, u32[]{:S(2)}, u32[]{:S(2)}) %collective-permute-start.1) | collective-permute-done | bytes 786464 | tf_op jit(solution)/shard_map/cond/branch_1_fun/ppermute | solution.py:37
  116.4 7.5 %collective-permute-done.2.refs_6_ = bf16[3072,128]{1,0:T(8,128)(2,1)S(1)} collective-permute-done((bf16[3072,128]{1,0:T(8,128)(2,1)}, bf16[3072,128]{1,0:T(8,128)(2,1)S(1)}, u32[]{:S(2)}, u32[]{:S(2)}) %collective-permute-start.2) | collective-permute-done | bytes 786464 | tf_op jit(solution)/shard_map/cond/branch_1_fun/ppermute | solution.py:37
  123.9 6.9 %branch_1_fun.3 = (f32[2304,128]{1,0:T(8,128)}, bf16[2304,128]{1,0:T(8,128)(2,1)S(1)}) custom-call(s32[577]{0:T(1024)S(1)} %get-tuple-element.48.jobs_ref, bf16[12288,128]{1,0:T(8,128)(2,1)} %get-tuple-element.49.own_ref, bf16[12288,128]{1,0:T(8,128)(2,1)} %get-tuple-element.50.other_ref, bf16[2304,128]{1,0:T(8,128)(2,1)S(1)} %get-tuple-element.51.refs_3_.refs_0_, ...), custom_call_target="tpu_custom_call" | custom-call | tf_op jit(solution)/shard_map/cond/branch_1_fun/pallas_call | solution.py:261
  130.8 9.8 %collective-permute-start.30 = (bf16[2304,128]{1,0:T(8,128)(2,1)S(1)}, bf16[2304,128]{1,0:T(8,128)(2,1)S(1)}, u32[]{:S(2)}, u32[]{:S(2)}) collective-permute-start(bf16[2304,128]{1,0:T(8,128)(2,1)S(1)} %get-tuple-element.103), channel_id=1, source_target_pairs={{0,64},{1,65},{2,66},{3,67},{4,68},{5,69},{6,70},{7,71},{8,72},{9,... | collective-permute-start | bytes 1769480 | tf_op jit(solution)/shard_map/ppermute | solution.py:37
  140.9 1.4 collective-permute-done.30
  142.3 1.4 add_multiply_fusion
  (69 shorter events, 19.5 us)
Async XLA Ops:
  6.5 50.5 %all-gather.2.cloned.1.call-start = ((), (), s32[]{:S(2)}) async-start(), calls=%async_computation | async-start | bytes 3538944 | tf_op jit(solution)/shard_map/all_gather | solution.py:327
  7.3 20.3 %collective-permute-start.11 = (bf16[1536,128]{1,0:T(8,128)(2,1)}, bf16[1536,128]{1,0:T(8,128)(2,1)S(1)}, u32[]{:S(2)}, u32[]{:S(2)}) collective-permute-start(bf16[1536,128]{1,0:T(8,128)(2,1)} %bitcast.9), channel_id=1, source_target_pairs={{0,1},{1,128},{2,3},{3,130},{4,5},{5,132},{6,7},{7,134},{8,9},{9,1... | collective-permute-start | bytes 1179656 | tf_op jit(solution)/shard_map/ppermute | solution.py:37
  8.6 19.0 %collective-permute-start.12 = (bf16[1536,128]{1,0:T(8,128)(2,1)}, bf16[1536,128]{1,0:T(8,128)(2,1)S(1)}, u32[]{:S(2)}, u32[]{:S(2)}) collective-permute-start(bf16[1536,128]{1,0:T(8,128)(2,1)} %bitcast.10), channel_id=1, source_target_pairs={{0,129},{1,0},{2,131},{3,2},{4,133},{5,4},{6,135},{7,6},{8,137},{9... | collective-permute-start | bytes 1179656 | tf_op jit(solution)/shard_map/ppermute | solution.py:37
  10.2 17.5 %collective-permute-start.13 = (bf16[1536,128]{1,0:T(8,128)(2,1)}, bf16[1536,128]{1,0:T(8,128)(2,1)S(1)}, u32[]{:S(2)}, u32[]{:S(2)}) collective-permute-start(bf16[1536,128]{1,0:T(8,128)(2,1)} %bitcast.11), channel_id=1, source_target_pairs={{0,128},{1,129},{2,130},{3,131},{4,132},{5,133},{6,134},{7,135},{8... | collective-permute-start | bytes 1179656 | tf_op jit(solution)/shard_map/ppermute | solution.py:37
  12.9 6.3 %collective-permute-start.7 = (s32[1,128]{1,0:T(1,128)S(1)}, s32[1,128]{1,0:T(1,128)S(1)}, u32[]{:S(2)}, u32[]{:S(2)}) collective-permute-start(s32[1,128]{1,0:T(1,128)S(1)} %pad.13), channel_id=1, source_target_pairs={{0,56},{1,57},{2,58},{3,59},{4,60},{5,61},{6,62},{7,63},{8,0},{9,1... | collective-permute-start | bytes 1544 | tf_op jit(solution)/shard_map/ppermute | solution.py:37
  18.5 2.4 %collective-permute-start.9 = (s32[1,128]{1,0:T(1,128)S(1)}, s32[1,128]{1,0:T(1,128)S(1)}, u32[]{:S(2)}, u32[]{:S(2)}) collective-permute-start(s32[1,128]{1,0:T(1,128)S(1)} %pad.13), channel_id=1, source_target_pairs={{0,129},{1,0},{2,131},{3,2},{4,133},{5,4},{6,135},{7,6},{8,137},{9... | collective-permute-start | bytes 1544 | tf_op jit(solution)/shard_map/ppermute | solution.py:37
  20.9 5.9 %collective-permute-start.10 = (s32[2,128]{1,0:T(2,128)S(1)}, s32[2,128]{1,0:T(2,128)S(1)}, u32[]{:S(2)}, u32[]{:S(2)}) collective-permute-start(s32[2,128]{1,0:T(2,128)S(1)} %get-tuple-element.109), channel_id=1, source_target_pairs={{0,128},{1,129},{2,130},{3,131},{4,132},{5,133},{6,134},{7,135},{8... | collective-permute-start | bytes 3080 | tf_op jit(solution)/shard_map/ppermute | solution.py:37
  21.9 5.7 %collective-permute-start.8 = (s32[2,128]{1,0:T(2,128)S(1)}, s32[2,128]{1,0:T(2,128)S(1)}, u32[]{:S(2)}, u32[]{:S(2)}) collective-permute-start(s32[2,128]{1,0:T(2,128)S(1)} %get-tuple-element.110), channel_id=1, source_target_pairs={{0,48},{1,49},{2,50},{3,51},{4,52},{5,53},{6,54},{7,55},{8,56},{9,... | collective-permute-start | bytes 3080 | tf_op jit(solution)/shard_map/ppermute | solution.py:37
  28.7 28.3 %collective-permute-start.14 = (bf16[6144,128]{1,0:T(8,128)(2,1)S(1)}, bf16[6144,128]{1,0:T(8,128)(2,1)S(1)}, u32[]{:S(2)}, u32[]{:S(2)}) collective-permute-start(bf16[6144,128]{1,0:T(8,128)(2,1)S(1)} %pad_maximum_fusion.refs_0_), channel_id=1, source_target_pairs={{0,2},{1,3},{2,4},{3,5},{4,6},{5,7},{6,0},{7,1},{8,10},{9,11},{10,... | collective-permute-start | bytes 4718600 | tf_op jit(solution)/shard_map/ppermute | solution.py:37
  30.3 26.7 %collective-permute-start.15 = (bf16[6144,128]{1,0:T(8,128)(2,1)S(1)}, bf16[6144,128]{1,0:T(8,128)(2,1)}, u32[]{:S(2)}, u32[]{:S(2)}) collective-permute-start(bf16[6144,128]{1,0:T(8,128)(2,1)S(1)} %pad_maximum_fusion.refs_0_), channel_id=1, source_target_pairs={{0,6},{1,7},{2,0},{3,1},{4,2},{5,3},{6,4},{7,5},{8,14},{9,15},{10,... | collective-permute-start | bytes 4718600 | tf_op jit(solution)/shard_map/ppermute | solution.py:37
  31.5 2.8 %collective-permute-start.18 = (s32[4,128]{1,0:T(4,128)S(1)}, s32[4,128]{1,0:T(4,128)S(1)}, u32[]{:S(2)}, u32[]{:S(2)}) collective-permute-start(s32[4,128]{1,0:T(4,128)S(1)} %get-tuple-element.85), channel_id=1, source_target_pairs={{0,6},{1,7},{2,0},{3,1},{4,2},{5,3},{6,4},{7,5},{8,14},{9,15},{10,... | collective-permute-start | bytes 6152 | tf_op jit(solution)/shard_map/ppermute | solution.py:37
  31.5 6.5 %collective-permute-start.16 = (s32[4,128]{1,0:T(4,128)S(1)}, s32[4,128]{1,0:T(4,128)S(1)}, u32[]{:S(2)}, u32[]{:S(2)}) collective-permute-start(s32[4,128]{1,0:T(4,128)S(1)} %get-tuple-element.84), channel_id=1, source_target_pairs={{0,32},{1,33},{2,34},{3,35},{4,36},{5,37},{6,38},{7,39},{8,40},{9,... | collective-permute-start | bytes 6152 | tf_op jit(solution)/shard_map/ppermute | solution.py:37
  34.4 21.9 %collective-permute-start.19 = (s32[8,128]{1,0:T(8,128)S(1)}, s32[8,128]{1,0:T(8,128)S(1)}, u32[]{:S(2)}, u32[]{:S(2)}) collective-permute-start(s32[8,128]{1,0:T(8,128)S(1)} %pad_add_fusion.2), channel_id=1, source_target_pairs={{0,4},{1,5},{2,6},{3,7},{4,0},{5,1},{6,2},{7,3},{8,12},{9,13},{10,... | collective-permute-start | bytes 12296 | tf_op jit(solution)/shard_map/ppermute | solution.py:37
  38.0 24.1 %copy-start.3 = (s32[8,128]{1,0:T(8,128)}, s32[8,128]{1,0:T(8,128)S(1)}, u32[]{:S(2)}) copy-start(s32[8,128]{1,0:T(8,128)S(1)} %pad_add_fusion.1.own_ref) | copy-start | bytes 12292
  38.0 19.0 %collective-permute-start.17 = (s32[8,128]{1,0:T(8,128)S(1)}, s32[8,128]{1,0:T(8,128)S(1)}, u32[]{:S(2)}, u32[]{:S(2)}) collective-permute-start(s32[8,128]{1,0:T(8,128)S(1)} %pad_add_fusion.1.own_ref), channel_id=1, source_target_pairs={{0,64},{1,65},{2,66},{3,67},{4,68},{5,69},{6,70},{7,71},{8,72},{9,... | collective-permute-start | bytes 12296 | tf_op jit(solution)/shard_map/ppermute | solution.py:37
  57.1 18.3 %collective-permute-start.20 = (bf16[12288,128]{1,0:T(8,128)(2,1)}, bf16[12288,128]{1,0:T(8,128)(2,1)}, u32[]{:S(2)}, u32[]{:S(2)}) collective-permute-start(bf16[12288,128]{1,0:T(8,128)(2,1)} %all-gather.2.cloned.1.call-done.own_ref), channel_id=1, source_target_pairs={{0,64},{1,65},{2,66},{3,67},{4,68},{5,69},{6,70},{7,71},{8,72},{9,... | collective-permute-start | bytes 9437192 | tf_op jit(solution)/shard_map/ppermute | solution.py:37
  62.1 12.1 %collective-permute-start.21 = (bf16[3072,128]{1,0:T(8,128)(2,1)}, bf16[3072,128]{1,0:T(8,128)(2,1)}, u32[]{:S(2)}, u32[]{:S(2)}) collective-permute-start(bf16[3072,128]{1,0:T(8,128)(2,1)} %slice.27), channel_id=1, source_target_pairs={{0,2},{1,3},{2,4},{3,5},{4,6},{5,7},{6,0},{7,1},{8,10},{9,11},{10,... | collective-permute-start | bytes 2359304 | tf_op jit(solution)/shard_map/ppermute | solution.py:37
  62.9 12.5 %collective-permute-start.22 = (bf16[3072,128]{1,0:T(8,128)(2,1)}, bf16[3072,128]{1,0:T(8,128)(2,1)}, u32[]{:S(2)}, u32[]{:S(2)}) collective-permute-start(bf16[3072,128]{1,0:T(8,128)(2,1)} %slice.28), channel_id=1, source_target_pairs={{0,6},{1,7},{2,0},{3,1},{4,2},{5,3},{6,4},{7,5},{8,14},{9,15},{10,... | collective-permute-start | bytes 2359304 | tf_op jit(solution)/shard_map/ppermute | solution.py:37
  79.7 7.0 %copy-start.5 = (s32[4,128]{1,0:T(4,128)S(1)}, s32[4,128]{1,0:T(4,128)}, u32[]{:S(2)}) copy-start(s32[4,128]{1,0:T(4,128)} %get-tuple-element.99) | copy-start | bytes 6148
  79.7 2.9 %collective-permute-start.23 = (bf16[2304,128]{1,0:T(8,128)(2,1)S(1)}, bf16[2304,128]{1,0:T(8,128)(2,1)S(1)}, u32[]{:S(2)}, u32[]{:S(2)}) collective-permute-start(bf16[2304,128]{1,0:T(8,128)(2,1)S(1)} %get-tuple-element.97), channel_id=1, source_target_pairs={{0,64},{1,65},{2,66},{3,67},{4,68},{5,69},{6,70},{7,71},{8,72},{9,... | collective-permute-start | bytes 1769480 | tf_op jit(solution)/shard_map/ppermute | solution.py:37
  82.7 13.3 %collective-permute-start.27 = (bf16[2304,128]{1,0:T(8,128)(2,1)S(1)}, bf16[2304,128]{1,0:T(8,128)(2,1)S(1)}, u32[]{:S(2)}, u32[]{:S(2)}) collective-permute-start(bf16[2304,128]{1,0:T(8,128)(2,1)S(1)} %add_convert_fusion), channel_id=1, source_target_pairs={{0,1},{1,128},{2,3},{3,130},{4,5},{5,132},{6,7},{7,134},{8,9},{9,1... | collective-permute-start | bytes 1769480 | tf_op jit(solution)/shard_map/ppermute | solution.py:37
  84.1 12.0 %collective-permute-start.28 = (bf16[2304,128]{1,0:T(8,128)(2,1)S(1)}, bf16[2304,128]{1,0:T(8,128)(2,1)S(1)}, u32[]{:S(2)}, u32[]{:S(2)}) collective-permute-start(bf16[2304,128]{1,0:T(8,128)(2,1)S(1)} %add_convert_fusion), channel_id=1, source_target_pairs={{0,129},{1,0},{2,131},{3,2},{4,133},{5,4},{6,135},{7,6},{8,137},{9... | collective-permute-start | bytes 1769480 | tf_op jit(solution)/shard_map/ppermute | solution.py:37
  85.5 14.7 %collective-permute-start.29 = (bf16[2304,128]{1,0:T(8,128)(2,1)S(1)}, bf16[2304,128]{1,0:T(8,128)(2,1)S(1)}, u32[]{:S(2)}, u32[]{:S(2)}) collective-permute-start(bf16[2304,128]{1,0:T(8,128)(2,1)S(1)} %add_convert_fusion), channel_id=1, source_target_pairs={{0,128},{1,129},{2,130},{3,131},{4,132},{5,133},{6,134},{7,135},{8... | collective-permute-start | bytes 1769480 | tf_op jit(solution)/shard_map/ppermute | solution.py:37
  86.6 3.9 %collective-permute-start.24 = (s32[1,128]{1,0:T(1,128)S(1)}, s32[1,128]{1,0:T(1,128)S(1)}, u32[]{:S(2)}, u32[]{:S(2)}) collective-permute-start(s32[1,128]{1,0:T(1,128)S(1)} %get-tuple-element.104), channel_id=1, source_target_pairs={{0,6},{1,7},{2,0},{3,1},{4,2},{5,3},{6,4},{7,5},{8,14},{9,15},{10,... | collective-permute-start | bytes 1544 | tf_op jit(solution)/shard_map/ppermute | solution.py:37
  88.5 3.3 %collective-permute-start.25 = (s32[1,128]{1,0:T(1,128)S(1)}, s32[1,128]{1,0:T(1,128)S(1)}, u32[]{:S(2)}, u32[]{:S(2)}) collective-permute-start(s32[1,128]{1,0:T(1,128)S(1)} %get-tuple-element.106), channel_id=1, source_target_pairs={{0,2},{1,3},{2,4},{3,5},{4,6},{5,7},{6,0},{7,1},{8,10},{9,11},{10,... | collective-permute-start | bytes 1544 | tf_op jit(solution)/shard_map/ppermute | solution.py:37
  90.6 4.3 %collective-permute-start.26 = (s32[1,128]{1,0:T(1,128)S(1)}, s32[1,128]{1,0:T(1,128)S(1)}, u32[]{:S(2)}, u32[]{:S(2)}) collective-permute-start(s32[1,128]{1,0:T(1,128)S(1)} %get-tuple-element.105), channel_id=1, source_target_pairs={{0,4},{1,5},{2,6},{3,7},{4,0},{5,1},{6,2},{7,3},{8,12},{9,13},{10,... | collective-permute-start | bytes 1544 | tf_op jit(solution)/shard_map/ppermute | solution.py:37
  100.2 40.5 %copy-start.6 = (s32[6,2]{0,1:T(2,128)S(1)}, s32[6,2]{0,1:T(2,128)}, u32[]{:S(2)}) copy-start(s32[6,2]{0,1:T(2,128)} %param.6) | copy-start | bytes 148
  100.2 40.6 %copy-start.2 = (bf16[6,2,128,128]{3,2,1,0:T(8,128)(2,1)S(1)}, bf16[6,2,128,128]{3,2,1,0:T(8,128)(2,1)}, u32[]{:S(2)}) copy-start(bf16[6,2,128,128]{3,2,1,0:T(8,128)(2,1)} %param.5) | copy-start | bytes 1179652
  102.3 12.0 %collective-permute-start = (bf16[3072,128]{1,0:T(8,128)(2,1)}, bf16[3072,128]{1,0:T(8,128)(2,1)S(1)}, u32[]{:S(2)}, u32[]{:S(2)}) collective-permute-start(bf16[3072,128]{1,0:T(8,128)(2,1)} %get-tuple-element.59), channel_id=1, source_target_pairs={{0,2},{1,3},{2,4},{3,5},{4,6},{5,7},{6,0},{7,1},{8,10},{9,11},{10,... | collective-permute-start | bytes 2359304 | tf_op jit(solution)/shard_map/cond/branch_1_fun/ppermute | solution.py:37
  105.1 11.3 %collective-permute-start.1 = (bf16[3072,128]{1,0:T(8,128)(2,1)}, bf16[3072,128]{1,0:T(8,128)(2,1)S(1)}, u32[]{:S(2)}, u32[]{:S(2)}) collective-permute-start(bf16[3072,128]{1,0:T(8,128)(2,1)} %get-tuple-element.60), channel_id=1, source_target_pairs={{0,6},{1,7},{2,0},{3,1},{4,2},{5,3},{6,4},{7,5},{8,14},{9,15},{10,... | collective-permute-start | bytes 2359304 | tf_op jit(solution)/shard_map/cond/branch_1_fun/ppermute | solution.py:37
  105.1 18.9 %collective-permute-start.2 = (bf16[3072,128]{1,0:T(8,128)(2,1)}, bf16[3072,128]{1,0:T(8,128)(2,1)S(1)}, u32[]{:S(2)}, u32[]{:S(2)}) collective-permute-start(bf16[3072,128]{1,0:T(8,128)(2,1)} %get-tuple-element.61), channel_id=1, source_target_pairs={{0,4},{1,5},{2,6},{3,7},{4,0},{5,1},{6,2},{7,3},{8,12},{9,13},{10,... | collective-permute-start | bytes 2359304 | tf_op jit(solution)/shard_map/cond/branch_1_fun/ppermute | solution.py:37
  130.8 11.5 %collective-permute-start.30 = (bf16[2304,128]{1,0:T(8,128)(2,1)S(1)}, bf16[2304,128]{1,0:T(8,128)(2,1)S(1)}, u32[]{:S(2)}, u32[]{:S(2)}) collective-permute-start(bf16[2304,128]{1,0:T(8,128)(2,1)S(1)} %get-tuple-element.103), channel_id=1, source_target_pairs={{0,64},{1,65},{2,66},{3,67},{4,68},{5,69},{6,70},{7,71},{8,72},{9,... | collective-permute-start | bytes 1769480 | tf_op jit(solution)/shard_map/ppermute | solution.py:37
  (3 other events, 10.9 us)
Sparse Core Ops, SparseCore 0:
  9.1 47.7 all-gather.1

commit v3 on v2

v3 whole, which is shorter than its diff:
```python
import functools

import jax
import jax.numpy as jnp
from jax import lax
from jax.experimental import pallas as pl
from jax.experimental.pallas import tpu as pltpu
from jax.sharding import PartitionSpec as P

BLK = 128
KA = 2
KC = 3
TP = 24
ROWS = 6
OUTS = ROWS * KC
LEFT = ROWS * KA
ROOM = 22
COUNT, MOST = 32, 33
PAY = LEFT * BLK + 16
UNIT = 16
SLOTS = 64
JOBS = 2 * ROWS * 8 * KC
ALL = ("row", "col", "depth")


def chip_of(device):
    row, col, depth = device // 64, device // 8 % 8, device % 8
    return row // 2 * 2 + depth % 2, depth // 2, col, row % 2


def device_of(x, y, z, core):
    return (x // 2 * 2 + core) * 64 + z * 8 + y * 2 + x % 2


def move(array, rule):
    pairs = []
    for device in range(256):
        x, y, z, core = rule(*chip_of(device))
        pairs.append((device, device_of(x % 4, y % 4, z % 8, core)))
    return lax.ppermute(array, ALL, pairs)


def first_ring(array, step):
    return move(array, lambda x, y, z, core: (x + step * (1 - core), y + step * core, z, core))


def second_ring(array, step):
    return move(array, lambda x, y, z, core: (x + step * core, y + step * (1 - core), z, core))


def swap(array):
    return move(array, lambda x, y, z, core: (x, y, z, 1 - core))


def ring_order(away):
    away = away & 3
    return jnp.where(away == 2, 3, jnp.where(away == 3, 2, away))


def first_pieces(piece):
    far, plus, minus = [first_ring(piece, step) for step in (2, 1, -1)]
    return piece, plus, minus, far


def far_pieces(plus, minus):
    half = plus.shape[0] // 2
    return second_ring(plus[:half], 1), second_ring(minus[half:], -1)


def block_copy(ref, unit, target, sem):
    offset = pl.multiple_of(unit * UNIT, UNIT)
    return pltpu.make_async_copy(ref.at[pl.ds(offset, BLK)], target, sem)


def plan_groups(here_ref, which, group_code):
    core, x, y = here_ref[0] ^ which, here_ref[1], here_ref[2]
    first, second = jnp.where(core == 0, x, y), jnp.where(core == 0, y, x)
    for group in range(16):
        at_x, at_y = group // 8 * 2 + group % 2, group // 4 % 2 * 2 + group // 2 % 2
        far = jnp.where(core == 0, at_x, at_y)
        group_code[0, which * 16 + group] = ring_order(first - far)
        group_code[1, which * 16 + group] = ring_order(second - jnp.where(core == 0, at_y, at_x))
        group_code[2, which * 16 + group] = far


def plan_scan(marks_ref, z, panels, plane_ref, group_code, slots, add):
    def scan_row(row, carry):
        wanted = [marks_ref[z, LEFT + row * KC + u] for u in range(KC)]
        for panel, base in panels:
            for side in range(KA):
                column = marks_ref[panel, row * KA + side]

                @pl.when(column >= 0)
                def _(panel=panel, base=base, side=side, column=column):
                    quarter = (column * 43) >> 8
                    place = column - quarter * ROWS
                    group = base + quarter
                    inner, outer = group_code[0, group], group_code[1, group]
                    table = (group & 16) + outer * 4 + inner
                    founds = []
                    for slot in range(slots):
                        start = place * KA if slots == KA else LEFT + place * KC
                        have = plane_ref[table, start + slot]
                        found = jnp.where(have == wanted[0], 0, jnp.where(have == wanted[1], 1, 2))
                        founds.append(jnp.where((found < 2) | (have == wanted[2]), found, -1))

                    @pl.when(functools.reduce(jnp.maximum, founds) >= 0)
                    def _():
                        left = (panel * LEFT + row * KA + side) * (BLK // UNIT)
                        for slot, found in enumerate(founds):
                            out = row * KC + found
                            pl.when(found >= 0)(functools.partial(add, group, inner, outer, place, slot, left, out))

        return carry

    lax.fori_loop(0, ROWS, scan_row, 0)


def plan_x_kernel(here_ref, own_ref, plane_ref, jobs, group_code):
    core, z = here_ref[0], here_ref[3]
    plan_groups(here_ref, 0, group_code)
    plan_groups(here_ref, 1, group_code)
    jobs[0] = 0

    def add(group, inner, outer, place, slot, left, out):
        count = jobs[0]
        jobs[0] = count + 1
        jobs[1 + count] = (left << 6) | out
        source = jnp.where(outer < 3, outer, 3 + (inner >> 1)) + jnp.where(group >= 16, 5, 0)
        ahead = jnp.where(outer < 3, inner, inner & 1) * (PAY // UNIT)
        jobs[1 + JOBS + count] = (source << 10) | (ahead + (place * KA + slot) * (BLK // UNIT))

    panels = [(panel, ((panel // 2 % 2) ^ core) * 16 + (panel // 4 * 2 + panel % 2) * 4) for panel in range(8)]
    plan_scan(own_ref, z, panels, plane_ref, group_code, KA, add)


def plan_s_kernel(here_ref, own_ref, other_ref, plane_ref, jobs, takes, seen, group_code):
    core, z = here_ref[0], here_ref[3]
    plan_groups(here_ref, 0, group_code)
    jobs[0] = 0
    for outer in range(4):
        takes[outer, COUNT] = 0

    def clear(n, carry):
        seen[n] = -1
        return carry

    lax.fori_loop(0, 16 * OUTS, clear, 0, unroll=16)

    def add(half, group, inner, outer, place, slot, left, out):
        block = place * KC + slot
        mark = group * OUTS + block

        @pl.when((outer > 0) & (seen[mark] < 0))
        def _():
            rank = takes[outer, COUNT]
            takes[outer, COUNT] = rank + 1
            seen[mark] = rank

            @pl.when(rank < ROOM)
            def _():
                takes[outer, rank] = (group_code[2, group] << 5) | block

        count = jobs[0]
        jobs[0] = count + 1
        jobs[1 + count] = ((half * 8 * LEFT * (BLK // UNIT) + left) << 6) | (half * OUTS + out)
        near = (inner << 10) | (block * (BLK // UNIT))
        packed = ((3 + outer) << 10) | ((seen[mark] & 31) * (BLK // UNIT))
        dense = ((6 + outer) << 10) | ((inner * OUTS + block) * (BLK // UNIT))
        jobs[1 + JOBS + count] = jnp.where(outer == 0, near, packed)
        jobs[1 + 2 * JOBS + count] = jnp.where(outer == 0, near, dense)

    panels = [(panel // 2 * 4 + 2 * core + panel % 2, panel * 4) for panel in range(4)]
    for half, marks_ref in enumerate((own_ref, other_ref)):
        plan_scan(marks_ref, z, panels, plane_ref, group_code, KC, functools.partial(add, half))
    most = jnp.maximum(takes[1, COUNT], jnp.maximum(takes[2, COUNT], takes[3, COUNT]))
    for outer in range(4):
        takes[outer, MOST] = most


SMEM = pl.BlockSpec(memory_space=pltpu.SMEM)
VMEM = pl.BlockSpec(memory_space=pltpu.VMEM)
ANY = pl.BlockSpec(memory_space=pl.ANY)


JOB_TABLE = jax.ShapeDtypeStruct((1 + 3 * JOBS,), jnp.int32)


def plan_x(here, own, plane):
    return pl.pallas_call(
        plan_x_kernel,
        out_shape=JOB_TABLE,
        in_specs=[SMEM] * 3,
        out_specs=SMEM,
        scratch_shapes=[pltpu.SMEM((3, 32), jnp.int32)],
    )(here, own, plane)


def plan_s(here, own, other, plane):
    return pl.pallas_call(
        plan_s_kernel,
        out_shape=(JOB_TABLE, jax.ShapeDtypeStruct((4, BLK), jnp.int32)),
        in_specs=[SMEM] * 4,
        out_specs=(SMEM, SMEM),
        scratch_shapes=[pltpu.SMEM((16 * OUTS,), jnp.int32), pltpu.SMEM((3, 16), jnp.int32)],
    )(here, own, other, plane)


def product_kernel(lefts, rights, most_ref, jobs_ref, *refs):
    left_refs, right_refs, refs = refs[:lefts], refs[lefts : lefts + rights], refs[lefts + rights :]
    outs_refs, (total, left_buf, right_buf, sems) = refs[:lefts], refs[lefts:]
    count = jobs_ref[0]
    codes = jnp.where(most_ref[0] <= ROOM, 1 + JOBS, 1 + 2 * JOBS)

    def start(n):
        slot = n & (SLOTS - 1)
        left = jobs_ref[1 + n] >> 6
        code = jobs_ref[codes + n]
        source, unit = code >> 10, code & 1023
        whole = 8 * LEFT * (BLK // UNIT)
        for index, ref in enumerate(left_refs):

            @pl.when((left >= index * whole) & (left < (index + 1) * whole))
            def _(ref=ref, index=index):
                block_copy(ref, left - index * whole, left_buf.at[slot], sems.at[0, slot]).start()

        def right(low, high):
            if high - low == 1:
                block_copy(right_refs[low], unit, right_buf.at[slot], sems.at[1, slot]).start()
            else:
                middle = (low + high) // 2
                pl.when(source < middle)(functools.partial(right, low, middle))
                pl.when(source >= middle)(functools.partial(right, middle, high))

        right(0, rights)

    def wait(n):
        slot = n & (SLOTS - 1)
        block_copy(left_refs[0], 0, left_buf.at[slot], sems.at[0, slot]).wait()
        block_copy(left_refs[0], 0, right_buf.at[slot], sems.at[1, slot]).wait()

    def first(n, carry):
        start(n)
        return carry

    lax.fori_loop(0, jnp.minimum(count, SLOTS), first, 0)
    total[...] = jnp.zeros_like(total)

    def multiply(group, carry):
        at = [group * 4 + index for index in range(4)]
        for n in at:
            pl.when(n < count)(functools.partial(wait, n))
        outs = [jnp.where(n < count, jobs_ref[jnp.minimum(1 + n, JOBS)] & 63, lefts * OUTS) for n in at]
        slots = [n & (SLOTS - 1) for n in at]
        dots = [jnp.dot(left_buf[slot], right_buf[slot], preferred_element_type=jnp.float32) for slot in slots]
        for out, dot in zip(outs, dots):
            total[out] += dot
        for n in at:
            pl.when(n + SLOTS < count)(functools.partial(start, n + SLOTS))
        return carry

    lax.fori_loop(0, (count + 3) // 4, multiply, 0)
    for half, ref in enumerate(outs_refs):
        for block in range(OUTS):
            ref[pl.ds(block * BLK, BLK), :] = total[half * OUTS + block].astype(jnp.bfloat16)


def product(most, jobs, lefts, rights):
    return pl.pallas_call(
        functools.partial(product_kernel, len(lefts), len(rights)),
        out_shape=(jax.ShapeDtypeStruct((OUTS * BLK, BLK), jnp.bfloat16),) * len(lefts),
        in_specs=[SMEM] * 2 + [ANY] * (len(lefts) + len(rights)),
        out_specs=(VMEM,) * len(lefts),
        scratch_shapes=[
            pltpu.VMEM((len(lefts) * OUTS + 1, BLK, BLK), jnp.float32),
            pltpu.VMEM((SLOTS, BLK, BLK), jnp.bfloat16),
            pltpu.VMEM((SLOTS, BLK, BLK), jnp.bfloat16),
            pltpu.SemaphoreType.DMA((2, SLOTS)),
        ],
        compiler_params=pltpu.CompilerParams(vmem_limit_bytes=24 * 1024 * 1024),
    )(most, jobs, *lefts, *rights)


def pack_kernel(here_ref, *refs):
    lists, pieces, outs, sems = refs[:3], refs[3:7], refs[7:10], refs[10]
    first = jnp.where(here_ref[0] == 0, here_ref[1], here_ref[2])

    for target, (asked, out) in enumerate(zip(lists, outs)):

        def start(n, carry, target=target, out=out, asked=asked):
            code = asked[0, n]
            inner = ring_order(first - (code >> 5))
            offset = pl.multiple_of(n * BLK, BLK)
            for index, ref in enumerate(pieces):

                @pl.when(inner == index)
                def _(ref=ref):
                    block_copy(ref, (code & 31) * (BLK // UNIT), out.at[pl.ds(offset, BLK)], sems.at[target, n]).start()

            return carry

        lax.fori_loop(0, jnp.minimum(asked[0, COUNT], ROOM), start, 0)

    for target, (asked, out) in enumerate(zip(lists, outs)):

        def wait(n, carry, target=target, out=out):
            block_copy(pieces[0], 0, out.at[pl.ds(0, BLK)], sems.at[target, n]).wait()
            return carry

        lax.fori_loop(0, jnp.minimum(asked[0, COUNT], ROOM), wait, 0)


def pack(here, lists, pieces):
    shape = jax.ShapeDtypeStruct((ROOM * BLK, BLK), jnp.bfloat16)
    return pl.pallas_call(
        pack_kernel,
        out_shape=(shape,) * 3,
        in_specs=[SMEM] * 4 + [ANY] * 4,
        out_specs=(VMEM,) * 3,
        scratch_shapes=[pltpu.SemaphoreType.DMA((3, ROOM))],
    )(here, *lists, *pieces)


def blank(rows):
    shape = jax.ShapeDtypeStruct((rows, BLK), jnp.bfloat16)
    return tuple(pl.pallas_call(lambda *refs: None, out_shape=(shape,) * 3, out_specs=(ANY,) * 3)())


def second_pieces(most, here, lists, pieces):
    steps = (1, -1, 2)

    def packed(pieces):
        sent = pack(here, lists, pieces)
        return tuple(second_ring(part, step) for part, step in zip(sent, steps)) + blank(4 * OUTS * BLK)

    def dense(pieces):
        near = jnp.concatenate(pieces, axis=0)
        return blank(ROOM * BLK) + tuple(second_ring(near, step) for step in steps)

    return pieces + lax.cond(most[0] <= ROOM, packed, dense, pieces)


def marks_of(array):
    return array.reshape(-1, PAY, BLK)[:, LEFT * BLK, :].astype(jnp.int32)


def local(block_values, block_columns, pattern_columns):
    row, depth, z = lax.axis_index("row"), lax.axis_index("depth"), lax.axis_index("col")
    here = jnp.stack([row % 2, row // 2 * 2 + depth % 2, depth // 2, z]).astype(jnp.int32)
    own_pattern = lax.dynamic_slice_in_dim(pattern_columns, depth * ROWS, ROWS, 0)

    marks = jnp.concatenate([block_columns.reshape(1, -1), own_pattern.reshape(1, -1)], axis=1)
    marks = jnp.pad(marks.astype(jnp.bfloat16), ((0, 15), (0, BLK - marks.shape[1])))
    values = block_values.reshape(LEFT * BLK, BLK)
    left = lax.all_gather(values, "col", axis=0, tiled=True)
    piece = lax.optimization_barrier(jnp.concatenate([values, marks], axis=0))

    near = jnp.concatenate(first_pieces(piece), axis=0)
    near, marks = lax.optimization_barrier((near, marks[:1].astype(jnp.int32)))
    near_marks = marks_of(near)
    plus, minus, far_marks = second_ring(near, 1), second_ring(near, -1), second_ring(near_marks, 2)
    row_marks = lax.all_gather(marks, "col", axis=0, tiled=True)
    plus, minus, far_marks, row_marks = lax.optimization_barrier((plus, minus, far_marks, row_marks))
    other_marks = swap(row_marks)
    far = far_pieces(plus, minus)
    plane_marks = jnp.concatenate([near_marks, marks_of(plus), marks_of(minus), far_marks], axis=0)
    both_marks = jnp.concatenate([plane_marks, swap(plane_marks)], axis=0)
    x_jobs = plan_x(here, row_marks, both_marks)
    s_jobs, takes = plan_s(here, row_marks, other_marks, plane_marks)
    far, x_jobs, s_jobs = lax.optimization_barrier((far, x_jobs, s_jobs))
    right = (near, plus, minus) + far
    other_right = tuple(swap(part) for part in right)
    left, plus = lax.optimization_barrier((left, plus))

    zero = jnp.zeros((1,), jnp.int32)
    (square,) = product(zero, x_jobs, (left,), right + other_right)
    square, left = lax.optimization_barrier((square, left))
    first, *rest = first_pieces(square)
    left_other = swap(left)
    asked = tuple(second_ring(takes[index : index + 1], step) for index, step in ((1, -1), (2, 1), (3, 2)))
    most = functools.reduce(jnp.maximum, asked, takes[:1])[0, MOST:][:1]

    stored = jnp.where((block_columns >= 0)[:, :, None, None], block_values, 0).astype(jnp.float32)
    scaled = 1.5 * jnp.pad(stored, ((0, 0), (0, KC - KA), (0, 0), (0, 0))).reshape(OUTS * BLK, BLK)
    first, scaled = lax.optimization_barrier((first, scaled))

    s_right = second_pieces(most, here, asked, (first, *rest))
    mine, theirs = product(most, s_jobs, (left, left_other), s_right)
    cube = mine.astype(jnp.float32) + swap(theirs).astype(jnp.float32)
    return (scaled - 0.5 * cube).astype(jnp.bfloat16).reshape(ROWS, KC, BLK, BLK)


def solution(mesh):
    placed = (P(("row", "depth"), "col", None, None), P(("row", "depth"), "col"), P("row", "col"))
    return jax.shard_map(
        local,
        mesh=mesh,
        in_specs=placed,
        out_specs=P(("row", "depth"), "col", None, None),
        check_vma=False,
    )
```

time: 151 us -> 147 us (0.974)
  the two profiles are of different devices: /device:TPU:5 before, /device:TPU:1 now
where the time goes in v3:
time: 147 us; the launch traced here: 145 us
  waiting for transfers between devices  43.9 us (30%)
  starting transfers between devices  29.8 us (20%)
  Pallas kernels  26.7 us (18%)
  blocking collectives  16.9 us (11%)
  between operations  14.2 us (10%)
  local copies, waits for them, and re-layouts  7.48 us (5%)
  other arithmetic  6.01 us (4%)
    ppermute x26, waiting for transfers between devices, move(): return lax.ppermute(array, ALL, pairs)  43.2 us
    ppermute x26, starting transfers between devices, move(): return lax.ppermute(array, ALL, pairs)  29.8 us
    all_gather x1, blocking collectives, local(): row_marks = lax.all_gather(marks, 'col', axis=0, tiled=True)  16.9 us
    pallas_call x2, Pallas kernels, product(): pl.pallas_call(functools.partial(product_kernel, len(lefts), len(rights))...  11.1 us
    pallas_call x1, Pallas kernels, plan_s(): pl.pallas_call(plan_s_kernel, out_shape=(JOB_TABLE, jax.ShapeDtypeStruct(...  7.21 us
    pallas_call x1, Pallas kernels, plan_x(): pl.pallas_call(plan_x_kernel, out_shape=JOB_TABLE, in_specs=[SMEM] * 3, o...  4.85 us
    pallas_call x1, Pallas kernels, pack(): pl.pallas_call(pack_kernel, out_shape=(shape,) * 3, in_specs=[SMEM] * 4 +...  3.52 us
    slice x2, local copies, waits for them, and re-layouts, far_pieces(): return (second_ring(plus[:half], 1), second_ring(minus[half:], -1))  3.08 us
  transfers between devices with their start and end apart: 27, of which 13 were waited for; matrix products, arithmetic and copies ran while one was open for 8% of the time, Pallas kernels for 11%

profile of v3, /device:TPU:1, one launch (start us, length us, event | category | flops | bytes accessed | tf_op | source)
XLA Modules:
  0.0 145.1 jit_solution(10388997859704741560)
XLA Ops:
  10.2 2.2 %collective-permute-start.6 = (bf16[1552,128]{1,0:T(8,128)(2,1)S(1)}, bf16[1552,128]{1,0:T(8,128)(2,1)S(1)}, u32[]{:S(2)}, u32[]{:S(2)}) collective-permute-start(bf16[1552,128]{1,0:T(8,128)(2,1)S(1)} %pad_maximum_fusion.1), channel_id=1, source_target_pairs={{0,1},{1,128},{2,3},{3,130},{4,5},{5,132},{6,7},{7,134},{8,9},{9,1... | collective-permute-start | bytes 1191944 | tf_op jit(solution)/shard_map/ppermute | solution.py:40
  12.4 1.5 %collective-permute-start.7 = (bf16[1552,128]{1,0:T(8,128)(2,1)S(1)}, bf16[1552,128]{1,0:T(8,128)(2,1)S(1)}, u32[]{:S(2)}, u32[]{:S(2)}) collective-permute-start(bf16[1552,128]{1,0:T(8,128)(2,1)S(1)} %pad_maximum_fusion.1), channel_id=1, source_target_pairs={{0,129},{1,0},{2,131},{3,2},{4,133},{5,4},{6,135},{7,6},{8,137},{9... | collective-permute-start | bytes 1191944 | tf_op jit(solution)/shard_map/ppermute | solution.py:40
  13.9 1.6 %collective-permute-start.8 = (bf16[1552,128]{1,0:T(8,128)(2,1)S(1)}, bf16[1552,128]{1,0:T(8,128)(2,1)S(1)}, u32[]{:S(2)}, u32[]{:S(2)}) collective-permute-start(bf16[1552,128]{1,0:T(8,128)(2,1)S(1)} %pad_maximum_fusion.1), channel_id=1, source_target_pairs={{0,128},{1,129},{2,130},{3,131},{4,132},{5,133},{6,134},{7,135},{8... | collective-permute-start | bytes 1191944 | tf_op jit(solution)/shard_map/ppermute | solution.py:40
  15.5 3.9 %collective-permute-done.6 = bf16[1552,128]{1,0:T(8,128)(2,1)S(1)} collective-permute-done((bf16[1552,128]{1,0:T(8,128)(2,1)S(1)}, bf16[1552,128]{1,0:T(8,128)(2,1)S(1)}, u32[]{:S(2)}, u32[]{:S(2)}) %collective-permute-start.6) | collective-permute-done | bytes 397344 | tf_op jit(solution)/shard_map/ppermute | solution.py:40
  19.4 3.6 %collective-permute-done.7 = bf16[1552,128]{1,0:T(8,128)(2,1)S(1)} collective-permute-done((bf16[1552,128]{1,0:T(8,128)(2,1)S(1)}, bf16[1552,128]{1,0:T(8,128)(2,1)S(1)}, u32[]{:S(2)}, u32[]{:S(2)}) %collective-permute-start.7) | collective-permute-done | bytes 397344 | tf_op jit(solution)/shard_map/ppermute | solution.py:40
  23.0 1.8 %collective-permute-done.8 = bf16[1552,128]{1,0:T(8,128)(2,1)S(1)} collective-permute-done((bf16[1552,128]{1,0:T(8,128)(2,1)S(1)}, bf16[1552,128]{1,0:T(8,128)(2,1)S(1)}, u32[]{:S(2)}, u32[]{:S(2)}) %collective-permute-start.8) | collective-permute-done | bytes 397344 | tf_op jit(solution)/shard_map/ppermute | solution.py:40
  24.9 2.6 %collective-permute-start.10 = (bf16[6208,128]{1,0:T(8,128)(2,1)S(1)}, bf16[6208,128]{1,0:T(8,128)(2,1)S(1)}, u32[]{:S(2)}, u32[]{:S(2)}) collective-permute-start(bf16[6208,128]{1,0:T(8,128)(2,1)S(1)} %pad_maximum_fusion.refs_1_), channel_id=1, source_target_pairs={{0,6},{1,7},{2,0},{3,1},{4,2},{5,3},{6,4},{7,5},{8,14},{9,15},{10,... | collective-permute-start | bytes 4767752 | tf_op jit(solution)/shard_map/ppermute | solution.py:40
  27.5 1.5 %collective-permute-start.11 = (s32[4,128]{1,0:T(4,128)S(1)}, s32[4,128]{1,0:T(4,128)S(1)}, u32[]{:S(2)}, u32[]{:S(2)}) collective-permute-start(s32[4,128]{1,0:T(4,128)S(1)} %fusion.8), channel_id=1, source_target_pairs={{0,4},{1,5},{2,6},{3,7},{4,0},{5,1},{6,2},{7,3},{8,12},{9,13},{10,... | collective-permute-start | bytes 6152 | tf_op jit(solution)/shard_map/ppermute | solution.py:40
  29.0 16.9 %all-gather = s32[8,1,128]{2,1,0:T(1,128)S(1)} all-gather(s32[1,1,128]{2,1,0:T(1,128)S(1)} %bitcast.37), channel_id=1, replica_groups=mesh['row'=4,'col'=8,'depth'=8] {'col'}, dimensions={0}, use_global_device_ids=true | all-gather | bytes 4608 | tf_op jit(solution)/shard_map/all_gather | solution.py:362
  47.0 1.5 %collective-permute-done.9.refs_2_ = bf16[6208,128]{1,0:T(8,128)(2,1)} collective-permute-done((bf16[6208,128]{1,0:T(8,128)(2,1)S(1)}, bf16[6208,128]{1,0:T(8,128)(2,1)}, u32[]{:S(2)}, u32[]{:S(2)}) %collective-permute-start.9) | collective-permute-done | bytes 1589280 | tf_op jit(solution)/shard_map/ppermute | solution.py:40
  49.3 2.8 %collective-permute-start.14 = (s32[16,128]{1,0:T(8,128)S(1)}, s32[16,128]{1,0:T(8,128)S(1)}, u32[]{:S(2)}, u32[]{:S(2)}) collective-permute-start(s32[16,128]{1,0:T(8,128)S(1)} %pad_add_fusion.plane_ref), channel_id=1, source_target_pairs={{0,64},{1,65},{2,66},{3,67},{4,68},{5,69},{6,70},{7,71},{8,72},{9,... | collective-permute-start | bytes 24584 | tf_op jit(solution)/shard_map/ppermute | solution.py:40
  52.1 2.1 %slice.40 = bf16[3104,128]{1,0:T(8,128)(2,1)} slice(bf16[6208,128]{1,0:T(8,128)(2,1)} %collective-permute-done.9.refs_2_), slice={[0:3104], [0:128]} | slice | bytes 1589248 | tf_op jit(solution)/shard_map/slice | solution.py:67
  56.3 1.5 %collective-permute-start.13 = (bf16[3104,128]{1,0:T(8,128)(2,1)}, bf16[3104,128]{1,0:T(8,128)(2,1)}, u32[]{:S(2)}, u32[]{:S(2)}) collective-permute-start(bf16[3104,128]{1,0:T(8,128)(2,1)} %slice.41), channel_id=1, source_target_pairs={{0,6},{1,7},{2,0},{3,1},{4,2},{5,3},{6,4},{7,5},{8,14},{9,15},{10,... | collective-permute-start | bytes 2383880 | tf_op jit(solution)/shard_map/ppermute | solution.py:40
  59.5 7.2 %shard_map.38 = (s32[865]{0:T(1024)}, s32[4,128]{1,0:T(4,128)}) custom-call(s32[4]{0:T(128)S(1)} %pad_add_fusion.1.here_ref, s32[8,128]{1,0:T(8,128)} %bitcast.35, s32[8,128]{1,0:T(8,128)} %copy-done.5, s32[16,128]{1,0:T(8,128)} %copy-done.4), custom_call_target="tpu_custom_call" | custom-call | tf_op jit(solution)/shard_map/pallas_call | solution.py:200
  66.7 1.8 %concatenate.38.plane_ref = s32[32,128]{1,0:T(8,128)} concatenate(s32[4,128]{1,0:T(4,128)S(1)} %fusion.8, s32[4,128]{1,0:T(4,128)S(1)} %get-tuple-element.104, s32[4,128]{1,0:T(4,128)S(1)} %get-tuple-element.103, s32[4,128]{1,0:T(4,128)S(1)} %collective-permute-done.11, s32[16,128]{1,0:T(8,128)S(1)} %collective-permute-done.14), dimensions={0} | concatenate | bytes 32768 | tf_op jit(solution)/shard_map/concatenate | solution.py:367
  68.5 4.9 %shard_map.37.jobs_ref = s32[865]{0:T(1024)} custom-call(s32[4]{0:T(128)S(1)} %pad_add_fusion.1.here_ref, s32[8,128]{1,0:T(8,128)} %bitcast.36, s32[32,128]{1,0:T(8,128)} %concatenate.38.plane_ref), custom_call_target="tpu_custom_call" | custom-call | tf_op jit(solution)/shard_map/pallas_call | solution.py:190
  74.2 2.1 %collective-permute-done.19.refs_9_ = bf16[3104,128]{1,0:T(8,128)(2,1)} collective-permute-done((bf16[3104,128]{1,0:T(8,128)(2,1)}, bf16[3104,128]{1,0:T(8,128)(2,1)}, u32[]{:S(2)}, u32[]{:S(2)}) %collective-permute-start.19) | collective-permute-done | bytes 794656 | tf_op jit(solution)/shard_map/ppermute | solution.py:40
  78.1 4.7 %shard_map.39.refs_2_ = bf16[2304,128]{1,0:T(8,128)(2,1)} custom-call(s32[1]{0:T(128)} %constant.52.clone.1.most_ref, s32[865]{0:T(1024)S(1)} %copy-done, bf16[12288,128]{1,0:T(8,128)(2,1)} %all-gather.3.cloned.1.call-done.refs_0_, bf16[6208,128]{1,0:T(8,128)(2,1)S(1)} %pad_maximum_fusion.refs_1_, bf16[6208,128]{1,0:T(8,128)(2,1)} %collective-permute-done.9.refs_2_, ...), custom_call_target="tpu_custom_call" | custom-call | tf_op jit(solution)/shard_map/pallas_call | solution.py:269
  83.0 2.5 %collective-permute-start.21 = (s32[1,128]{1,0:T(1,128)S(1)}, s32[1,128]{1,0:T(1,128)S(1)}, u32[]{:S(2)}, u32[]{:S(2)}) collective-permute-start(s32[1,128]{1,0:T(1,128)S(1)} %get-tuple-element.100), channel_id=1, source_target_pairs={{0,6},{1,7},{2,0},{3,1},{4,2},{5,3},{6,4},{7,5},{8,14},{9,15},{10,... | collective-permute-start | bytes 1544 | tf_op jit(solution)/shard_map/ppermute | solution.py:40
  85.8 2.7 %collective-permute-start.26 = (bf16[2304,128]{1,0:T(8,128)(2,1)}, bf16[2304,128]{1,0:T(8,128)(2,1)}, u32[]{:S(2)}, u32[]{:S(2)}) collective-permute-start(bf16[2304,128]{1,0:T(8,128)(2,1)} %shard_map.39.refs_2_), channel_id=1, source_target_pairs={{0,129},{1,0},{2,131},{3,2},{4,133},{5,4},{6,135},{7,6},{8,137},{9... | collective-permute-start | bytes 1769480 | tf_op jit(solution)/shard_map/ppermute | solution.py:40
  89.6 1.2 collective-permute-start.23
  91.9 1.7 %collective-permute-done.23 = s32[1,128]{1,0:T(1,128)S(1)} collective-permute-done((s32[1,128]{1,0:T(1,128)S(1)}, s32[1,128]{1,0:T(1,128)S(1)}, u32[]{:S(2)}, u32[]{:S(2)}) %collective-permute-start.23) | collective-permute-done | bytes 544 | tf_op jit(solution)/shard_map/ppermute | solution.py:40
  95.0 7.7 %collective-permute-done.25.refs_3_ = bf16[2304,128]{1,0:T(8,128)(2,1)} collective-permute-done((bf16[2304,128]{1,0:T(8,128)(2,1)}, bf16[2304,128]{1,0:T(8,128)(2,1)}, u32[]{:S(2)}, u32[]{:S(2)}) %collective-permute-start.25) | collective-permute-done | bytes 589856 | tf_op jit(solution)/shard_map/ppermute | solution.py:40
  102.7 24.5 %conditional.1 = (bf16[2816,128]{1,0:T(8,128)(2,1)}, bf16[2816,128]{1,0:T(8,128)(2,1)}, bf16[2816,128]{1,0:T(8,128)(2,1)}, bf16[9216,128]{1,0:T(8,128)(2,1)}, bf...) conditional(s32[]{:T(128)} %bitcast.18, (bf16[2304,128]{1,0:T(8,128)(2,1)}, bf16[2304,128]{1,0:T(8,128)(2,1)}, ...), branch_computations={%region_0.1_spmd, %region_1.2_spmd} | conditional | bytes 33030312 | solution.py:340
  102.7 3.5 %branch_1_fun.2 = (bf16[2816,128]{1,0:T(8,128)(2,1)}, bf16[2816,128]{1,0:T(8,128)(2,1)}, bf16[2816,128]{1,0:T(8,128)(2,1)}) custom-call(s32[4]{0:T(128)S(1)} %get-tuple-element.36.here_ref, s32[1,128]{1,0:T(1,128)S(1)} %get-tuple-element.37.refs_0_, s32[1,128]{1,0:T(1,128)S(1)} %get-tuple-element.38.refs_1_, s32[1,128]{1,0:T(1,128)S(1)} %get-tuple-element.39.refs_2_, ...), custom_call_target="tpu_custom_call" | custom-call | tf_op jit(solution)/shard_map/cond/branch_1_fun/pallas_call | solution.py:315
  106.3 2.8 %collective-permute-start.1 = (bf16[2816,128]{1,0:T(8,128)(2,1)}, bf16[2816,128]{1,0:T(8,128)(2,1)}, u32[]{:S(2)}, u32[]{:S(2)}) collective-permute-start(bf16[2816,128]{1,0:T(8,128)(2,1)} %get-tuple-element.45), channel_id=1, source_target_pairs={{0,6},{1,7},{2,0},{3,1},{4,2},{5,3},{6,4},{7,5},{8,14},{9,15},{10,... | collective-permute-start | bytes 2162696 | tf_op jit(solution)/shard_map/cond/branch_1_fun/ppermute | solution.py:40
  110.1 8.1 %collective-permute-done = bf16[2816,128]{1,0:T(8,128)(2,1)} collective-permute-done((bf16[2816,128]{1,0:T(8,128)(2,1)}, bf16[2816,128]{1,0:T(8,128)(2,1)}, u32[]{:S(2)}, u32[]{:S(2)}) %collective-permute-start) | collective-permute-done | bytes 720928 | tf_op jit(solution)/shard_map/cond/branch_1_fun/ppermute | solution.py:40
  118.2 7.1 %collective-permute-done.1 = bf16[2816,128]{1,0:T(8,128)(2,1)} collective-permute-done((bf16[2816,128]{1,0:T(8,128)(2,1)}, bf16[2816,128]{1,0:T(8,128)(2,1)}, u32[]{:S(2)}, u32[]{:S(2)}) %collective-permute-start.1) | collective-permute-done | bytes 720928 | tf_op jit(solution)/shard_map/cond/branch_1_fun/ppermute | solution.py:40
  125.3 1.8 %collective-permute-done.2 = bf16[2816,128]{1,0:T(8,128)(2,1)} collective-permute-done((bf16[2816,128]{1,0:T(8,128)(2,1)}, bf16[2816,128]{1,0:T(8,128)(2,1)}, u32[]{:S(2)}, u32[]{:S(2)}) %collective-permute-start.2) | collective-permute-done | bytes 720928 | tf_op jit(solution)/shard_map/cond/branch_1_fun/ppermute | solution.py:40
  127.2 6.4 %shard_map.40 = (bf16[2304,128]{1,0:T(8,128)(2,1)S(1)}, bf16[2304,128]{1,0:T(8,128)(2,1)S(1)}) custom-call(s32[1]{0:T(128)} %bitcast.17.most_ref, s32[865]{0:T(1024)S(1)} %copy-done.1, bf16[12288,128]{1,0:T(8,128)(2,1)} %all-gather.3.cloned.1.call-done.refs_0_, bf16[12288,128]{1,0:T(8,128)(2,1)S(1)} %collective-permute-done.24.refs_1_, ...), custom_call_target="tpu_custom_call" | custom-call | tf_op jit(solution)/shard_map/pallas_call | solution.py:269
  133.6 2.0 %collective-permute-start.28 = (bf16[2304,128]{1,0:T(8,128)(2,1)S(1)}, bf16[2304,128]{1,0:T(8,128)(2,1)S(1)}, u32[]{:S(2)}, u32[]{:S(2)}) collective-permute-start(bf16[2304,128]{1,0:T(8,128)(2,1)S(1)} %get-tuple-element.99), channel_id=1, source_target_pairs={{0,64},{1,65},{2,66},{3,67},{4,68},{5,69},{6,70},{7,71},{8,72},{9,... | collective-permute-start | bytes 1769480 | tf_op jit(solution)/shard_map/ppermute | solution.py:40
  135.5 1.6 %collective-permute-done.28 = bf16[2304,128]{1,0:T(8,128)(2,1)S(1)} collective-permute-done((bf16[2304,128]{1,0:T(8,128)(2,1)S(1)}, bf16[2304,128]{1,0:T(8,128)(2,1)S(1)}, u32[]{:S(2)}, u32[]{:S(2)}) %collective-permute-start.28) | collective-permute-done | bytes 589856 | tf_op jit(solution)/shard_map/ppermute | solution.py:40
  (75 shorter events, 17.6 us)
Async XLA Ops:
  6.5 67.6 %all-gather.3.cloned.1.call-start = ((), (), s32[]{:S(2)}) async-start(), calls=%async_computation | async-start | bytes 3538944 | tf_op jit(solution)/shard_map/all_gather | solution.py:355
  10.2 9.1 %collective-permute-start.6 = (bf16[1552,128]{1,0:T(8,128)(2,1)S(1)}, bf16[1552,128]{1,0:T(8,128)(2,1)S(1)}, u32[]{:S(2)}, u32[]{:S(2)}) collective-permute-start(bf16[1552,128]{1,0:T(8,128)(2,1)S(1)} %pad_maximum_fusion.1), channel_id=1, source_target_pairs={{0,1},{1,128},{2,3},{3,130},{4,5},{5,132},{6,7},{7,134},{8,9},{9,1... | collective-permute-start | bytes 1191944 | tf_op jit(solution)/shard_map/ppermute | solution.py:40
  12.4 10.5 %collective-permute-start.7 = (bf16[1552,128]{1,0:T(8,128)(2,1)S(1)}, bf16[1552,128]{1,0:T(8,128)(2,1)S(1)}, u32[]{:S(2)}, u32[]{:S(2)}) collective-permute-start(bf16[1552,128]{1,0:T(8,128)(2,1)S(1)} %pad_maximum_fusion.1), channel_id=1, source_target_pairs={{0,129},{1,0},{2,131},{3,2},{4,133},{5,4},{6,135},{7,6},{8,137},{9... | collective-permute-start | bytes 1191944 | tf_op jit(solution)/shard_map/ppermute | solution.py:40
  13.9 10.8 %collective-permute-start.8 = (bf16[1552,128]{1,0:T(8,128)(2,1)S(1)}, bf16[1552,128]{1,0:T(8,128)(2,1)S(1)}, u32[]{:S(2)}, u32[]{:S(2)}) collective-permute-start(bf16[1552,128]{1,0:T(8,128)(2,1)S(1)} %pad_maximum_fusion.1), channel_id=1, source_target_pairs={{0,128},{1,129},{2,130},{3,131},{4,132},{5,133},{6,134},{7,135},{8... | collective-permute-start | bytes 1191944 | tf_op jit(solution)/shard_map/ppermute | solution.py:40
  24.9 22.1 %collective-permute-start.10 = (bf16[6208,128]{1,0:T(8,128)(2,1)S(1)}, bf16[6208,128]{1,0:T(8,128)(2,1)S(1)}, u32[]{:S(2)}, u32[]{:S(2)}) collective-permute-start(bf16[6208,128]{1,0:T(8,128)(2,1)S(1)} %pad_maximum_fusion.refs_1_), channel_id=1, source_target_pairs={{0,6},{1,7},{2,0},{3,1},{4,2},{5,3},{6,4},{7,5},{8,14},{9,15},{10,... | collective-permute-start | bytes 4767752 | tf_op jit(solution)/shard_map/ppermute | solution.py:40
  27.5 21.1 %collective-permute-start.9 = (bf16[6208,128]{1,0:T(8,128)(2,1)S(1)}, bf16[6208,128]{1,0:T(8,128)(2,1)}, u32[]{:S(2)}, u32[]{:S(2)}) collective-permute-start(bf16[6208,128]{1,0:T(8,128)(2,1)S(1)} %pad_maximum_fusion.refs_1_), channel_id=1, source_target_pairs={{0,2},{1,3},{2,4},{3,5},{4,6},{5,7},{6,0},{7,1},{8,10},{9,11},{10,... | collective-permute-start | bytes 4767752 | tf_op jit(solution)/shard_map/ppermute | solution.py:40
  27.5 19.5 %collective-permute-start.11 = (s32[4,128]{1,0:T(4,128)S(1)}, s32[4,128]{1,0:T(4,128)S(1)}, u32[]{:S(2)}, u32[]{:S(2)}) collective-permute-start(s32[4,128]{1,0:T(4,128)S(1)} %fusion.8), channel_id=1, source_target_pairs={{0,4},{1,5},{2,6},{3,7},{4,0},{5,1},{6,2},{7,3},{8,12},{9,13},{10,... | collective-permute-start | bytes 6152 | tf_op jit(solution)/shard_map/ppermute | solution.py:40
  45.9 13.6 %copy-start.3 = (s32[8,1,128]{2,1,0:T(1,128)}, s32[8,1,128]{2,1,0:T(1,128)S(1)}, u32[]{:S(2)}) copy-start(s32[8,1,128]{2,1,0:T(1,128)S(1)} %all-gather) | copy-start | bytes 12292
  49.3 10.2 %copy-start.4 = (s32[16,128]{1,0:T(8,128)}, s32[16,128]{1,0:T(8,128)S(1)}, u32[]{:S(2)}) copy-start(s32[16,128]{1,0:T(8,128)S(1)} %pad_add_fusion.plane_ref) | copy-start | bytes 24580
  49.3 9.7 %collective-permute-start.14 = (s32[16,128]{1,0:T(8,128)S(1)}, s32[16,128]{1,0:T(8,128)S(1)}, u32[]{:S(2)}, u32[]{:S(2)}) collective-permute-start(s32[16,128]{1,0:T(8,128)S(1)} %pad_add_fusion.plane_ref), channel_id=1, source_target_pairs={{0,64},{1,65},{2,66},{3,67},{4,68},{5,69},{6,70},{7,71},{8,72},{9,... | collective-permute-start | bytes 24584 | tf_op jit(solution)/shard_map/ppermute | solution.py:40
  52.0 6.8 %collective-permute-start.15 = (s32[8,128]{1,0:T(8,128)S(1)}, s32[8,128]{1,0:T(8,128)S(1)}, u32[]{:S(2)}, u32[]{:S(2)}) collective-permute-start(s32[8,128]{1,0:T(8,128)S(1)} %bitcast.34), channel_id=1, source_target_pairs={{0,64},{1,65},{2,66},{3,67},{4,68},{5,69},{6,70},{7,71},{8,72},{9,... | collective-permute-start | bytes 12296 | tf_op jit(solution)/shard_map/ppermute | solution.py:40
  55.2 18.2 %collective-permute-start.12 = (bf16[3104,128]{1,0:T(8,128)(2,1)}, bf16[3104,128]{1,0:T(8,128)(2,1)}, u32[]{:S(2)}, u32[]{:S(2)}) collective-permute-start(bf16[3104,128]{1,0:T(8,128)(2,1)} %slice.40), channel_id=1, source_target_pairs={{0,2},{1,3},{2,4},{3,5},{4,6},{5,7},{6,0},{7,1},{8,10},{9,11},{10,... | collective-permute-start | bytes 2383880 | tf_op jit(solution)/shard_map/ppermute | solution.py:40
  56.3 17.0 %collective-permute-start.13 = (bf16[3104,128]{1,0:T(8,128)(2,1)}, bf16[3104,128]{1,0:T(8,128)(2,1)}, u32[]{:S(2)}, u32[]{:S(2)}) collective-permute-start(bf16[3104,128]{1,0:T(8,128)(2,1)} %slice.41), channel_id=1, source_target_pairs={{0,6},{1,7},{2,0},{3,1},{4,2},{5,3},{6,4},{7,5},{8,14},{9,15},{10,... | collective-permute-start | bytes 2383880 | tf_op jit(solution)/shard_map/ppermute | solution.py:40
  57.9 16.3 %collective-permute-start.16 = (bf16[6208,128]{1,0:T(8,128)(2,1)S(1)}, bf16[6208,128]{1,0:T(8,128)(2,1)}, u32[]{:S(2)}, u32[]{:S(2)}) collective-permute-start(bf16[6208,128]{1,0:T(8,128)(2,1)S(1)} %pad_maximum_fusion.refs_1_), channel_id=1, source_target_pairs={{0,64},{1,65},{2,66},{3,67},{4,68},{5,69},{6,70},{7,71},{8,72},{9,... | collective-permute-start | bytes 4767752 | tf_op jit(solution)/shard_map/ppermute | solution.py:40
  58.9 18.6 %collective-permute-start.17 = (bf16[6208,128]{1,0:T(8,128)(2,1)}, bf16[6208,128]{1,0:T(8,128)(2,1)}, u32[]{:S(2)}, u32[]{:S(2)}) collective-permute-start(bf16[6208,128]{1,0:T(8,128)(2,1)} %collective-permute-done.9.refs_2_), channel_id=1, source_target_pairs={{0,64},{1,65},{2,66},{3,67},{4,68},{5,69},{6,70},{7,71},{8,72},{9,... | collective-permute-start | bytes 4767752 | tf_op jit(solution)/shard_map/ppermute | solution.py:40
  59.0 18.5 %collective-permute-start.18 = (bf16[6208,128]{1,0:T(8,128)(2,1)S(1)}, bf16[6208,128]{1,0:T(8,128)(2,1)}, u32[]{:S(2)}, u32[]{:S(2)}) collective-permute-start(bf16[6208,128]{1,0:T(8,128)(2,1)S(1)} %collective-permute-done.10.refs_3_), channel_id=1, source_target_pairs={{0,64},{1,65},{2,66},{3,67},{4,68},{5,69},{6,70},{7,71},{8,72},{9,... | collective-permute-start | bytes 4767752 | tf_op jit(solution)/shard_map/ppermute | solution.py:40
  68.5 14.5 %copy-start.6 = (s32[4,128]{1,0:T(4,128)S(1)}, s32[4,128]{1,0:T(4,128)}, u32[]{:S(2)}) copy-start(s32[4,128]{1,0:T(4,128)} %get-tuple-element.88) | copy-start | bytes 6148
  73.4 12.2 %copy-start.7 = (s32[6,2]{0,1:T(2,128)S(1)}, s32[6,2]{0,1:T(2,128)}, u32[]{:S(2)}) copy-start(s32[6,2]{0,1:T(2,128)} %param.6) | copy-start | bytes 148
  73.4 2.9 %collective-permute-start.19 = (bf16[3104,128]{1,0:T(8,128)(2,1)}, bf16[3104,128]{1,0:T(8,128)(2,1)}, u32[]{:S(2)}, u32[]{:S(2)}) collective-permute-start(bf16[3104,128]{1,0:T(8,128)(2,1)} %collective-permute-done.12.refs_4_), channel_id=1, source_target_pairs={{0,64},{1,65},{2,66},{3,67},{4,68},{5,69},{6,70},{7,71},{8,72},{9,... | collective-permute-start | bytes 2383880 | tf_op jit(solution)/shard_map/ppermute | solution.py:40
  74.0 3.4 %collective-permute-start.20 = (bf16[3104,128]{1,0:T(8,128)(2,1)}, bf16[3104,128]{1,0:T(8,128)(2,1)}, u32[]{:S(2)}, u32[]{:S(2)}) collective-permute-start(bf16[3104,128]{1,0:T(8,128)(2,1)} %collective-permute-done.13.refs_5_), channel_id=1, source_target_pairs={{0,64},{1,65},{2,66},{3,67},{4,68},{5,69},{6,70},{7,71},{8,72},{9,... | collective-permute-start | bytes 2383880 | tf_op jit(solution)/shard_map/ppermute | solution.py:40
  82.8 44.4 %collective-permute-start.24 = (bf16[12288,128]{1,0:T(8,128)(2,1)}, bf16[12288,128]{1,0:T(8,128)(2,1)S(1)}, u32[]{:S(2)}, u32[]{:S(2)}) collective-permute-start(bf16[12288,128]{1,0:T(8,128)(2,1)} %all-gather.3.cloned.1.call-done.refs_0_), channel_id=1, source_target_pairs={{0,64},{1,65},{2,66},{3,67},{4,68},{5,69},{6,70},{7,71},{8,72},{9,... | collective-permute-start | bytes 9437192 | tf_op jit(solution)/shard_map/ppermute | solution.py:40
  83.0 5.4 %collective-permute-start.21 = (s32[1,128]{1,0:T(1,128)S(1)}, s32[1,128]{1,0:T(1,128)S(1)}, u32[]{:S(2)}, u32[]{:S(2)}) collective-permute-start(s32[1,128]{1,0:T(1,128)S(1)} %get-tuple-element.100), channel_id=1, source_target_pairs={{0,6},{1,7},{2,0},{3,1},{4,2},{5,3},{6,4},{7,5},{8,14},{9,15},{10,... | collective-permute-start | bytes 1544 | tf_op jit(solution)/shard_map/ppermute | solution.py:40
  85.7 3.9 %collective-permute-start.22 = (s32[1,128]{1,0:T(1,128)S(1)}, s32[1,128]{1,0:T(1,128)S(1)}, u32[]{:S(2)}, u32[]{:S(2)}) collective-permute-start(s32[1,128]{1,0:T(1,128)S(1)} %get-tuple-element.102), channel_id=1, source_target_pairs={{0,2},{1,3},{2,4},{3,5},{4,6},{5,7},{6,0},{7,1},{8,10},{9,11},{10,... | collective-permute-start | bytes 1544 | tf_op jit(solution)/shard_map/ppermute | solution.py:40
  85.7 17.0 %collective-permute-start.25 = (bf16[2304,128]{1,0:T(8,128)(2,1)}, bf16[2304,128]{1,0:T(8,128)(2,1)}, u32[]{:S(2)}, u32[]{:S(2)}) collective-permute-start(bf16[2304,128]{1,0:T(8,128)(2,1)} %shard_map.39.refs_2_), channel_id=1, source_target_pairs={{0,1},{1,128},{2,3},{3,130},{4,5},{5,132},{6,7},{7,134},{8,9},{9,1... | collective-permute-start | bytes 1769480 | tf_op jit(solution)/shard_map/ppermute | solution.py:40
  85.8 16.9 %collective-permute-start.26 = (bf16[2304,128]{1,0:T(8,128)(2,1)}, bf16[2304,128]{1,0:T(8,128)(2,1)}, u32[]{:S(2)}, u32[]{:S(2)}) collective-permute-start(bf16[2304,128]{1,0:T(8,128)(2,1)} %shard_map.39.refs_2_), channel_id=1, source_target_pairs={{0,129},{1,0},{2,131},{3,2},{4,133},{5,4},{6,135},{7,6},{8,137},{9... | collective-permute-start | bytes 1769480 | tf_op jit(solution)/shard_map/ppermute | solution.py:40
  88.4 14.2 %collective-permute-start.27 = (bf16[2304,128]{1,0:T(8,128)(2,1)}, bf16[2304,128]{1,0:T(8,128)(2,1)}, u32[]{:S(2)}, u32[]{:S(2)}) collective-permute-start(bf16[2304,128]{1,0:T(8,128)(2,1)} %shard_map.39.refs_2_), channel_id=1, source_target_pairs={{0,128},{1,129},{2,130},{3,131},{4,132},{5,133},{6,134},{7,135},{8... | collective-permute-start | bytes 1769480 | tf_op jit(solution)/shard_map/ppermute | solution.py:40
  89.6 4.0 %collective-permute-start.23 = (s32[1,128]{1,0:T(1,128)S(1)}, s32[1,128]{1,0:T(1,128)S(1)}, u32[]{:S(2)}, u32[]{:S(2)}) collective-permute-start(s32[1,128]{1,0:T(1,128)S(1)} %get-tuple-element.101), channel_id=1, source_target_pairs={{0,4},{1,5},{2,6},{3,7},{4,0},{5,1},{6,2},{7,3},{8,12},{9,13},{10,... | collective-permute-start | bytes 1544 | tf_op jit(solution)/shard_map/ppermute | solution.py:40
  102.7 24.5 %copy-start.1 = (s32[865]{0:T(1024)S(1)}, s32[865]{0:T(1024)}, u32[]{:S(2)}) copy-start(s32[865]{0:T(1024)} %get-tuple-element.89.jobs_ref) | copy-start | bytes 10384
  106.2 12.0 %collective-permute-start = (bf16[2816,128]{1,0:T(8,128)(2,1)}, bf16[2816,128]{1,0:T(8,128)(2,1)}, u32[]{:S(2)}, u32[]{:S(2)}) collective-permute-start(bf16[2816,128]{1,0:T(8,128)(2,1)} %get-tuple-element.44), channel_id=1, source_target_pairs={{0,2},{1,3},{2,4},{3,5},{4,6},{5,7},{6,0},{7,1},{8,10},{9,11},{10,... | collective-permute-start | bytes 2162696 | tf_op jit(solution)/shard_map/cond/branch_1_fun/ppermute | solution.py:40
  106.3 19.0 %collective-permute-start.1 = (bf16[2816,128]{1,0:T(8,128)(2,1)}, bf16[2816,128]{1,0:T(8,128)(2,1)}, u32[]{:S(2)}, u32[]{:S(2)}) collective-permute-start(bf16[2816,128]{1,0:T(8,128)(2,1)} %get-tuple-element.45), channel_id=1, source_target_pairs={{0,6},{1,7},{2,0},{3,1},{4,2},{5,3},{6,4},{7,5},{8,14},{9,15},{10,... | collective-permute-start | bytes 2162696 | tf_op jit(solution)/shard_map/cond/branch_1_fun/ppermute | solution.py:40
  109.1 18.1 %collective-permute-start.2 = (bf16[2816,128]{1,0:T(8,128)(2,1)}, bf16[2816,128]{1,0:T(8,128)(2,1)}, u32[]{:S(2)}, u32[]{:S(2)}) collective-permute-start(bf16[2816,128]{1,0:T(8,128)(2,1)} %get-tuple-element.46), channel_id=1, source_target_pairs={{0,4},{1,5},{2,6},{3,7},{4,0},{5,1},{6,2},{7,3},{8,12},{9,13},{10,... | collective-permute-start | bytes 2162696 | tf_op jit(solution)/shard_map/cond/branch_1_fun/ppermute | solution.py:40
  133.6 3.6 %collective-permute-start.28 = (bf16[2304,128]{1,0:T(8,128)(2,1)S(1)}, bf16[2304,128]{1,0:T(8,128)(2,1)S(1)}, u32[]{:S(2)}, u32[]{:S(2)}) collective-permute-start(bf16[2304,128]{1,0:T(8,128)(2,1)S(1)} %get-tuple-element.99), channel_id=1, source_target_pairs={{0,64},{1,65},{2,66},{3,67},{4,68},{5,69},{6,70},{7,71},{8,72},{9,... | collective-permute-start | bytes 1769480 | tf_op jit(solution)/shard_map/ppermute | solution.py:40
  (3 other events, 11.3 us)
Sparse Core Ops, SparseCore 0:
  9.1 48.5 all-gather.2

commit v4 on v3

--- a/solution.py
+++ b/solution.py
@@ -62,11 +62,6 @@
     return piece, plus, minus, far
 
 
-def far_pieces(plus, minus):
-    half = plus.shape[0] // 2
-    return second_ring(plus[:half], 1), second_ring(minus[half:], -1)
-
-
 def block_copy(ref, unit, target, sem):
     offset = pl.multiple_of(unit * UNIT, UNIT)
     return pltpu.make_async_copy(ref.at[pl.ds(offset, BLK)], target, sem)
@@ -78,66 +73,57 @@
     for group in range(16):
         at_x, at_y = group // 8 * 2 + group % 2, group // 4 % 2 * 2 + group // 2 % 2
         far = jnp.where(core == 0, at_x, at_y)
-        group_code[0, which * 16 + group] = ring_order(first - far)
-        group_code[1, which * 16 + group] = ring_order(second - jnp.where(core == 0, at_y, at_x))
+        inner = ring_order(first - far)
+        outer = ring_order(second - jnp.where(core == 0, at_y, at_x))
+        group_code[0, which * 16 + group] = inner
+        group_code[1, which * 16 + group] = outer
         group_code[2, which * 16 + group] = far
+        group_code[3, which * 16 + group] = outer * 4 + inner
 
 
 def plan_scan(marks_ref, z, panels, plane_ref, group_code, slots, add):
+    def look(row, panel, base, side, wanted):
+        column = marks_ref[panel, row * KA + side]
+        known = jnp.maximum(column, 0)
+        quarter = (known * 43) >> 8
+        place = known - quarter * ROWS
+        group = base + quarter
+        table = group_code[3, group]
+        founds = []
+        for slot in range(slots):
+            start = place * KA + (group & 16) * 4 if slots == KA else LEFT + place * KC
+            have = plane_ref[table, start + slot]
+            found = jnp.where(have == wanted[0], 0, jnp.where(have == wanted[1], 1, 2))
+            founds.append(jnp.where((found < 2) | (have == wanted[2]), found, -1))
+        best = jnp.where(column >= 0, functools.reduce(jnp.maximum, founds), -1)
+        return best, founds, group, place
+
     def scan_row(row, carry):
         wanted = [marks_ref[z, LEFT + row * KC + u] for u in range(KC)]
-        for panel, base in panels:
-            for side in range(KA):
-                column = marks_ref[panel, row * KA + side]
-
-                @pl.when(column >= 0)
-                def _(panel=panel, base=base, side=side, column=column):
-                    quarter = (column * 43) >> 8
-                    place = column - quarter * ROWS
-                    group = base + quarter
+        entries = [(panel, base, side) for panel, base in panels for side in range(KA)]
+        for first in range(0, len(entries), 4):
+            some = entries[first : first + 4]
+            for (panel, _, side), (best, founds, group, place) in zip(some, [look(row, *entry, wanted) for entry in some]):
+
+                @pl.when(best >= 0)
+                def _(panel=panel, side=side, founds=founds, group=group, place=place):
+                    left = (panel * LEFT + row * KA + side) * (BLK // UNIT)
                     inner, outer = group_code[0, group], group_code[1, group]
-                    table = (group & 16) + outer * 4 + inner
-                    founds = []
-                    for slot in range(slots):
-                        start = place * KA if slots == KA else LEFT + place * KC
-                        have = plane_ref[table, start + slot]
-                        found = jnp.where(have == wanted[0], 0, jnp.where(have == wanted[1], 1, 2))
-                        founds.append(jnp.where((found < 2) | (have == wanted[2]), found, -1))
-
-                    @pl.when(functools.reduce(jnp.maximum, founds) >= 0)
-                    def _():
-                        left = (panel * LEFT + row * KA + side) * (BLK // UNIT)
-                        for slot, found in enumerate(founds):
-                            out = row * KC + found
-                            pl.when(found >= 0)(functools.partial(add, group, inner, outer, place, slot, left, out))
+                    for slot, found in enumerate(founds):
+                        out = row * KC + found
+                        pl.when(found >= 0)(functools.partial(add, group, inner, outer, place, slot, left, out))
 
         return carry
 
     lax.fori_loop(0, ROWS, scan_row, 0)
 
 
-def plan_x_kernel(here_ref, own_ref, plane_ref, jobs, group_code):
+def plan_kernel(here_ref, own_ref, other_ref, plane_ref, x_jobs, s_jobs, takes, seen, group_code):
     core, z = here_ref[0], here_ref[3]
     plan_groups(here_ref, 0, group_code)
     plan_groups(here_ref, 1, group_code)
-    jobs[0] = 0
-
-    def add(group, inner, outer, place, slot, left, out):
-        count = jobs[0]
-        jobs[0] = count + 1
-        jobs[1 + count] = (left << 6) | out
-        source = jnp.where(outer < 3, outer, 3 + (inner >> 1)) + jnp.where(group >= 16, 5, 0)
-        ahead = jnp.where(outer < 3, inner, inner & 1) * (PAY // UNIT)
-        jobs[1 + JOBS + count] = (source << 10) | (ahead + (place * KA + slot) * (BLK // UNIT))
-
-    panels = [(panel, ((panel // 2 % 2) ^ core) * 16 + (panel // 4 * 2 + panel % 2) * 4) for panel in range(8)]
-    plan_scan(own_ref, z, panels, plane_ref, group_code, KA, add)
-
-
-def plan_s_kernel(here_ref, own_ref, other_ref, plane_ref, jobs, takes, seen, group_code):
-    core, z = here_ref[0], here_ref[3]
-    plan_groups(here_ref, 0, group_code)
-    jobs[0] = 0
+    x_jobs[0] = 0
+    s_jobs[0] = 0
     for outer in range(4):
         takes[outer, COUNT] = 0
 
@@ -147,7 +133,15 @@
 
     lax.fori_loop(0, 16 * OUTS, clear, 0, unroll=16)
 
-    def add(half, group, inner, outer, place, slot, left, out):
+    def add_x(group, inner, outer, place, slot, left, out):
+        count = x_jobs[0]
+        x_jobs[0] = count + 1
+        x_jobs[1 + count] = (left << 6) | out
+        source = jnp.where(outer < 3, outer, 3 + (inner >> 1)) + jnp.where(group >= 16, 5, 0)
+        ahead = jnp.where(outer < 3, inner, inner & 1) * (PAY // UNIT)
+        x_jobs[1 + JOBS + count] = (source << 10) | (ahead + (place * KA + slot) * (BLK // UNIT))
+
+    def add_s(half, group, inner, outer, place, slot, left, out):
         block = place * KC + slot
         mark = group * OUTS + block
 
@@ -161,18 +155,20 @@
             def _():
                 takes[outer, rank] = (group_code[2, group] << 5) | block
 
-        count = jobs[0]
-        jobs[0] = count + 1
-        jobs[1 + count] = ((half * 8 * LEFT * (BLK // UNIT) + left) << 6) | (half * OUTS + out)
+        count = s_jobs[0]
+        s_jobs[0] = count + 1
+        s_jobs[1 + count] = ((half * 8 * LEFT * (BLK // UNIT) + left) << 6) | (half * OUTS + out)
         near = (inner << 10) | (block * (BLK // UNIT))
         packed = ((3 + outer) << 10) | ((seen[mark] & 31) * (BLK // UNIT))
         dense = ((6 + outer) << 10) | ((inner * OUTS + block) * (BLK // UNIT))
-        jobs[1 + JOBS + count] = jnp.where(outer == 0, near, packed)
-        jobs[1 + 2 * JOBS + count] = jnp.where(outer == 0, near, dense)
-
+        s_jobs[1 + JOBS + count] = jnp.where(outer == 0, near, packed)
+        s_jobs[1 + 2 * JOBS + count] = jnp.where(outer == 0, near, dense)
+
+    panels = [(panel, ((panel // 2 % 2) ^ core) * 16 + (panel // 4 * 2 + panel % 2) * 4) for panel in range(8)]
+    plan_scan(own_ref, z, panels, plane_ref, group_code, KA, add_x)
     panels = [(panel // 2 * 4 + 2 * core + panel % 2, panel * 4) for panel in range(4)]
     for half, marks_ref in enumerate((own_ref, other_ref)):
-        plan_scan(marks_ref, z, panels, plane_ref, group_code, KC, functools.partial(add, half))
+        plan_scan(marks_ref, z, panels, plane_ref, group_code, KC, functools.partial(add_s, half))
     most = jnp.maximum(takes[1, COUNT], jnp.maximum(takes[2, COUNT], takes[3, COUNT]))
     for outer in range(4):
         takes[outer, MOST] = most
@@ -183,26 +179,18 @@
 ANY = pl.BlockSpec(memory_space=pl.ANY)
 
 
+SMALL = pl.CostEstimate(flops=1000, bytes_accessed=1000, transcendentals=0)
 JOB_TABLE = jax.ShapeDtypeStruct((1 + 3 * JOBS,), jnp.int32)
 
 
-def plan_x(here, own, plane):
+def plan(here, own, other, plane):
     return pl.pallas_call(
-        plan_x_kernel,
-        out_shape=JOB_TABLE,
-        in_specs=[SMEM] * 3,
-        out_specs=SMEM,
-        scratch_shapes=[pltpu.SMEM((3, 32), jnp.int32)],
-    )(here, own, plane)
-
-
-def plan_s(here, own, other, plane):
-    return pl.pallas_call(
-        plan_s_kernel,
-        out_shape=(JOB_TABLE, jax.ShapeDtypeStruct((4, BLK), jnp.int32)),
+        plan_kernel,
+        out_shape=(JOB_TABLE, JOB_TABLE, jax.ShapeDtypeStruct((4, BLK), jnp.int32)),
         in_specs=[SMEM] * 4,
-        out_specs=(SMEM, SMEM),
-        scratch_shapes=[pltpu.SMEM((16 * OUTS,), jnp.int32), pltpu.SMEM((3, 16), jnp.int32)],
+        out_specs=(SMEM,) * 3,
+        scratch_shapes=[pltpu.SMEM((16 * OUTS,), jnp.int32), pltpu.SMEM((4, 32), jnp.int32)],
+        cost_estimate=SMALL,
     )(here, own, other, plane)
 
 
@@ -277,7 +265,7 @@
             pltpu.VMEM((SLOTS, BLK, BLK), jnp.bfloat16),
             pltpu.SemaphoreType.DMA((2, SLOTS)),
         ],
-        compiler_params=pltpu.CompilerParams(vmem_limit_bytes=24 * 1024 * 1024),
+        compiler_params=pltpu.CompilerParams(vmem_limit_bytes=10 * 1024 * 1024),
     )(most, jobs, *lefts, *rights)
 
 
@@ -361,16 +349,15 @@
     plus, minus, far_marks = second_ring(near, 1), second_ring(near, -1), second_ring(near_marks, 2)
     row_marks = lax.all_gather(marks, "col", axis=0, tiled=True)
     plus, minus, far_marks, row_marks = lax.optimization_barrier((plus, minus, far_marks, row_marks))
-    other_marks = swap(row_marks)
-    far = far_pieces(plus, minus)
+    half = plus.shape[0] // 2
+    far = second_ring(plus[:half], 1), second_ring(minus[half:], -1)
     plane_marks = jnp.concatenate([near_marks, marks_of(plus), marks_of(minus), far_marks], axis=0)
-    both_marks = jnp.concatenate([plane_marks, swap(plane_marks)], axis=0)
-    x_jobs = plan_x(here, row_marks, both_marks)
-    s_jobs, takes = plan_s(here, row_marks, other_marks, plane_marks)
-    far, x_jobs, s_jobs = lax.optimization_barrier((far, x_jobs, s_jobs))
+    beside = jnp.pad(swap(plane_marks)[:, : BLK // 2], ((0, 0), (BLK // 2, 0)))
+    x_jobs, s_jobs, takes = plan(here, row_marks, swap(row_marks), plane_marks + beside)
+    far, x_jobs = lax.optimization_barrier((far, x_jobs))
     right = (near, plus, minus) + far
     other_right = tuple(swap(part) for part in right)
-    left, plus = lax.optimization_barrier((left, plus))
+    left, x_jobs = lax.optimization_barrier((left, x_jobs))
 
     zero = jnp.zeros((1,), jnp.int32)
     (square,) = product(zero, x_jobs, (left,), right + other_right)

time: 147 us -> 143 us (0.973)
  local copies, waits for them, and re-layouts: 7.48 us -> 5.58 us
    concatenate x1 -> x0, local copies, waits for them, and re-layouts: 1.81 us -> none  [local(): both_marks = jnp.concatenate([plane_marks, swap(plane_marks)], axis=0)]
    pallas_call x2 -> x1, Pallas kernels: 12.1 us -> 10.4 us  [plan(): pl.pallas_call(plan_kernel, out_shape=(JOB_TABLE, JOB_TABLE, jax.ShapeDty...]
  transfers between devices with their start and end apart: 27 -> 27, of which waited for: 13 -> 13; matrix products, arithmetic and copies ran while one was open for 8% -> 7% of each run, Pallas kernels for 11% -> 10%
where the time goes in v4:
time: 143 us; the launch traced here: 142 us
  waiting for transfers between devices  44.2 us (31%)
  starting transfers between devices  28.5 us (20%)
  Pallas kernels  25.7 us (18%)
  blocking collectives  16.9 us (12%)
  between operations  14.1 us (10%)
  other arithmetic  6.69 us (5%)
  local copies, waits for them, and re-layouts  5.58 us (4%)
    ppermute x26, waiting for transfers between devices, move(): return lax.ppermute(array, ALL, pairs)  43.5 us
    ppermute x26, starting transfers between devices, move(): return lax.ppermute(array, ALL, pairs)  28.5 us
    all_gather x1, blocking collectives, local(): row_marks = lax.all_gather(marks, 'col', axis=0, tiled=True)  16.9 us
    pallas_call x2, Pallas kernels, product(): pl.pallas_call(functools.partial(product_kernel, len(lefts), len(rights))...  11.6 us
    pallas_call x1, Pallas kernels, plan(): pl.pallas_call(plan_kernel, out_shape=(JOB_TABLE, JOB_TABLE, jax.ShapeDty...  10.4 us
    pallas_call x1, Pallas kernels, pack(): pl.pallas_call(pack_kernel, out_shape=(shape,) * 3, in_specs=[SMEM] * 4 +...  3.68 us
    slice x2, local copies, waits for them, and re-layouts, local(): far = (second_ring(plus[:half], 1), second_ring(minus[half:], -1))  3.11 us
  transfers between devices with their start and end apart: 27, of which 13 were waited for; matrix products, arithmetic and copies ran while one was open for 7% of the time, Pallas kernels for 10%

profile of v4, /device:TPU:1, one launch (start us, length us, event | category | flops | bytes accessed | tf_op | source)
XLA Modules:
  0.0 141.7 jit_solution(14243605129091088559)
XLA Ops:
  10.2 2.2 %collective-permute-start.6 = (bf16[1552,128]{1,0:T(8,128)(2,1)S(1)}, bf16[1552,128]{1,0:T(8,128)(2,1)S(1)}, u32[]{:S(2)}, u32[]{:S(2)}) collective-permute-start(bf16[1552,128]{1,0:T(8,128)(2,1)S(1)} %pad_maximum_fusion.1), channel_id=1, source_target_pairs={{0,1},{1,128},{2,3},{3,130},{4,5},{5,132},{6,7},{7,134},{8,9},{9,1... | collective-permute-start | bytes 1191944 | tf_op jit(solution)/shard_map/ppermute | solution.py:40
  12.4 1.5 %collective-permute-start.7 = (bf16[1552,128]{1,0:T(8,128)(2,1)S(1)}, bf16[1552,128]{1,0:T(8,128)(2,1)S(1)}, u32[]{:S(2)}, u32[]{:S(2)}) collective-permute-start(bf16[1552,128]{1,0:T(8,128)(2,1)S(1)} %pad_maximum_fusion.1), channel_id=1, source_target_pairs={{0,129},{1,0},{2,131},{3,2},{4,133},{5,4},{6,135},{7,6},{8,137},{9... | collective-permute-start | bytes 1191944 | tf_op jit(solution)/shard_map/ppermute | solution.py:40
  13.9 1.6 %collective-permute-start.8 = (bf16[1552,128]{1,0:T(8,128)(2,1)S(1)}, bf16[1552,128]{1,0:T(8,128)(2,1)S(1)}, u32[]{:S(2)}, u32[]{:S(2)}) collective-permute-start(bf16[1552,128]{1,0:T(8,128)(2,1)S(1)} %pad_maximum_fusion.1), channel_id=1, source_target_pairs={{0,128},{1,129},{2,130},{3,131},{4,132},{5,133},{6,134},{7,135},{8... | collective-permute-start | bytes 1191944 | tf_op jit(solution)/shard_map/ppermute | solution.py:40
  15.5 3.9 %collective-permute-done.6 = bf16[1552,128]{1,0:T(8,128)(2,1)S(1)} collective-permute-done((bf16[1552,128]{1,0:T(8,128)(2,1)S(1)}, bf16[1552,128]{1,0:T(8,128)(2,1)S(1)}, u32[]{:S(2)}, u32[]{:S(2)}) %collective-permute-start.6) | collective-permute-done | bytes 397344 | tf_op jit(solution)/shard_map/ppermute | solution.py:40
  19.4 3.6 %collective-permute-done.7 = bf16[1552,128]{1,0:T(8,128)(2,1)S(1)} collective-permute-done((bf16[1552,128]{1,0:T(8,128)(2,1)S(1)}, bf16[1552,128]{1,0:T(8,128)(2,1)S(1)}, u32[]{:S(2)}, u32[]{:S(2)}) %collective-permute-start.7) | collective-permute-done | bytes 397344 | tf_op jit(solution)/shard_map/ppermute | solution.py:40
  23.0 1.8 %collective-permute-done.8 = bf16[1552,128]{1,0:T(8,128)(2,1)S(1)} collective-permute-done((bf16[1552,128]{1,0:T(8,128)(2,1)S(1)}, bf16[1552,128]{1,0:T(8,128)(2,1)S(1)}, u32[]{:S(2)}, u32[]{:S(2)}) %collective-permute-start.8) | collective-permute-done | bytes 397344 | tf_op jit(solution)/shard_map/ppermute | solution.py:40
  24.9 2.6 %collective-permute-start.10 = (bf16[6208,128]{1,0:T(8,128)(2,1)S(1)}, bf16[6208,128]{1,0:T(8,128)(2,1)S(1)}, u32[]{:S(2)}, u32[]{:S(2)}) collective-permute-start(bf16[6208,128]{1,0:T(8,128)(2,1)S(1)} %pad_maximum_fusion.refs_1_), channel_id=1, source_target_pairs={{0,6},{1,7},{2,0},{3,1},{4,2},{5,3},{6,4},{7,5},{8,14},{9,15},{10,... | collective-permute-start | bytes 4767752 | tf_op jit(solution)/shard_map/ppermute | solution.py:40
  27.5 1.5 %collective-permute-start.11 = (s32[4,128]{1,0:T(4,128)S(1)}, s32[4,128]{1,0:T(4,128)S(1)}, u32[]{:S(2)}, u32[]{:S(2)}) collective-permute-start(s32[4,128]{1,0:T(4,128)S(1)} %fusion.8), channel_id=1, source_target_pairs={{0,4},{1,5},{2,6},{3,7},{4,0},{5,1},{6,2},{7,3},{8,12},{9,13},{10,... | collective-permute-start | bytes 6152 | tf_op jit(solution)/shard_map/ppermute | solution.py:40
  29.0 16.9 %all-gather = s32[8,1,128]{2,1,0:T(1,128)S(1)} all-gather(s32[1,1,128]{2,1,0:T(1,128)S(1)} %bitcast.38), channel_id=1, replica_groups=mesh['row'=4,'col'=8,'depth'=8] {'col'}, dimensions={0}, use_global_device_ids=true | all-gather | bytes 4608 | tf_op jit(solution)/shard_map/all_gather | solution.py:350
  47.0 1.5 %collective-permute-done.9.refs_2_ = bf16[6208,128]{1,0:T(8,128)(2,1)} collective-permute-done((bf16[6208,128]{1,0:T(8,128)(2,1)S(1)}, bf16[6208,128]{1,0:T(8,128)(2,1)}, u32[]{:S(2)}, u32[]{:S(2)}) %collective-permute-start.9) | collective-permute-done | bytes 1589280 | tf_op jit(solution)/shard_map/ppermute | solution.py:40
  49.3 2.8 %collective-permute-start.15 = (s32[16,128]{1,0:T(8,128)S(1)}, s32[16,128]{1,0:T(8,128)S(1)}, u32[]{:S(2)}, u32[]{:S(2)}) collective-permute-start(s32[16,128]{1,0:T(8,128)S(1)} %pad_add_fusion), channel_id=1, source_target_pairs={{0,64},{1,65},{2,66},{3,67},{4,68},{5,69},{6,70},{7,71},{8,72},{9,... | collective-permute-start | bytes 24584 | tf_op jit(solution)/shard_map/ppermute | solution.py:40
  52.1 2.1 %slice.43 = bf16[3104,128]{1,0:T(8,128)(2,1)} slice(bf16[6208,128]{1,0:T(8,128)(2,1)} %collective-permute-done.9.refs_2_), slice={[0:3104], [0:128]} | slice | bytes 1589248 | tf_op jit(solution)/shard_map/slice | solution.py:353
  55.2 1.1 collective-permute-start.12
  56.4 1.5 %collective-permute-start.13 = (bf16[3104,128]{1,0:T(8,128)(2,1)}, bf16[3104,128]{1,0:T(8,128)(2,1)}, u32[]{:S(2)}, u32[]{:S(2)}) collective-permute-start(bf16[3104,128]{1,0:T(8,128)(2,1)} %slice.44), channel_id=1, source_target_pairs={{0,6},{1,7},{2,0},{3,1},{4,2},{5,3},{6,4},{7,5},{8,14},{9,15},{10,... | collective-permute-start | bytes 2383880 | tf_op jit(solution)/shard_map/ppermute | solution.py:40
  60.2 10.4 %shard_map.37 = (s32[865]{0:T(1024)}, s32[865]{0:T(1024)}, s32[4,128]{1,0:T(4,128)}) custom-call(s32[4]{0:T(128)S(1)} %pad_add_fusion.2.here_ref, s32[8,128]{1,0:T(8,128)} %bitcast.36, s32[8,128]{1,0:T(8,128)} %copy-done.4, s32[16,128]{1,0:T(8,128)} %pad_add_fusion.1.plane_ref), custom_call_target="tpu_custom_call" | custom-call | flops 1000 | bytes 1000 | tf_op jit(solution)/shard_map/pallas_call | solution.py:187
  71.4 2.1 %collective-permute-done.19.refs_9_ = bf16[3104,128]{1,0:T(8,128)(2,1)} collective-permute-done((bf16[3104,128]{1,0:T(8,128)(2,1)}, bf16[3104,128]{1,0:T(8,128)(2,1)}, u32[]{:S(2)}, u32[]{:S(2)}) %collective-permute-start.19) | collective-permute-done | bytes 794656 | tf_op jit(solution)/shard_map/ppermute | solution.py:40
  73.5 1.1 collective-permute-done.20.refs_10_
  75.4 4.7 %shard_map.38.refs_2_ = bf16[2304,128]{1,0:T(8,128)(2,1)} custom-call(s32[1]{0:T(128)} %constant.52.clone.1.most_ref, s32[865]{0:T(1024)S(1)} %copy-done.1, bf16[12288,128]{1,0:T(8,128)(2,1)} %all-gather.3.cloned.1.call-done.refs_0_, bf16[6208,128]{1,0:T(8,128)(2,1)S(1)} %pad_maximum_fusion.refs_1_, bf16[6208,128]{1,0:T(8,128)(2,1)} %collective-permute-done.9.refs_2_, ...), custom_call_target="tpu_custom_call" | custom-call | tf_op jit(solution)/shard_map/pallas_call | solution.py:257
  80.2 1.8 %collective-permute-start.21 = (s32[1,128]{1,0:T(1,128)S(1)}, s32[1,128]{1,0:T(1,128)S(1)}, u32[]{:S(2)}, u32[]{:S(2)}) collective-permute-start(s32[1,128]{1,0:T(1,128)S(1)} %get-tuple-element.102), channel_id=1, source_target_pairs={{0,6},{1,7},{2,0},{3,1},{4,2},{5,3},{6,4},{7,5},{8,14},{9,15},{10,... | collective-permute-start | bytes 1544 | tf_op jit(solution)/shard_map/ppermute | solution.py:40
  82.8 2.1 %collective-permute-start.26 = (bf16[2304,128]{1,0:T(8,128)(2,1)}, bf16[2304,128]{1,0:T(8,128)(2,1)}, u32[]{:S(2)}, u32[]{:S(2)}) collective-permute-start(bf16[2304,128]{1,0:T(8,128)(2,1)} %shard_map.38.refs_2_), channel_id=1, source_target_pairs={{0,129},{1,0},{2,131},{3,2},{4,133},{5,4},{6,135},{7,6},{8,137},{9... | collective-permute-start | bytes 1769480 | tf_op jit(solution)/shard_map/ppermute | solution.py:40
  86.0 1.2 collective-permute-start.23
  88.4 1.7 %collective-permute-done.23 = s32[1,128]{1,0:T(1,128)S(1)} collective-permute-done((s32[1,128]{1,0:T(1,128)S(1)}, s32[1,128]{1,0:T(1,128)S(1)}, u32[]{:S(2)}, u32[]{:S(2)}) %collective-permute-start.23) | collective-permute-done | bytes 544 | tf_op jit(solution)/shard_map/ppermute | solution.py:40
  91.2 7.9 %collective-permute-done.25.refs_3_ = bf16[2304,128]{1,0:T(8,128)(2,1)} collective-permute-done((bf16[2304,128]{1,0:T(8,128)(2,1)}, bf16[2304,128]{1,0:T(8,128)(2,1)}, u32[]{:S(2)}, u32[]{:S(2)}) %collective-permute-start.25) | collective-permute-done | bytes 589856 | tf_op jit(solution)/shard_map/ppermute | solution.py:40
  99.1 24.5 %conditional.1 = (bf16[2816,128]{1,0:T(8,128)(2,1)}, bf16[2816,128]{1,0:T(8,128)(2,1)}, bf16[2816,128]{1,0:T(8,128)(2,1)}, bf16[9216,128]{1,0:T(8,128)(2,1)}, bf...) conditional(s32[]{:T(128)} %bitcast.16, (bf16[2304,128]{1,0:T(8,128)(2,1)}, bf16[2304,128]{1,0:T(8,128)(2,1)}, ...), branch_computations={%region_0.1_spmd, %region_1.2_spmd} | conditional | bytes 33030312 | solution.py:328
  99.2 3.7 %branch_1_fun.2 = (bf16[2816,128]{1,0:T(8,128)(2,1)}, bf16[2816,128]{1,0:T(8,128)(2,1)}, bf16[2816,128]{1,0:T(8,128)(2,1)}) custom-call(s32[4]{0:T(128)S(1)} %get-tuple-element.36.here_ref, s32[1,128]{1,0:T(1,128)S(1)} %get-tuple-element.37.refs_0_, s32[1,128]{1,0:T(1,128)S(1)} %get-tuple-element.38.refs_1_, s32[1,128]{1,0:T(1,128)S(1)} %get-tuple-element.39.refs_2_, ...), custom_call_target="tpu_custom_call" | custom-call | tf_op jit(solution)/shard_map/cond/branch_1_fun/pallas_call | solution.py:303
  102.9 2.7 %collective-permute-start.1 = (bf16[2816,128]{1,0:T(8,128)(2,1)}, bf16[2816,128]{1,0:T(8,128)(2,1)}, u32[]{:S(2)}, u32[]{:S(2)}) collective-permute-start(bf16[2816,128]{1,0:T(8,128)(2,1)} %get-tuple-element.45), channel_id=1, source_target_pairs={{0,6},{1,7},{2,0},{3,1},{4,2},{5,3},{6,4},{7,5},{8,14},{9,15},{10,... | collective-permute-start | bytes 2162696 | tf_op jit(solution)/shard_map/cond/branch_1_fun/ppermute | solution.py:40
  106.7 8.2 %collective-permute-done = bf16[2816,128]{1,0:T(8,128)(2,1)} collective-permute-done((bf16[2816,128]{1,0:T(8,128)(2,1)}, bf16[2816,128]{1,0:T(8,128)(2,1)}, u32[]{:S(2)}, u32[]{:S(2)}) %collective-permute-start) | collective-permute-done | bytes 720928 | tf_op jit(solution)/shard_map/cond/branch_1_fun/ppermute | solution.py:40
  114.9 7.0 %collective-permute-done.1 = bf16[2816,128]{1,0:T(8,128)(2,1)} collective-permute-done((bf16[2816,128]{1,0:T(8,128)(2,1)}, bf16[2816,128]{1,0:T(8,128)(2,1)}, u32[]{:S(2)}, u32[]{:S(2)}) %collective-permute-start.1) | collective-permute-done | bytes 720928 | tf_op jit(solution)/shard_map/cond/branch_1_fun/ppermute | solution.py:40
  121.9 1.8 %collective-permute-done.2 = bf16[2816,128]{1,0:T(8,128)(2,1)} collective-permute-done((bf16[2816,128]{1,0:T(8,128)(2,1)}, bf16[2816,128]{1,0:T(8,128)(2,1)}, u32[]{:S(2)}, u32[]{:S(2)}) %collective-permute-start.2) | collective-permute-done | bytes 720928 | tf_op jit(solution)/shard_map/cond/branch_1_fun/ppermute | solution.py:40
  123.7 6.8 %shard_map.39 = (bf16[2304,128]{1,0:T(8,128)(2,1)S(1)}, bf16[2304,128]{1,0:T(8,128)(2,1)S(1)}) custom-call(s32[1]{0:T(128)} %bitcast.15.most_ref, s32[865]{0:T(1024)S(1)} %copy-done, bf16[12288,128]{1,0:T(8,128)(2,1)} %all-gather.3.cloned.1.call-done.refs_0_, bf16[12288,128]{1,0:T(8,128)(2,1)S(1)} %collective-permute-done.24.refs_1_, ...), custom_call_target="tpu_custom_call" | custom-call | tf_op jit(solution)/shard_map/pallas_call | solution.py:257
  130.5 1.6 %collective-permute-start.28 = (bf16[2304,128]{1,0:T(8,128)(2,1)S(1)}, bf16[2304,128]{1,0:T(8,128)(2,1)S(1)}, u32[]{:S(2)}, u32[]{:S(2)}) collective-permute-start(bf16[2304,128]{1,0:T(8,128)(2,1)S(1)} %get-tuple-element.101), channel_id=1, source_target_pairs={{0,64},{1,65},{2,66},{3,67},{4,68},{5,69},{6,70},{7,71},{8,72},{9,... | collective-permute-start | bytes 1769480 | tf_op jit(solution)/shard_map/ppermute | solution.py:40
  132.2 1.6 %collective-permute-done.28 = bf16[2304,128]{1,0:T(8,128)(2,1)S(1)} collective-permute-done((bf16[2304,128]{1,0:T(8,128)(2,1)S(1)}, bf16[2304,128]{1,0:T(8,128)(2,1)S(1)}, u32[]{:S(2)}, u32[]{:S(2)}) %collective-permute-start.28) | collective-permute-done | bytes 589856 | tf_op jit(solution)/shard_map/ppermute | solution.py:40
  (72 shorter events, 16.2 us)
Async XLA Ops:
  6.5 64.9 %all-gather.3.cloned.1.call-start = ((), (), s32[]{:S(2)}) async-start(), calls=%async_computation | async-start | bytes 3538944 | tf_op jit(solution)/shard_map/all_gather | solution.py:343
  10.2 9.1 %collective-permute-start.6 = (bf16[1552,128]{1,0:T(8,128)(2,1)S(1)}, bf16[1552,128]{1,0:T(8,128)(2,1)S(1)}, u32[]{:S(2)}, u32[]{:S(2)}) collective-permute-start(bf16[1552,128]{1,0:T(8,128)(2,1)S(1)} %pad_maximum_fusion.1), channel_id=1, source_target_pairs={{0,1},{1,128},{2,3},{3,130},{4,5},{5,132},{6,7},{7,134},{8,9},{9,1... | collective-permute-start | bytes 1191944 | tf_op jit(solution)/shard_map/ppermute | solution.py:40
  12.4 10.5 %collective-permute-start.7 = (bf16[1552,128]{1,0:T(8,128)(2,1)S(1)}, bf16[1552,128]{1,0:T(8,128)(2,1)S(1)}, u32[]{:S(2)}, u32[]{:S(2)}) collective-permute-start(bf16[1552,128]{1,0:T(8,128)(2,1)S(1)} %pad_maximum_fusion.1), channel_id=1, source_target_pairs={{0,129},{1,0},{2,131},{3,2},{4,133},{5,4},{6,135},{7,6},{8,137},{9... | collective-permute-start | bytes 1191944 | tf_op jit(solution)/shard_map/ppermute | solution.py:40
  13.9 10.8 %collective-permute-start.8 = (bf16[1552,128]{1,0:T(8,128)(2,1)S(1)}, bf16[1552,128]{1,0:T(8,128)(2,1)S(1)}, u32[]{:S(2)}, u32[]{:S(2)}) collective-permute-start(bf16[1552,128]{1,0:T(8,128)(2,1)S(1)} %pad_maximum_fusion.1), channel_id=1, source_target_pairs={{0,128},{1,129},{2,130},{3,131},{4,132},{5,133},{6,134},{7,135},{8... | collective-permute-start | bytes 1191944 | tf_op jit(solution)/shard_map/ppermute | solution.py:40
  24.9 22.1 %collective-permute-start.10 = (bf16[6208,128]{1,0:T(8,128)(2,1)S(1)}, bf16[6208,128]{1,0:T(8,128)(2,1)S(1)}, u32[]{:S(2)}, u32[]{:S(2)}) collective-permute-start(bf16[6208,128]{1,0:T(8,128)(2,1)S(1)} %pad_maximum_fusion.refs_1_), channel_id=1, source_target_pairs={{0,6},{1,7},{2,0},{3,1},{4,2},{5,3},{6,4},{7,5},{8,14},{9,15},{10,... | collective-permute-start | bytes 4767752 | tf_op jit(solution)/shard_map/ppermute | solution.py:40
  27.5 21.1 %collective-permute-start.9 = (bf16[6208,128]{1,0:T(8,128)(2,1)S(1)}, bf16[6208,128]{1,0:T(8,128)(2,1)}, u32[]{:S(2)}, u32[]{:S(2)}) collective-permute-start(bf16[6208,128]{1,0:T(8,128)(2,1)S(1)} %pad_maximum_fusion.refs_1_), channel_id=1, source_target_pairs={{0,2},{1,3},{2,4},{3,5},{4,6},{5,7},{6,0},{7,1},{8,10},{9,11},{10,... | collective-permute-start | bytes 4767752 | tf_op jit(solution)/shard_map/ppermute | solution.py:40
  27.5 19.5 %collective-permute-start.11 = (s32[4,128]{1,0:T(4,128)S(1)}, s32[4,128]{1,0:T(4,128)S(1)}, u32[]{:S(2)}, u32[]{:S(2)}) collective-permute-start(s32[4,128]{1,0:T(4,128)S(1)} %fusion.8), channel_id=1, source_target_pairs={{0,4},{1,5},{2,6},{3,7},{4,0},{5,1},{6,2},{7,3},{8,12},{9,13},{10,... | collective-permute-start | bytes 6152 | tf_op jit(solution)/shard_map/ppermute | solution.py:40
  45.9 14.3 %copy-start.3 = (s32[8,1,128]{2,1,0:T(1,128)}, s32[8,1,128]{2,1,0:T(1,128)S(1)}, u32[]{:S(2)}) copy-start(s32[8,1,128]{2,1,0:T(1,128)S(1)} %all-gather) | copy-start | bytes 12292
  49.3 9.7 %collective-permute-start.15 = (s32[16,128]{1,0:T(8,128)S(1)}, s32[16,128]{1,0:T(8,128)S(1)}, u32[]{:S(2)}, u32[]{:S(2)}) collective-permute-start(s32[16,128]{1,0:T(8,128)S(1)} %pad_add_fusion), channel_id=1, source_target_pairs={{0,64},{1,65},{2,66},{3,67},{4,68},{5,69},{6,70},{7,71},{8,72},{9,... | collective-permute-start | bytes 24584 | tf_op jit(solution)/shard_map/ppermute | solution.py:40
  52.0 6.9 %collective-permute-start.14 = (s32[8,128]{1,0:T(8,128)S(1)}, s32[8,128]{1,0:T(8,128)S(1)}, u32[]{:S(2)}, u32[]{:S(2)}) collective-permute-start(s32[8,128]{1,0:T(8,128)S(1)} %bitcast.35), channel_id=1, source_target_pairs={{0,64},{1,65},{2,66},{3,67},{4,68},{5,69},{6,70},{7,71},{8,72},{9,... | collective-permute-start | bytes 12296 | tf_op jit(solution)/shard_map/ppermute | solution.py:40
  55.2 15.4 %collective-permute-start.12 = (bf16[3104,128]{1,0:T(8,128)(2,1)}, bf16[3104,128]{1,0:T(8,128)(2,1)}, u32[]{:S(2)}, u32[]{:S(2)}) collective-permute-start(bf16[3104,128]{1,0:T(8,128)(2,1)} %slice.43), channel_id=1, source_target_pairs={{0,2},{1,3},{2,4},{3,5},{4,6},{5,7},{6,0},{7,1},{8,10},{9,11},{10,... | collective-permute-start | bytes 2383880 | tf_op jit(solution)/shard_map/ppermute | solution.py:40
  56.4 14.2 %collective-permute-start.13 = (bf16[3104,128]{1,0:T(8,128)(2,1)}, bf16[3104,128]{1,0:T(8,128)(2,1)}, u32[]{:S(2)}, u32[]{:S(2)}) collective-permute-start(bf16[3104,128]{1,0:T(8,128)(2,1)} %slice.44), channel_id=1, source_target_pairs={{0,6},{1,7},{2,0},{3,1},{4,2},{5,3},{6,4},{7,5},{8,14},{9,15},{10,... | collective-permute-start | bytes 2383880 | tf_op jit(solution)/shard_map/ppermute | solution.py:40
  57.9 13.5 %collective-permute-start.16 = (bf16[6208,128]{1,0:T(8,128)(2,1)S(1)}, bf16[6208,128]{1,0:T(8,128)(2,1)}, u32[]{:S(2)}, u32[]{:S(2)}) collective-permute-start(bf16[6208,128]{1,0:T(8,128)(2,1)S(1)} %pad_maximum_fusion.refs_1_), channel_id=1, source_target_pairs={{0,64},{1,65},{2,66},{3,67},{4,68},{5,69},{6,70},{7,71},{8,72},{9,... | collective-permute-start | bytes 4767752 | tf_op jit(solution)/shard_map/ppermute | solution.py:40
  58.9 15.8 %collective-permute-start.17 = (bf16[6208,128]{1,0:T(8,128)(2,1)}, bf16[6208,128]{1,0:T(8,128)(2,1)}, u32[]{:S(2)}, u32[]{:S(2)}) collective-permute-start(bf16[6208,128]{1,0:T(8,128)(2,1)} %collective-permute-done.9.refs_2_), channel_id=1, source_target_pairs={{0,64},{1,65},{2,66},{3,67},{4,68},{5,69},{6,70},{7,71},{8,72},{9,... | collective-permute-start | bytes 4767752 | tf_op jit(solution)/shard_map/ppermute | solution.py:40
  59.0 15.7 %collective-permute-start.18 = (bf16[6208,128]{1,0:T(8,128)(2,1)S(1)}, bf16[6208,128]{1,0:T(8,128)(2,1)}, u32[]{:S(2)}, u32[]{:S(2)}) collective-permute-start(bf16[6208,128]{1,0:T(8,128)(2,1)S(1)} %collective-permute-done.10.refs_3_), channel_id=1, source_target_pairs={{0,64},{1,65},{2,66},{3,67},{4,68},{5,69},{6,70},{7,71},{8,72},{9,... | collective-permute-start | bytes 4767752 | tf_op jit(solution)/shard_map/ppermute | solution.py:40
  70.6 11.4 %copy-start.6 = (s32[6,2]{0,1:T(2,128)S(1)}, s32[6,2]{0,1:T(2,128)}, u32[]{:S(2)}) copy-start(s32[6,2]{0,1:T(2,128)} %param.6) | copy-start | bytes 148
  70.6 2.9 %collective-permute-start.19 = (bf16[3104,128]{1,0:T(8,128)(2,1)}, bf16[3104,128]{1,0:T(8,128)(2,1)}, u32[]{:S(2)}, u32[]{:S(2)}) collective-permute-start(bf16[3104,128]{1,0:T(8,128)(2,1)} %collective-permute-done.12.refs_4_), channel_id=1, source_target_pairs={{0,64},{1,65},{2,66},{3,67},{4,68},{5,69},{6,70},{7,71},{8,72},{9,... | collective-permute-start | bytes 2383880 | tf_op jit(solution)/shard_map/ppermute | solution.py:40
  70.9 3.8 %collective-permute-start.20 = (bf16[3104,128]{1,0:T(8,128)(2,1)}, bf16[3104,128]{1,0:T(8,128)(2,1)}, u32[]{:S(2)}, u32[]{:S(2)}) collective-permute-start(bf16[3104,128]{1,0:T(8,128)(2,1)} %collective-permute-done.13.refs_5_), channel_id=1, source_target_pairs={{0,64},{1,65},{2,66},{3,67},{4,68},{5,69},{6,70},{7,71},{8,72},{9,... | collective-permute-start | bytes 2383880 | tf_op jit(solution)/shard_map/ppermute | solution.py:40
  75.4 4.9 %copy-start.5 = (s32[4,128]{1,0:T(4,128)S(1)}, s32[4,128]{1,0:T(4,128)}, u32[]{:S(2)}) copy-start(s32[4,128]{1,0:T(4,128)} %get-tuple-element.90) | copy-start | bytes 6148
  80.1 43.6 %collective-permute-start.24 = (bf16[12288,128]{1,0:T(8,128)(2,1)}, bf16[12288,128]{1,0:T(8,128)(2,1)S(1)}, u32[]{:S(2)}, u32[]{:S(2)}) collective-permute-start(bf16[12288,128]{1,0:T(8,128)(2,1)} %all-gather.3.cloned.1.call-done.refs_0_), channel_id=1, source_target_pairs={{0,64},{1,65},{2,66},{3,67},{4,68},{5,69},{6,70},{7,71},{8,72},{9,... | collective-permute-start | bytes 9437192 | tf_op jit(solution)/shard_map/ppermute | solution.py:40
  80.2 4.7 %collective-permute-start.21 = (s32[1,128]{1,0:T(1,128)S(1)}, s32[1,128]{1,0:T(1,128)S(1)}, u32[]{:S(2)}, u32[]{:S(2)}) collective-permute-start(s32[1,128]{1,0:T(1,128)S(1)} %get-tuple-element.102), channel_id=1, source_target_pairs={{0,6},{1,7},{2,0},{3,1},{4,2},{5,3},{6,4},{7,5},{8,14},{9,15},{10,... | collective-permute-start | bytes 1544 | tf_op jit(solution)/shard_map/ppermute | solution.py:40
  82.2 3.9 %collective-permute-start.22 = (s32[1,128]{1,0:T(1,128)S(1)}, s32[1,128]{1,0:T(1,128)S(1)}, u32[]{:S(2)}, u32[]{:S(2)}) collective-permute-start(s32[1,128]{1,0:T(1,128)S(1)} %get-tuple-element.104), channel_id=1, source_target_pairs={{0,2},{1,3},{2,4},{3,5},{4,6},{5,7},{6,0},{7,1},{8,10},{9,11},{10,... | collective-permute-start | bytes 1544 | tf_op jit(solution)/shard_map/ppermute | solution.py:40
  82.2 17.0 %collective-permute-start.25 = (bf16[2304,128]{1,0:T(8,128)(2,1)}, bf16[2304,128]{1,0:T(8,128)(2,1)}, u32[]{:S(2)}, u32[]{:S(2)}) collective-permute-start(bf16[2304,128]{1,0:T(8,128)(2,1)} %shard_map.38.refs_2_), channel_id=1, source_target_pairs={{0,1},{1,128},{2,3},{3,130},{4,5},{5,132},{6,7},{7,134},{8,9},{9,1... | collective-permute-start | bytes 1769480 | tf_op jit(solution)/shard_map/ppermute | solution.py:40
  82.8 16.3 %collective-permute-start.26 = (bf16[2304,128]{1,0:T(8,128)(2,1)}, bf16[2304,128]{1,0:T(8,128)(2,1)}, u32[]{:S(2)}, u32[]{:S(2)}) collective-permute-start(bf16[2304,128]{1,0:T(8,128)(2,1)} %shard_map.38.refs_2_), channel_id=1, source_target_pairs={{0,129},{1,0},{2,131},{3,2},{4,133},{5,4},{6,135},{7,6},{8,137},{9... | collective-permute-start | bytes 1769480 | tf_op jit(solution)/shard_map/ppermute | solution.py:40
  84.9 14.2 %collective-permute-start.27 = (bf16[2304,128]{1,0:T(8,128)(2,1)}, bf16[2304,128]{1,0:T(8,128)(2,1)}, u32[]{:S(2)}, u32[]{:S(2)}) collective-permute-start(bf16[2304,128]{1,0:T(8,128)(2,1)} %shard_map.38.refs_2_), channel_id=1, source_target_pairs={{0,128},{1,129},{2,130},{3,131},{4,132},{5,133},{6,134},{7,135},{8... | collective-permute-start | bytes 1769480 | tf_op jit(solution)/shard_map/ppermute | solution.py:40
  86.0 4.1 %collective-permute-start.23 = (s32[1,128]{1,0:T(1,128)S(1)}, s32[1,128]{1,0:T(1,128)S(1)}, u32[]{:S(2)}, u32[]{:S(2)}) collective-permute-start(s32[1,128]{1,0:T(1,128)S(1)} %get-tuple-element.103), channel_id=1, source_target_pairs={{0,4},{1,5},{2,6},{3,7},{4,0},{5,1},{6,2},{7,3},{8,12},{9,13},{10,... | collective-permute-start | bytes 1544 | tf_op jit(solution)/shard_map/ppermute | solution.py:40
  99.1 24.5 %copy-start = (s32[865]{0:T(1024)S(1)}, s32[865]{0:T(1024)}, u32[]{:S(2)}) copy-start(s32[865]{0:T(1024)} %get-tuple-element.91.jobs_ref) | copy-start | bytes 10384
  102.8 12.0 %collective-permute-start = (bf16[2816,128]{1,0:T(8,128)(2,1)}, bf16[2816,128]{1,0:T(8,128)(2,1)}, u32[]{:S(2)}, u32[]{:S(2)}) collective-permute-start(bf16[2816,128]{1,0:T(8,128)(2,1)} %get-tuple-element.44), channel_id=1, source_target_pairs={{0,2},{1,3},{2,4},{3,5},{4,6},{5,7},{6,0},{7,1},{8,10},{9,11},{10,... | collective-permute-start | bytes 2162696 | tf_op jit(solution)/shard_map/cond/branch_1_fun/ppermute | solution.py:40
  102.9 18.9 %collective-permute-start.1 = (bf16[2816,128]{1,0:T(8,128)(2,1)}, bf16[2816,128]{1,0:T(8,128)(2,1)}, u32[]{:S(2)}, u32[]{:S(2)}) collective-permute-start(bf16[2816,128]{1,0:T(8,128)(2,1)} %get-tuple-element.45), channel_id=1, source_target_pairs={{0,6},{1,7},{2,0},{3,1},{4,2},{5,3},{6,4},{7,5},{8,14},{9,15},{10,... | collective-permute-start | bytes 2162696 | tf_op jit(solution)/shard_map/cond/branch_1_fun/ppermute | solution.py:40
  105.6 18.1 %collective-permute-start.2 = (bf16[2816,128]{1,0:T(8,128)(2,1)}, bf16[2816,128]{1,0:T(8,128)(2,1)}, u32[]{:S(2)}, u32[]{:S(2)}) collective-permute-start(bf16[2816,128]{1,0:T(8,128)(2,1)} %get-tuple-element.46), channel_id=1, source_target_pairs={{0,4},{1,5},{2,6},{3,7},{4,0},{5,1},{6,2},{7,3},{8,12},{9,13},{10,... | collective-permute-start | bytes 2162696 | tf_op jit(solution)/shard_map/cond/branch_1_fun/ppermute | solution.py:40
  123.7 10.1 %copy-start.2 = (f32[6,3,128,128]{3,2,1,0:T(8,128)S(1)}, f32[6,3,128,128]{3,2,1,0:T(8,128)}, u32[]{:S(2)}) copy-start(f32[6,3,128,128]{3,2,1,0:T(8,128)} %convert_multiply_fusion) | copy-start | bytes 3538948
  130.5 3.3 %collective-permute-start.28 = (bf16[2304,128]{1,0:T(8,128)(2,1)S(1)}, bf16[2304,128]{1,0:T(8,128)(2,1)S(1)}, u32[]{:S(2)}, u32[]{:S(2)}) collective-permute-start(bf16[2304,128]{1,0:T(8,128)(2,1)S(1)} %get-tuple-element.101), channel_id=1, source_target_pairs={{0,64},{1,65},{2,66},{3,67},{4,68},{5,69},{6,70},{7,71},{8,72},{9,... | collective-permute-start | bytes 1769480 | tf_op jit(solution)/shard_map/ppermute | solution.py:40
  (2 other events, 2.0 us)
Sparse Core Ops, SparseCore 0:
  9.1 48.5 all-gather.2

commit v5 on v4

--- a/solution.py
+++ b/solution.py
@@ -164,11 +164,17 @@
         s_jobs[1 + JOBS + count] = jnp.where(outer == 0, near, packed)
         s_jobs[1 + 2 * JOBS + count] = jnp.where(outer == 0, near, dense)
 
-    panels = [(panel, ((panel // 2 % 2) ^ core) * 16 + (panel // 4 * 2 + panel % 2) * 4) for panel in range(8)]
+    def add_both(group, inner, outer, place, slot, left, out):
+        add_s(0, group, inner, outer, place, slot, left, out)
+        if slot < KA:
+            held = plane_ref[group_code[3, group], place * KA + slot] >= 0
+            pl.when(held)(functools.partial(add_x, group, inner, outer, place, slot, left, out))
+
+    panels = [(panel // 2 * 4 + 2 * core + panel % 2, panel * 4) for panel in range(4)]
+    plan_scan(own_ref, z, panels, plane_ref, group_code, KC, add_both)
+    plan_scan(other_ref, z, panels, plane_ref, group_code, KC, functools.partial(add_s, 1))
+    panels = [(panel // 2 * 4 + 2 * (1 - core) + panel % 2, 16 + panel * 4) for panel in range(4)]
     plan_scan(own_ref, z, panels, plane_ref, group_code, KA, add_x)
-    panels = [(panel // 2 * 4 + 2 * core + panel % 2, panel * 4) for panel in range(4)]
-    for half, marks_ref in enumerate((own_ref, other_ref)):
-        plan_scan(marks_ref, z, panels, plane_ref, group_code, KC, functools.partial(add_s, half))
     most = jnp.maximum(takes[1, COUNT], jnp.maximum(takes[2, COUNT], takes[3, COUNT]))
     for outer in range(4):
         takes[outer, MOST] = most
@@ -350,8 +356,9 @@
     row_marks = lax.all_gather(marks, "col", axis=0, tiled=True)
     plus, minus, far_marks, row_marks = lax.optimization_barrier((plus, minus, far_marks, row_marks))
     half = plus.shape[0] // 2
-    far = second_ring(plus[:half], 1), second_ring(minus[half:], -1)
     plane_marks = jnp.concatenate([near_marks, marks_of(plus), marks_of(minus), far_marks], axis=0)
+    ahead, behind, plane_marks = lax.optimization_barrier((plus[:half], minus[half:], plane_marks))
+    far = second_ring(ahead, 1), second_ring(behind, -1)
     beside = jnp.pad(swap(plane_marks)[:, : BLK // 2], ((0, 0), (BLK // 2, 0)))
     x_jobs, s_jobs, takes = plan(here, row_marks, swap(row_marks), plane_marks + beside)
     far, x_jobs = lax.optimization_barrier((far, x_jobs))

time: 143 us -> 144 us (level)
  starting transfers between devices: 28.5 us -> 31.1 us
    ppermute x26, starting transfers between devices: 28.5 us -> 31.1 us  [move(): return lax.ppermute(array, ALL, pairs)]
  transfers between devices with their start and end apart: 27 -> 27, of which waited for: 13 -> 15; matrix products, arithmetic and copies ran while one was open for 7% -> 7% of each run, Pallas kernels for 10% -> 9%
where the time goes in v5:
time: 144 us; the launch traced here: 143 us
  waiting for transfers between devices  44.2 us (31%)
  starting transfers between devices  31.1 us (22%)
  Pallas kernels  24.3 us (17%)
  blocking collectives  16.9 us (12%)
  between operations  14.1 us (10%)
  other arithmetic  6.68 us (5%)
  local copies, waits for them, and re-layouts  5.58 us (4%)
    ppermute x26, waiting for transfers between devices, move(): return lax.ppermute(array, ALL, pairs)  43.4 us
    ppermute x26, starting transfers between devices, move(): return lax.ppermute(array, ALL, pairs)  31.1 us
    all_gather x1, blocking collectives, local(): row_marks = lax.all_gather(marks, 'col', axis=0, tiled=True)  16.9 us
    pallas_call x2, Pallas kernels, product(): pl.pallas_call(functools.partial(product_kernel, len(lefts), len(rights))...  11.5 us
    pallas_call x1, Pallas kernels, plan(): pl.pallas_call(plan_kernel, out_shape=(JOB_TABLE, JOB_TABLE, jax.ShapeDty...  9.35 us
    pallas_call x1, Pallas kernels, pack(): pl.pallas_call(pack_kernel, out_shape=(shape,) * 3, in_specs=[SMEM] * 4 +...  3.49 us
  transfers between devices with their start and end apart: 27, of which 15 were waited for; matrix products, arithmetic and copies ran while one was open for 7% of the time, Pallas kernels for 9%

profile of v5, /device:TPU:1, one launch (start us, length us, event | category | flops | bytes accessed | tf_op | source)
XLA Modules:
  0.0 142.8 jit_solution(8540271629520443861)
XLA Ops:
  10.2 2.2 %collective-permute-start.6 = (bf16[1552,128]{1,0:T(8,128)(2,1)S(1)}, bf16[1552,128]{1,0:T(8,128)(2,1)S(1)}, u32[]{:S(2)}, u32[]{:S(2)}) collective-permute-start(bf16[1552,128]{1,0:T(8,128)(2,1)S(1)} %pad_maximum_fusion.1), channel_id=1, source_target_pairs={{0,1},{1,128},{2,3},{3,130},{4,5},{5,132},{6,7},{7,134},{8,9},{9,1... | collective-permute-start | bytes 1191944 | tf_op jit(solution)/shard_map/ppermute | solution.py:40
  12.4 1.5 %collective-permute-start.7 = (bf16[1552,128]{1,0:T(8,128)(2,1)S(1)}, bf16[1552,128]{1,0:T(8,128)(2,1)S(1)}, u32[]{:S(2)}, u32[]{:S(2)}) collective-permute-start(bf16[1552,128]{1,0:T(8,128)(2,1)S(1)} %pad_maximum_fusion.1), channel_id=1, source_target_pairs={{0,129},{1,0},{2,131},{3,2},{4,133},{5,4},{6,135},{7,6},{8,137},{9... | collective-permute-start | bytes 1191944 | tf_op jit(solution)/shard_map/ppermute | solution.py:40
  13.9 1.6 %collective-permute-start.8 = (bf16[1552,128]{1,0:T(8,128)(2,1)S(1)}, bf16[1552,128]{1,0:T(8,128)(2,1)S(1)}, u32[]{:S(2)}, u32[]{:S(2)}) collective-permute-start(bf16[1552,128]{1,0:T(8,128)(2,1)S(1)} %pad_maximum_fusion.1), channel_id=1, source_target_pairs={{0,128},{1,129},{2,130},{3,131},{4,132},{5,133},{6,134},{7,135},{8... | collective-permute-start | bytes 1191944 | tf_op jit(solution)/shard_map/ppermute | solution.py:40
  15.5 3.9 %collective-permute-done.6 = bf16[1552,128]{1,0:T(8,128)(2,1)S(1)} collective-permute-done((bf16[1552,128]{1,0:T(8,128)(2,1)S(1)}, bf16[1552,128]{1,0:T(8,128)(2,1)S(1)}, u32[]{:S(2)}, u32[]{:S(2)}) %collective-permute-start.6) | collective-permute-done | bytes 397344 | tf_op jit(solution)/shard_map/ppermute | solution.py:40
  19.4 3.6 %collective-permute-done.7 = bf16[1552,128]{1,0:T(8,128)(2,1)S(1)} collective-permute-done((bf16[1552,128]{1,0:T(8,128)(2,1)S(1)}, bf16[1552,128]{1,0:T(8,128)(2,1)S(1)}, u32[]{:S(2)}, u32[]{:S(2)}) %collective-permute-start.7) | collective-permute-done | bytes 397344 | tf_op jit(solution)/shard_map/ppermute | solution.py:40
  23.0 1.8 %collective-permute-done.8 = bf16[1552,128]{1,0:T(8,128)(2,1)S(1)} collective-permute-done((bf16[1552,128]{1,0:T(8,128)(2,1)S(1)}, bf16[1552,128]{1,0:T(8,128)(2,1)S(1)}, u32[]{:S(2)}, u32[]{:S(2)}) %collective-permute-start.8) | collective-permute-done | bytes 397344 | tf_op jit(solution)/shard_map/ppermute | solution.py:40
  24.9 2.6 %collective-permute-start.10 = (bf16[6208,128]{1,0:T(8,128)(2,1)S(1)}, bf16[6208,128]{1,0:T(8,128)(2,1)S(1)}, u32[]{:S(2)}, u32[]{:S(2)}) collective-permute-start(bf16[6208,128]{1,0:T(8,128)(2,1)S(1)} %pad_maximum_fusion.refs_1_), channel_id=1, source_target_pairs={{0,6},{1,7},{2,0},{3,1},{4,2},{5,3},{6,4},{7,5},{8,14},{9,15},{10,... | collective-permute-start | bytes 4767752 | tf_op jit(solution)/shard_map/ppermute | solution.py:40
  27.5 1.5 %collective-permute-start.11 = (s32[4,128]{1,0:T(4,128)S(1)}, s32[4,128]{1,0:T(4,128)S(1)}, u32[]{:S(2)}, u32[]{:S(2)}) collective-permute-start(s32[4,128]{1,0:T(4,128)S(1)} %fusion.8), channel_id=1, source_target_pairs={{0,4},{1,5},{2,6},{3,7},{4,0},{5,1},{6,2},{7,3},{8,12},{9,13},{10,... | collective-permute-start | bytes 6152 | tf_op jit(solution)/shard_map/ppermute | solution.py:40
  29.0 16.9 %all-gather = s32[8,1,128]{2,1,0:T(1,128)S(1)} all-gather(s32[1,1,128]{2,1,0:T(1,128)S(1)} %bitcast.38), channel_id=1, replica_groups=mesh['row'=4,'col'=8,'depth'=8] {'col'}, dimensions={0}, use_global_device_ids=true | all-gather | bytes 4608 | tf_op jit(solution)/shard_map/all_gather | solution.py:356
  47.0 1.5 %collective-permute-done.9.refs_2_ = bf16[6208,128]{1,0:T(8,128)(2,1)} collective-permute-done((bf16[6208,128]{1,0:T(8,128)(2,1)S(1)}, bf16[6208,128]{1,0:T(8,128)(2,1)}, u32[]{:S(2)}, u32[]{:S(2)}) %collective-permute-start.9) | collective-permute-done | bytes 1589280 | tf_op jit(solution)/shard_map/ppermute | solution.py:40
  48.5 2.1 %slice.43 = bf16[3104,128]{1,0:T(8,128)(2,1)} slice(bf16[6208,128]{1,0:T(8,128)(2,1)} %collective-permute-done.9.refs_2_), slice={[0:3104], [0:128]} | slice | bytes 1589248 | tf_op jit(solution)/shard_map/slice | solution.py:360
  52.4 2.7 %collective-permute-start.15 = (s32[16,128]{1,0:T(8,128)S(1)}, s32[16,128]{1,0:T(8,128)S(1)}, u32[]{:S(2)}, u32[]{:S(2)}) collective-permute-start(s32[16,128]{1,0:T(8,128)S(1)} %pad_add_fusion), channel_id=1, source_target_pairs={{0,64},{1,65},{2,66},{3,67},{4,68},{5,69},{6,70},{7,71},{8,72},{9,... | collective-permute-start | bytes 24584 | tf_op jit(solution)/shard_map/ppermute | solution.py:40
  55.2 1.1 collective-permute-start.12
  56.4 1.5 %collective-permute-start.13 = (bf16[3104,128]{1,0:T(8,128)(2,1)}, bf16[3104,128]{1,0:T(8,128)(2,1)}, u32[]{:S(2)}, u32[]{:S(2)}) collective-permute-start(bf16[3104,128]{1,0:T(8,128)(2,1)} %slice.44), channel_id=1, source_target_pairs={{0,6},{1,7},{2,0},{3,1},{4,2},{5,3},{6,4},{7,5},{8,14},{9,15},{10,... | collective-permute-start | bytes 2383880 | tf_op jit(solution)/shard_map/ppermute | solution.py:40
  60.1 9.3 %shard_map.37 = (s32[865]{0:T(1024)}, s32[865]{0:T(1024)}, s32[4,128]{1,0:T(4,128)}) custom-call(s32[4]{0:T(128)S(1)} %pad_add_fusion.2.here_ref, s32[8,128]{1,0:T(8,128)} %bitcast.36, s32[8,128]{1,0:T(8,128)} %copy-done.4, s32[16,128]{1,0:T(8,128)} %pad_add_fusion.1.plane_ref), custom_call_target="tpu_custom_call" | custom-call | flops 1000 | bytes 1000 | tf_op jit(solution)/shard_map/pallas_call | solution.py:193
  70.1 2.1 %collective-permute-done.19.refs_9_ = bf16[3104,128]{1,0:T(8,128)(2,1)} collective-permute-done((bf16[3104,128]{1,0:T(8,128)(2,1)}, bf16[3104,128]{1,0:T(8,128)(2,1)}, u32[]{:S(2)}, u32[]{:S(2)}) %collective-permute-start.19) | collective-permute-done | bytes 794656 | tf_op jit(solution)/shard_map/ppermute | solution.py:40
  74.1 4.8 %shard_map.38.refs_2_ = bf16[2304,128]{1,0:T(8,128)(2,1)} custom-call(s32[1]{0:T(128)} %constant.52.clone.1.most_ref, s32[865]{0:T(1024)S(1)} %copy-done.1, bf16[12288,128]{1,0:T(8,128)(2,1)} %all-gather.3.cloned.1.call-done.refs_0_, bf16[6208,128]{1,0:T(8,128)(2,1)S(1)} %pad_maximum_fusion.refs_1_, bf16[6208,128]{1,0:T(8,128)(2,1)} %collective-permute-done.9.refs_2_, ...), custom_call_target="tpu_custom_call" | custom-call | tf_op jit(solution)/shard_map/pallas_call | solution.py:263
  79.1 1.3 collective-permute-start.21
  81.0 2.5 %collective-permute-start.26 = (bf16[2304,128]{1,0:T(8,128)(2,1)}, bf16[2304,128]{1,0:T(8,128)(2,1)}, u32[]{:S(2)}, u32[]{:S(2)}) collective-permute-start(bf16[2304,128]{1,0:T(8,128)(2,1)} %shard_map.38.refs_2_), channel_id=1, source_target_pairs={{0,129},{1,0},{2,131},{3,2},{4,133},{5,4},{6,135},{7,6},{8,137},{9... | collective-permute-start | bytes 1769480 | tf_op jit(solution)/shard_map/ppermute | solution.py:40
  85.7 1.3 collective-permute-start.23
  88.1 1.7 %collective-permute-done.23 = s32[1,128]{1,0:T(1,128)S(1)} collective-permute-done((s32[1,128]{1,0:T(1,128)S(1)}, s32[1,128]{1,0:T(1,128)S(1)}, u32[]{:S(2)}, u32[]{:S(2)}) %collective-permute-start.23) | collective-permute-done | bytes 544 | tf_op jit(solution)/shard_map/ppermute | solution.py:40
  91.3 5.7 %collective-permute-done.26.refs_4_ = bf16[2304,128]{1,0:T(8,128)(2,1)} collective-permute-done((bf16[2304,128]{1,0:T(8,128)(2,1)}, bf16[2304,128]{1,0:T(8,128)(2,1)}, u32[]{:S(2)}, u32[]{:S(2)}) %collective-permute-start.26) | collective-permute-done | bytes 589856 | tf_op jit(solution)/shard_map/ppermute | solution.py:40
  97.0 1.8 %collective-permute-done.27.refs_5_ = bf16[2304,128]{1,0:T(8,128)(2,1)} collective-permute-done((bf16[2304,128]{1,0:T(8,128)(2,1)}, bf16[2304,128]{1,0:T(8,128)(2,1)}, u32[]{:S(2)}, u32[]{:S(2)}) %collective-permute-start.27) | collective-permute-done | bytes 589856 | tf_op jit(solution)/shard_map/ppermute | solution.py:40
  98.8 24.6 %conditional.1 = (bf16[2816,128]{1,0:T(8,128)(2,1)}, bf16[2816,128]{1,0:T(8,128)(2,1)}, bf16[2816,128]{1,0:T(8,128)(2,1)}, bf16[9216,128]{1,0:T(8,128)(2,1)}, bf...) conditional(s32[]{:T(128)} %bitcast.16, (bf16[2304,128]{1,0:T(8,128)(2,1)}, bf16[2304,128]{1,0:T(8,128)(2,1)}, ...), branch_computations={%region_0.1_spmd, %region_1.2_spmd} | conditional | bytes 33030312 | solution.py:334
  98.8 3.5 %branch_1_fun.2 = (bf16[2816,128]{1,0:T(8,128)(2,1)}, bf16[2816,128]{1,0:T(8,128)(2,1)}, bf16[2816,128]{1,0:T(8,128)(2,1)}) custom-call(s32[4]{0:T(128)S(1)} %get-tuple-element.36.here_ref, s32[1,128]{1,0:T(1,128)S(1)} %get-tuple-element.37.refs_0_, s32[1,128]{1,0:T(1,128)S(1)} %get-tuple-element.38.refs_1_, s32[1,128]{1,0:T(1,128)S(1)} %get-tuple-element.39.refs_2_, ...), custom_call_target="tpu_custom_call" | custom-call | tf_op jit(solution)/shard_map/cond/branch_1_fun/pallas_call | solution.py:309
  102.9 2.4 %collective-permute-start.1 = (bf16[2816,128]{1,0:T(8,128)(2,1)}, bf16[2816,128]{1,0:T(8,128)(2,1)}, u32[]{:S(2)}, u32[]{:S(2)}) collective-permute-start(bf16[2816,128]{1,0:T(8,128)(2,1)} %get-tuple-element.45), channel_id=1, source_target_pairs={{0,6},{1,7},{2,0},{3,1},{4,2},{5,3},{6,4},{7,5},{8,14},{9,15},{10,... | collective-permute-start | bytes 2162696 | tf_op jit(solution)/shard_map/cond/branch_1_fun/ppermute | solution.py:40
  106.4 8.1 %collective-permute-done = bf16[2816,128]{1,0:T(8,128)(2,1)} collective-permute-done((bf16[2816,128]{1,0:T(8,128)(2,1)}, bf16[2816,128]{1,0:T(8,128)(2,1)}, u32[]{:S(2)}, u32[]{:S(2)}) %collective-permute-start) | collective-permute-done | bytes 720928 | tf_op jit(solution)/shard_map/cond/branch_1_fun/ppermute | solution.py:40
  114.5 7.1 %collective-permute-done.1 = bf16[2816,128]{1,0:T(8,128)(2,1)} collective-permute-done((bf16[2816,128]{1,0:T(8,128)(2,1)}, bf16[2816,128]{1,0:T(8,128)(2,1)}, u32[]{:S(2)}, u32[]{:S(2)}) %collective-permute-start.1) | collective-permute-done | bytes 720928 | tf_op jit(solution)/shard_map/cond/branch_1_fun/ppermute | solution.py:40
  121.6 1.8 %collective-permute-done.2 = bf16[2816,128]{1,0:T(8,128)(2,1)} collective-permute-done((bf16[2816,128]{1,0:T(8,128)(2,1)}, bf16[2816,128]{1,0:T(8,128)(2,1)}, u32[]{:S(2)}, u32[]{:S(2)}) %collective-permute-start.2) | collective-permute-done | bytes 720928 | tf_op jit(solution)/shard_map/cond/branch_1_fun/ppermute | solution.py:40
  123.4 6.7 %shard_map.39 = (bf16[2304,128]{1,0:T(8,128)(2,1)S(1)}, bf16[2304,128]{1,0:T(8,128)(2,1)S(1)}) custom-call(s32[1]{0:T(128)} %bitcast.15.most_ref, s32[865]{0:T(1024)S(1)} %copy-done, bf16[12288,128]{1,0:T(8,128)(2,1)} %all-gather.3.cloned.1.call-done.refs_0_, bf16[12288,128]{1,0:T(8,128)(2,1)S(1)} %collective-permute-done.24.refs_1_, ...), custom_call_target="tpu_custom_call" | custom-call | tf_op jit(solution)/shard_map/pallas_call | solution.py:263
  130.2 3.1 %collective-permute-start.28 = (bf16[2304,128]{1,0:T(8,128)(2,1)S(1)}, bf16[2304,128]{1,0:T(8,128)(2,1)S(1)}, u32[]{:S(2)}, u32[]{:S(2)}) collective-permute-start(bf16[2304,128]{1,0:T(8,128)(2,1)S(1)} %get-tuple-element.107), channel_id=1, source_target_pairs={{0,64},{1,65},{2,66},{3,67},{4,68},{5,69},{6,70},{7,71},{8,72},{9,... | collective-permute-start | bytes 1769480 | tf_op jit(solution)/shard_map/ppermute | solution.py:40
  133.3 1.6 %collective-permute-done.28 = bf16[2304,128]{1,0:T(8,128)(2,1)S(1)} collective-permute-done((bf16[2304,128]{1,0:T(8,128)(2,1)S(1)}, bf16[2304,128]{1,0:T(8,128)(2,1)S(1)}, u32[]{:S(2)}, u32[]{:S(2)}) %collective-permute-start.28) | collective-permute-done | bytes 589856 | tf_op jit(solution)/shard_map/ppermute | solution.py:40
  (72 shorter events, 19.2 us)
Async XLA Ops:
  6.5 63.6 %all-gather.3.cloned.1.call-start = ((), (), s32[]{:S(2)}) async-start(), calls=%async_computation | async-start | bytes 3538944 | tf_op jit(solution)/shard_map/all_gather | solution.py:349
  10.2 9.1 %collective-permute-start.6 = (bf16[1552,128]{1,0:T(8,128)(2,1)S(1)}, bf16[1552,128]{1,0:T(8,128)(2,1)S(1)}, u32[]{:S(2)}, u32[]{:S(2)}) collective-permute-start(bf16[1552,128]{1,0:T(8,128)(2,1)S(1)} %pad_maximum_fusion.1), channel_id=1, source_target_pairs={{0,1},{1,128},{2,3},{3,130},{4,5},{5,132},{6,7},{7,134},{8,9},{9,1... | collective-permute-start | bytes 1191944 | tf_op jit(solution)/shard_map/ppermute | solution.py:40
  12.4 10.5 %collective-permute-start.7 = (bf16[1552,128]{1,0:T(8,128)(2,1)S(1)}, bf16[1552,128]{1,0:T(8,128)(2,1)S(1)}, u32[]{:S(2)}, u32[]{:S(2)}) collective-permute-start(bf16[1552,128]{1,0:T(8,128)(2,1)S(1)} %pad_maximum_fusion.1), channel_id=1, source_target_pairs={{0,129},{1,0},{2,131},{3,2},{4,133},{5,4},{6,135},{7,6},{8,137},{9... | collective-permute-start | bytes 1191944 | tf_op jit(solution)/shard_map/ppermute | solution.py:40
  13.9 10.8 %collective-permute-start.8 = (bf16[1552,128]{1,0:T(8,128)(2,1)S(1)}, bf16[1552,128]{1,0:T(8,128)(2,1)S(1)}, u32[]{:S(2)}, u32[]{:S(2)}) collective-permute-start(bf16[1552,128]{1,0:T(8,128)(2,1)S(1)} %pad_maximum_fusion.1), channel_id=1, source_target_pairs={{0,128},{1,129},{2,130},{3,131},{4,132},{5,133},{6,134},{7,135},{8... | collective-permute-start | bytes 1191944 | tf_op jit(solution)/shard_map/ppermute | solution.py:40
  24.9 22.1 %collective-permute-start.10 = (bf16[6208,128]{1,0:T(8,128)(2,1)S(1)}, bf16[6208,128]{1,0:T(8,128)(2,1)S(1)}, u32[]{:S(2)}, u32[]{:S(2)}) collective-permute-start(bf16[6208,128]{1,0:T(8,128)(2,1)S(1)} %pad_maximum_fusion.refs_1_), channel_id=1, source_target_pairs={{0,6},{1,7},{2,0},{3,1},{4,2},{5,3},{6,4},{7,5},{8,14},{9,15},{10,... | collective-permute-start | bytes 4767752 | tf_op jit(solution)/shard_map/ppermute | solution.py:40
  27.5 21.1 %collective-permute-start.9 = (bf16[6208,128]{1,0:T(8,128)(2,1)S(1)}, bf16[6208,128]{1,0:T(8,128)(2,1)}, u32[]{:S(2)}, u32[]{:S(2)}) collective-permute-start(bf16[6208,128]{1,0:T(8,128)(2,1)S(1)} %pad_maximum_fusion.refs_1_), channel_id=1, source_target_pairs={{0,2},{1,3},{2,4},{3,5},{4,6},{5,7},{6,0},{7,1},{8,10},{9,11},{10,... | collective-permute-start | bytes 4767752 | tf_op jit(solution)/shard_map/ppermute | solution.py:40
  27.5 19.5 %collective-permute-start.11 = (s32[4,128]{1,0:T(4,128)S(1)}, s32[4,128]{1,0:T(4,128)S(1)}, u32[]{:S(2)}, u32[]{:S(2)}) collective-permute-start(s32[4,128]{1,0:T(4,128)S(1)} %fusion.8), channel_id=1, source_target_pairs={{0,4},{1,5},{2,6},{3,7},{4,0},{5,1},{6,2},{7,3},{8,12},{9,13},{10,... | collective-permute-start | bytes 6152 | tf_op jit(solution)/shard_map/ppermute | solution.py:40
  45.9 14.2 %copy-start.3 = (s32[8,1,128]{2,1,0:T(1,128)}, s32[8,1,128]{2,1,0:T(1,128)S(1)}, u32[]{:S(2)}) copy-start(s32[8,1,128]{2,1,0:T(1,128)S(1)} %all-gather) | copy-start | bytes 12292
  52.4 6.6 %collective-permute-start.15 = (s32[16,128]{1,0:T(8,128)S(1)}, s32[16,128]{1,0:T(8,128)S(1)}, u32[]{:S(2)}, u32[]{:S(2)}) collective-permute-start(s32[16,128]{1,0:T(8,128)S(1)} %pad_add_fusion), channel_id=1, source_target_pairs={{0,64},{1,65},{2,66},{3,67},{4,68},{5,69},{6,70},{7,71},{8,72},{9,... | collective-permute-start | bytes 24584 | tf_op jit(solution)/shard_map/ppermute | solution.py:40
  55.1 3.8 %collective-permute-start.14 = (s32[8,128]{1,0:T(8,128)S(1)}, s32[8,128]{1,0:T(8,128)S(1)}, u32[]{:S(2)}, u32[]{:S(2)}) collective-permute-start(s32[8,128]{1,0:T(8,128)S(1)} %bitcast.35), channel_id=1, source_target_pairs={{0,64},{1,65},{2,66},{3,67},{4,68},{5,69},{6,70},{7,71},{8,72},{9,... | collective-permute-start | bytes 12296 | tf_op jit(solution)/shard_map/ppermute | solution.py:40
  55.2 14.3 %collective-permute-start.12 = (bf16[3104,128]{1,0:T(8,128)(2,1)}, bf16[3104,128]{1,0:T(8,128)(2,1)}, u32[]{:S(2)}, u32[]{:S(2)}) collective-permute-start(bf16[3104,128]{1,0:T(8,128)(2,1)} %slice.43), channel_id=1, source_target_pairs={{0,2},{1,3},{2,4},{3,5},{4,6},{5,7},{6,0},{7,1},{8,10},{9,11},{10,... | collective-permute-start | bytes 2383880 | tf_op jit(solution)/shard_map/ppermute | solution.py:40
  56.4 13.2 %collective-permute-start.13 = (bf16[3104,128]{1,0:T(8,128)(2,1)}, bf16[3104,128]{1,0:T(8,128)(2,1)}, u32[]{:S(2)}, u32[]{:S(2)}) collective-permute-start(bf16[3104,128]{1,0:T(8,128)(2,1)} %slice.44), channel_id=1, source_target_pairs={{0,6},{1,7},{2,0},{3,1},{4,2},{5,3},{6,4},{7,5},{8,14},{9,15},{10,... | collective-permute-start | bytes 2383880 | tf_op jit(solution)/shard_map/ppermute | solution.py:40
  57.9 12.2 %collective-permute-start.16 = (bf16[6208,128]{1,0:T(8,128)(2,1)S(1)}, bf16[6208,128]{1,0:T(8,128)(2,1)}, u32[]{:S(2)}, u32[]{:S(2)}) collective-permute-start(bf16[6208,128]{1,0:T(8,128)(2,1)S(1)} %pad_maximum_fusion.refs_1_), channel_id=1, source_target_pairs={{0,64},{1,65},{2,66},{3,67},{4,68},{5,69},{6,70},{7,71},{8,72},{9,... | collective-permute-start | bytes 4767752 | tf_op jit(solution)/shard_map/ppermute | solution.py:40
  58.9 14.5 %collective-permute-start.17 = (bf16[6208,128]{1,0:T(8,128)(2,1)}, bf16[6208,128]{1,0:T(8,128)(2,1)}, u32[]{:S(2)}, u32[]{:S(2)}) collective-permute-start(bf16[6208,128]{1,0:T(8,128)(2,1)} %collective-permute-done.9.refs_2_), channel_id=1, source_target_pairs={{0,64},{1,65},{2,66},{3,67},{4,68},{5,69},{6,70},{7,71},{8,72},{9,... | collective-permute-start | bytes 4767752 | tf_op jit(solution)/shard_map/ppermute | solution.py:40
  59.0 14.4 %collective-permute-start.18 = (bf16[6208,128]{1,0:T(8,128)(2,1)S(1)}, bf16[6208,128]{1,0:T(8,128)(2,1)}, u32[]{:S(2)}, u32[]{:S(2)}) collective-permute-start(bf16[6208,128]{1,0:T(8,128)(2,1)S(1)} %collective-permute-done.10.refs_3_), channel_id=1, source_target_pairs={{0,64},{1,65},{2,66},{3,67},{4,68},{5,69},{6,70},{7,71},{8,72},{9,... | collective-permute-start | bytes 4767752 | tf_op jit(solution)/shard_map/ppermute | solution.py:40
  69.5 10.9 %copy-start.6 = (s32[6,2]{0,1:T(2,128)S(1)}, s32[6,2]{0,1:T(2,128)}, u32[]{:S(2)}) copy-start(s32[6,2]{0,1:T(2,128)} %param.6) | copy-start | bytes 148
  69.5 2.7 %collective-permute-start.19 = (bf16[3104,128]{1,0:T(8,128)(2,1)}, bf16[3104,128]{1,0:T(8,128)(2,1)}, u32[]{:S(2)}, u32[]{:S(2)}) collective-permute-start(bf16[3104,128]{1,0:T(8,128)(2,1)} %collective-permute-done.12.refs_4_), channel_id=1, source_target_pairs={{0,64},{1,65},{2,66},{3,67},{4,68},{5,69},{6,70},{7,71},{8,72},{9,... | collective-permute-start | bytes 2383880 | tf_op jit(solution)/shard_map/ppermute | solution.py:40
  69.8 3.6 %collective-permute-start.20 = (bf16[3104,128]{1,0:T(8,128)(2,1)}, bf16[3104,128]{1,0:T(8,128)(2,1)}, u32[]{:S(2)}, u32[]{:S(2)}) collective-permute-start(bf16[3104,128]{1,0:T(8,128)(2,1)} %collective-permute-done.13.refs_5_), channel_id=1, source_target_pairs={{0,64},{1,65},{2,66},{3,67},{4,68},{5,69},{6,70},{7,71},{8,72},{9,... | collective-permute-start | bytes 2383880 | tf_op jit(solution)/shard_map/ppermute | solution.py:40
  74.1 5.0 %copy-start.5 = (s32[4,128]{1,0:T(4,128)S(1)}, s32[4,128]{1,0:T(4,128)}, u32[]{:S(2)}) copy-start(s32[4,128]{1,0:T(4,128)} %get-tuple-element.96) | copy-start | bytes 6148
  78.9 44.6 %collective-permute-start.24 = (bf16[12288,128]{1,0:T(8,128)(2,1)}, bf16[12288,128]{1,0:T(8,128)(2,1)S(1)}, u32[]{:S(2)}, u32[]{:S(2)}) collective-permute-start(bf16[12288,128]{1,0:T(8,128)(2,1)} %all-gather.3.cloned.1.call-done.refs_0_), channel_id=1, source_target_pairs={{0,64},{1,65},{2,66},{3,67},{4,68},{5,69},{6,70},{7,71},{8,72},{9,... | collective-permute-start | bytes 9437192 | tf_op jit(solution)/shard_map/ppermute | solution.py:40
  79.1 4.4 %collective-permute-start.21 = (s32[1,128]{1,0:T(1,128)S(1)}, s32[1,128]{1,0:T(1,128)S(1)}, u32[]{:S(2)}, u32[]{:S(2)}) collective-permute-start(s32[1,128]{1,0:T(1,128)S(1)} %get-tuple-element.108), channel_id=1, source_target_pairs={{0,6},{1,7},{2,0},{3,1},{4,2},{5,3},{6,4},{7,5},{8,14},{9,15},{10,... | collective-permute-start | bytes 1544 | tf_op jit(solution)/shard_map/ppermute | solution.py:40
  80.5 5.2 %collective-permute-start.22 = (s32[1,128]{1,0:T(1,128)S(1)}, s32[1,128]{1,0:T(1,128)S(1)}, u32[]{:S(2)}, u32[]{:S(2)}) collective-permute-start(s32[1,128]{1,0:T(1,128)S(1)} %get-tuple-element.110), channel_id=1, source_target_pairs={{0,2},{1,3},{2,4},{3,5},{4,6},{5,7},{6,0},{7,1},{8,10},{9,11},{10,... | collective-permute-start | bytes 1544 | tf_op jit(solution)/shard_map/ppermute | solution.py:40
  80.7 10.6 %collective-permute-start.25 = (bf16[2304,128]{1,0:T(8,128)(2,1)}, bf16[2304,128]{1,0:T(8,128)(2,1)}, u32[]{:S(2)}, u32[]{:S(2)}) collective-permute-start(bf16[2304,128]{1,0:T(8,128)(2,1)} %shard_map.38.refs_2_), channel_id=1, source_target_pairs={{0,1},{1,128},{2,3},{3,130},{4,5},{5,132},{6,7},{7,134},{8,9},{9,1... | collective-permute-start | bytes 1769480 | tf_op jit(solution)/shard_map/ppermute | solution.py:40
  81.0 16.0 %collective-permute-start.26 = (bf16[2304,128]{1,0:T(8,128)(2,1)}, bf16[2304,128]{1,0:T(8,128)(2,1)}, u32[]{:S(2)}, u32[]{:S(2)}) collective-permute-start(bf16[2304,128]{1,0:T(8,128)(2,1)} %shard_map.38.refs_2_), channel_id=1, source_target_pairs={{0,129},{1,0},{2,131},{3,2},{4,133},{5,4},{6,135},{7,6},{8,137},{9... | collective-permute-start | bytes 1769480 | tf_op jit(solution)/shard_map/ppermute | solution.py:40
  83.5 15.3 %collective-permute-start.27 = (bf16[2304,128]{1,0:T(8,128)(2,1)}, bf16[2304,128]{1,0:T(8,128)(2,1)}, u32[]{:S(2)}, u32[]{:S(2)}) collective-permute-start(bf16[2304,128]{1,0:T(8,128)(2,1)} %shard_map.38.refs_2_), channel_id=1, source_target_pairs={{0,128},{1,129},{2,130},{3,131},{4,132},{5,133},{6,134},{7,135},{8... | collective-permute-start | bytes 1769480 | tf_op jit(solution)/shard_map/ppermute | solution.py:40
  85.7 4.1 %collective-permute-start.23 = (s32[1,128]{1,0:T(1,128)S(1)}, s32[1,128]{1,0:T(1,128)S(1)}, u32[]{:S(2)}, u32[]{:S(2)}) collective-permute-start(s32[1,128]{1,0:T(1,128)S(1)} %get-tuple-element.109), channel_id=1, source_target_pairs={{0,4},{1,5},{2,6},{3,7},{4,0},{5,1},{6,2},{7,3},{8,12},{9,13},{10,... | collective-permute-start | bytes 1544 | tf_op jit(solution)/shard_map/ppermute | solution.py:40
  98.8 24.6 %copy-start = (s32[865]{0:T(1024)S(1)}, s32[865]{0:T(1024)}, u32[]{:S(2)}) copy-start(s32[865]{0:T(1024)} %get-tuple-element.97.jobs_ref) | copy-start | bytes 10384
  102.3 12.2 %collective-permute-start = (bf16[2816,128]{1,0:T(8,128)(2,1)}, bf16[2816,128]{1,0:T(8,128)(2,1)}, u32[]{:S(2)}, u32[]{:S(2)}) collective-permute-start(bf16[2816,128]{1,0:T(8,128)(2,1)} %get-tuple-element.44), channel_id=1, source_target_pairs={{0,2},{1,3},{2,4},{3,5},{4,6},{5,7},{6,0},{7,1},{8,10},{9,11},{10,... | collective-permute-start | bytes 2162696 | tf_op jit(solution)/shard_map/cond/branch_1_fun/ppermute | solution.py:40
  102.9 18.7 %collective-permute-start.1 = (bf16[2816,128]{1,0:T(8,128)(2,1)}, bf16[2816,128]{1,0:T(8,128)(2,1)}, u32[]{:S(2)}, u32[]{:S(2)}) collective-permute-start(bf16[2816,128]{1,0:T(8,128)(2,1)} %get-tuple-element.45), channel_id=1, source_target_pairs={{0,6},{1,7},{2,0},{3,1},{4,2},{5,3},{6,4},{7,5},{8,14},{9,15},{10,... | collective-permute-start | bytes 2162696 | tf_op jit(solution)/shard_map/cond/branch_1_fun/ppermute | solution.py:40
  105.3 18.1 %collective-permute-start.2 = (bf16[2816,128]{1,0:T(8,128)(2,1)}, bf16[2816,128]{1,0:T(8,128)(2,1)}, u32[]{:S(2)}, u32[]{:S(2)}) collective-permute-start(bf16[2816,128]{1,0:T(8,128)(2,1)} %get-tuple-element.46), channel_id=1, source_target_pairs={{0,4},{1,5},{2,6},{3,7},{4,0},{5,1},{6,2},{7,3},{8,12},{9,13},{10,... | collective-permute-start | bytes 2162696 | tf_op jit(solution)/shard_map/cond/branch_1_fun/ppermute | solution.py:40
  123.4 11.5 %copy-start.2 = (f32[6,3,128,128]{3,2,1,0:T(8,128)S(1)}, f32[6,3,128,128]{3,2,1,0:T(8,128)}, u32[]{:S(2)}) copy-start(f32[6,3,128,128]{3,2,1,0:T(8,128)} %convert_multiply_fusion) | copy-start | bytes 3538948
  130.2 4.7 %collective-permute-start.28 = (bf16[2304,128]{1,0:T(8,128)(2,1)S(1)}, bf16[2304,128]{1,0:T(8,128)(2,1)S(1)}, u32[]{:S(2)}, u32[]{:S(2)}) collective-permute-start(bf16[2304,128]{1,0:T(8,128)(2,1)S(1)} %get-tuple-element.107), channel_id=1, source_target_pairs={{0,64},{1,65},{2,66},{3,67},{4,68},{5,69},{6,70},{7,71},{8,72},{9,... | collective-permute-start | bytes 1769480 | tf_op jit(solution)/shard_map/ppermute | solution.py:40
  (2 other events, 2.0 us)
Sparse Core Ops, SparseCore 0:
  9.1 48.5 all-gather.2

commit v6 on v5

--- a/solution.py
+++ b/solution.py
@@ -18,7 +18,7 @@
 COUNT, MOST = 32, 33
 PAY = LEFT * BLK + 16
 UNIT = 16
-SLOTS = 64
+SLOTS = 32
 JOBS = 2 * ROWS * 8 * KC
 ALL = ("row", "col", "depth")
 
@@ -271,7 +271,7 @@
             pltpu.VMEM((SLOTS, BLK, BLK), jnp.bfloat16),
             pltpu.SemaphoreType.DMA((2, SLOTS)),
         ],
-        compiler_params=pltpu.CompilerParams(vmem_limit_bytes=10 * 1024 * 1024),
+        compiler_params=pltpu.CompilerParams(vmem_limit_bytes=7 * 1024 * 1024),
     )(most, jobs, *lefts, *rights)
 
 

time: 144 us -> 142 us (0.986)
  starting transfers between devices: 31.1 us -> 29 us
    ppermute x26, starting transfers between devices: 31.1 us -> 29 us  [move(): return lax.ppermute(array, ALL, pairs)]
  transfers between devices with their start and end apart: 27 -> 27, of which waited for: 15 -> 15; matrix products, arithmetic and copies ran while one was open for 7% -> 8% of each run, Pallas kernels for 9% -> 9%
where the time goes in v6:
time: 142 us; the launch traced here: 140 us
  waiting for transfers between devices  44.2 us (31%)
  starting transfers between devices  29 us (20%)
  Pallas kernels  23.7 us (17%)
  blocking collectives  16.9 us (12%)
  between operations  14.1 us (10%)
  other arithmetic  6.68 us (5%)
  local copies, waits for them, and re-layouts  5.58 us (4%)
    ppermute x26, waiting for transfers between devices, move(): return lax.ppermute(array, ALL, pairs)  43.5 us
    ppermute x26, starting transfers between devices, move(): return lax.ppermute(array, ALL, pairs)  29 us
    all_gather x1, blocking collectives, local(): row_marks = lax.all_gather(marks, 'col', axis=0, tiled=True)  16.9 us
    pallas_call x2, Pallas kernels, product(): pl.pallas_call(functools.partial(product_kernel, len(lefts), len(rights))...  10.6 us
    pallas_call x1, Pallas kernels, plan(): pl.pallas_call(plan_kernel, out_shape=(JOB_TABLE, JOB_TABLE, jax.ShapeDty...  9.38 us
    pallas_call x1, Pallas kernels, pack(): pl.pallas_call(pack_kernel, out_shape=(shape,) * 3, in_specs=[SMEM] * 4 +...  3.67 us
  transfers between devices with their start and end apart: 27, of which 15 were waited for; matrix products, arithmetic and copies ran while one was open for 8% of the time, Pallas kernels for 9%

profile of v6, /device:TPU:1, one launch (start us, length us, event | category | flops | bytes accessed | tf_op | source)
XLA Modules:
  0.0 140.1 jit_solution(10702490961074867562)
XLA Ops:
  10.2 2.2 %collective-permute-start.6 = (bf16[1552,128]{1,0:T(8,128)(2,1)S(1)}, bf16[1552,128]{1,0:T(8,128)(2,1)S(1)}, u32[]{:S(2)}, u32[]{:S(2)}) collective-permute-start(bf16[1552,128]{1,0:T(8,128)(2,1)S(1)} %pad_maximum_fusion.1), channel_id=1, source_target_pairs={{0,1},{1,128},{2,3},{3,130},{4,5},{5,132},{6,7},{7,134},{8,9},{9,1... | collective-permute-start | bytes 1191944 | tf_op jit(solution)/shard_map/ppermute | solution.py:40
  12.4 1.5 %collective-permute-start.7 = (bf16[1552,128]{1,0:T(8,128)(2,1)S(1)}, bf16[1552,128]{1,0:T(8,128)(2,1)S(1)}, u32[]{:S(2)}, u32[]{:S(2)}) collective-permute-start(bf16[1552,128]{1,0:T(8,128)(2,1)S(1)} %pad_maximum_fusion.1), channel_id=1, source_target_pairs={{0,129},{1,0},{2,131},{3,2},{4,133},{5,4},{6,135},{7,6},{8,137},{9... | collective-permute-start | bytes 1191944 | tf_op jit(solution)/shard_map/ppermute | solution.py:40
  13.9 1.6 %collective-permute-start.8 = (bf16[1552,128]{1,0:T(8,128)(2,1)S(1)}, bf16[1552,128]{1,0:T(8,128)(2,1)S(1)}, u32[]{:S(2)}, u32[]{:S(2)}) collective-permute-start(bf16[1552,128]{1,0:T(8,128)(2,1)S(1)} %pad_maximum_fusion.1), channel_id=1, source_target_pairs={{0,128},{1,129},{2,130},{3,131},{4,132},{5,133},{6,134},{7,135},{8... | collective-permute-start | bytes 1191944 | tf_op jit(solution)/shard_map/ppermute | solution.py:40
  15.5 3.9 %collective-permute-done.6 = bf16[1552,128]{1,0:T(8,128)(2,1)S(1)} collective-permute-done((bf16[1552,128]{1,0:T(8,128)(2,1)S(1)}, bf16[1552,128]{1,0:T(8,128)(2,1)S(1)}, u32[]{:S(2)}, u32[]{:S(2)}) %collective-permute-start.6) | collective-permute-done | bytes 397344 | tf_op jit(solution)/shard_map/ppermute | solution.py:40
  19.4 3.6 %collective-permute-done.7 = bf16[1552,128]{1,0:T(8,128)(2,1)S(1)} collective-permute-done((bf16[1552,128]{1,0:T(8,128)(2,1)S(1)}, bf16[1552,128]{1,0:T(8,128)(2,1)S(1)}, u32[]{:S(2)}, u32[]{:S(2)}) %collective-permute-start.7) | collective-permute-done | bytes 397344 | tf_op jit(solution)/shard_map/ppermute | solution.py:40
  23.0 1.8 %collective-permute-done.8 = bf16[1552,128]{1,0:T(8,128)(2,1)S(1)} collective-permute-done((bf16[1552,128]{1,0:T(8,128)(2,1)S(1)}, bf16[1552,128]{1,0:T(8,128)(2,1)S(1)}, u32[]{:S(2)}, u32[]{:S(2)}) %collective-permute-start.8) | collective-permute-done | bytes 397344 | tf_op jit(solution)/shard_map/ppermute | solution.py:40
  24.9 2.6 %collective-permute-start.10 = (bf16[6208,128]{1,0:T(8,128)(2,1)S(1)}, bf16[6208,128]{1,0:T(8,128)(2,1)S(1)}, u32[]{:S(2)}, u32[]{:S(2)}) collective-permute-start(bf16[6208,128]{1,0:T(8,128)(2,1)S(1)} %pad_maximum_fusion.refs_1_), channel_id=1, source_target_pairs={{0,6},{1,7},{2,0},{3,1},{4,2},{5,3},{6,4},{7,5},{8,14},{9,15},{10,... | collective-permute-start | bytes 4767752 | tf_op jit(solution)/shard_map/ppermute | solution.py:40
  27.5 1.5 %collective-permute-start.11 = (s32[4,128]{1,0:T(4,128)S(1)}, s32[4,128]{1,0:T(4,128)S(1)}, u32[]{:S(2)}, u32[]{:S(2)}) collective-permute-start(s32[4,128]{1,0:T(4,128)S(1)} %fusion.8), channel_id=1, source_target_pairs={{0,4},{1,5},{2,6},{3,7},{4,0},{5,1},{6,2},{7,3},{8,12},{9,13},{10,... | collective-permute-start | bytes 6152 | tf_op jit(solution)/shard_map/ppermute | solution.py:40
  29.0 16.9 %all-gather = s32[8,1,128]{2,1,0:T(1,128)S(1)} all-gather(s32[1,1,128]{2,1,0:T(1,128)S(1)} %bitcast.38), channel_id=1, replica_groups=mesh['row'=4,'col'=8,'depth'=8] {'col'}, dimensions={0}, use_global_device_ids=true | all-gather | bytes 4608 | tf_op jit(solution)/shard_map/all_gather | solution.py:356
  47.0 1.5 %collective-permute-done.9.refs_2_ = bf16[6208,128]{1,0:T(8,128)(2,1)} collective-permute-done((bf16[6208,128]{1,0:T(8,128)(2,1)S(1)}, bf16[6208,128]{1,0:T(8,128)(2,1)}, u32[]{:S(2)}, u32[]{:S(2)}) %collective-permute-start.9) | collective-permute-done | bytes 1589280 | tf_op jit(solution)/shard_map/ppermute | solution.py:40
  48.5 2.1 %slice.43 = bf16[3104,128]{1,0:T(8,128)(2,1)} slice(bf16[6208,128]{1,0:T(8,128)(2,1)} %collective-permute-done.9.refs_2_), slice={[0:3104], [0:128]} | slice | bytes 1589248 | tf_op jit(solution)/shard_map/slice | solution.py:360
  52.4 2.7 %collective-permute-start.15 = (s32[16,128]{1,0:T(8,128)S(1)}, s32[16,128]{1,0:T(8,128)S(1)}, u32[]{:S(2)}, u32[]{:S(2)}) collective-permute-start(s32[16,128]{1,0:T(8,128)S(1)} %pad_add_fusion), channel_id=1, source_target_pairs={{0,64},{1,65},{2,66},{3,67},{4,68},{5,69},{6,70},{7,71},{8,72},{9,... | collective-permute-start | bytes 24584 | tf_op jit(solution)/shard_map/ppermute | solution.py:40
  55.2 1.1 collective-permute-start.12
  56.4 1.5 %collective-permute-start.13 = (bf16[3104,128]{1,0:T(8,128)(2,1)}, bf16[3104,128]{1,0:T(8,128)(2,1)}, u32[]{:S(2)}, u32[]{:S(2)}) collective-permute-start(bf16[3104,128]{1,0:T(8,128)(2,1)} %slice.44), channel_id=1, source_target_pairs={{0,6},{1,7},{2,0},{3,1},{4,2},{5,3},{6,4},{7,5},{8,14},{9,15},{10,... | collective-permute-start | bytes 2383880 | tf_op jit(solution)/shard_map/ppermute | solution.py:40
  60.1 9.4 %shard_map.37 = (s32[865]{0:T(1024)}, s32[865]{0:T(1024)}, s32[4,128]{1,0:T(4,128)}) custom-call(s32[4]{0:T(128)S(1)} %pad_add_fusion.2.here_ref, s32[8,128]{1,0:T(8,128)} %bitcast.36, s32[8,128]{1,0:T(8,128)} %copy-done.4, s32[16,128]{1,0:T(8,128)} %pad_add_fusion.1.plane_ref), custom_call_target="tpu_custom_call" | custom-call | flops 1000 | bytes 1000 | tf_op jit(solution)/shard_map/pallas_call | solution.py:193
  70.2 2.1 %collective-permute-done.19.refs_9_ = bf16[3104,128]{1,0:T(8,128)(2,1)} collective-permute-done((bf16[3104,128]{1,0:T(8,128)(2,1)}, bf16[3104,128]{1,0:T(8,128)(2,1)}, u32[]{:S(2)}, u32[]{:S(2)}) %collective-permute-start.19) | collective-permute-done | bytes 794656 | tf_op jit(solution)/shard_map/ppermute | solution.py:40
  74.1 4.2 %shard_map.38.refs_2_ = bf16[2304,128]{1,0:T(8,128)(2,1)} custom-call(s32[1]{0:T(128)} %constant.52.clone.1.most_ref, s32[865]{0:T(1024)S(1)} %copy-done.1, bf16[12288,128]{1,0:T(8,128)(2,1)} %all-gather.3.cloned.1.call-done.refs_0_, bf16[6208,128]{1,0:T(8,128)(2,1)S(1)} %pad_maximum_fusion.refs_1_, bf16[6208,128]{1,0:T(8,128)(2,1)} %collective-permute-done.9.refs_2_, ...), custom_call_target="tpu_custom_call" | custom-call | tf_op jit(solution)/shard_map/pallas_call | solution.py:263
  78.4 1.6 %collective-permute-start.21 = (s32[1,128]{1,0:T(1,128)S(1)}, s32[1,128]{1,0:T(1,128)S(1)}, u32[]{:S(2)}, u32[]{:S(2)}) collective-permute-start(s32[1,128]{1,0:T(1,128)S(1)} %get-tuple-element.108), channel_id=1, source_target_pairs={{0,6},{1,7},{2,0},{3,1},{4,2},{5,3},{6,4},{7,5},{8,14},{9,15},{10,... | collective-permute-start | bytes 1544 | tf_op jit(solution)/shard_map/ppermute | solution.py:40
  80.9 2.0 %collective-permute-start.26 = (bf16[2304,128]{1,0:T(8,128)(2,1)}, bf16[2304,128]{1,0:T(8,128)(2,1)}, u32[]{:S(2)}, u32[]{:S(2)}) collective-permute-start(bf16[2304,128]{1,0:T(8,128)(2,1)} %shard_map.38.refs_2_), channel_id=1, source_target_pairs={{0,129},{1,0},{2,131},{3,2},{4,133},{5,4},{6,135},{7,6},{8,137},{9... | collective-permute-start | bytes 1769480 | tf_op jit(solution)/shard_map/ppermute | solution.py:40
  85.1 1.2 collective-permute-start.23
  87.5 1.7 %collective-permute-done.23 = s32[1,128]{1,0:T(1,128)S(1)} collective-permute-done((s32[1,128]{1,0:T(1,128)S(1)}, s32[1,128]{1,0:T(1,128)S(1)}, u32[]{:S(2)}, u32[]{:S(2)}) %collective-permute-start.23) | collective-permute-done | bytes 544 | tf_op jit(solution)/shard_map/ppermute | solution.py:40
  90.8 5.6 %collective-permute-done.26.refs_4_ = bf16[2304,128]{1,0:T(8,128)(2,1)} collective-permute-done((bf16[2304,128]{1,0:T(8,128)(2,1)}, bf16[2304,128]{1,0:T(8,128)(2,1)}, u32[]{:S(2)}, u32[]{:S(2)}) %collective-permute-start.26) | collective-permute-done | bytes 589856 | tf_op jit(solution)/shard_map/ppermute | solution.py:40
  96.5 1.8 %collective-permute-done.27.refs_5_ = bf16[2304,128]{1,0:T(8,128)(2,1)} collective-permute-done((bf16[2304,128]{1,0:T(8,128)(2,1)}, bf16[2304,128]{1,0:T(8,128)(2,1)}, u32[]{:S(2)}, u32[]{:S(2)}) %collective-permute-start.27) | collective-permute-done | bytes 589856 | tf_op jit(solution)/shard_map/ppermute | solution.py:40
  98.2 24.5 %conditional.1 = (bf16[2816,128]{1,0:T(8,128)(2,1)}, bf16[2816,128]{1,0:T(8,128)(2,1)}, bf16[2816,128]{1,0:T(8,128)(2,1)}, bf16[9216,128]{1,0:T(8,128)(2,1)}, bf...) conditional(s32[]{:T(128)} %bitcast.16, (bf16[2304,128]{1,0:T(8,128)(2,1)}, bf16[2304,128]{1,0:T(8,128)(2,1)}, ...), branch_computations={%region_0.1_spmd, %region_1.2_spmd} | conditional | bytes 33030312 | solution.py:334
  98.2 3.7 %branch_1_fun.2 = (bf16[2816,128]{1,0:T(8,128)(2,1)}, bf16[2816,128]{1,0:T(8,128)(2,1)}, bf16[2816,128]{1,0:T(8,128)(2,1)}) custom-call(s32[4]{0:T(128)S(1)} %get-tuple-element.36.here_ref, s32[1,128]{1,0:T(1,128)S(1)} %get-tuple-element.37.refs_0_, s32[1,128]{1,0:T(1,128)S(1)} %get-tuple-element.38.refs_1_, s32[1,128]{1,0:T(1,128)S(1)} %get-tuple-element.39.refs_2_, ...), custom_call_target="tpu_custom_call" | custom-call | tf_op jit(solution)/shard_map/cond/branch_1_fun/pallas_call | solution.py:309
  102.3 2.4 %collective-permute-start.1 = (bf16[2816,128]{1,0:T(8,128)(2,1)}, bf16[2816,128]{1,0:T(8,128)(2,1)}, u32[]{:S(2)}, u32[]{:S(2)}) collective-permute-start(bf16[2816,128]{1,0:T(8,128)(2,1)} %get-tuple-element.45), channel_id=1, source_target_pairs={{0,6},{1,7},{2,0},{3,1},{4,2},{5,3},{6,4},{7,5},{8,14},{9,15},{10,... | collective-permute-start | bytes 2162696 | tf_op jit(solution)/shard_map/cond/branch_1_fun/ppermute | solution.py:40
  105.7 8.3 %collective-permute-done = bf16[2816,128]{1,0:T(8,128)(2,1)} collective-permute-done((bf16[2816,128]{1,0:T(8,128)(2,1)}, bf16[2816,128]{1,0:T(8,128)(2,1)}, u32[]{:S(2)}, u32[]{:S(2)}) %collective-permute-start) | collective-permute-done | bytes 720928 | tf_op jit(solution)/shard_map/cond/branch_1_fun/ppermute | solution.py:40
  113.9 7.0 %collective-permute-done.1 = bf16[2816,128]{1,0:T(8,128)(2,1)} collective-permute-done((bf16[2816,128]{1,0:T(8,128)(2,1)}, bf16[2816,128]{1,0:T(8,128)(2,1)}, u32[]{:S(2)}, u32[]{:S(2)}) %collective-permute-start.1) | collective-permute-done | bytes 720928 | tf_op jit(solution)/shard_map/cond/branch_1_fun/ppermute | solution.py:40
  121.0 1.7 %collective-permute-done.2 = bf16[2816,128]{1,0:T(8,128)(2,1)} collective-permute-done((bf16[2816,128]{1,0:T(8,128)(2,1)}, bf16[2816,128]{1,0:T(8,128)(2,1)}, u32[]{:S(2)}, u32[]{:S(2)}) %collective-permute-start.2) | collective-permute-done | bytes 720928 | tf_op jit(solution)/shard_map/cond/branch_1_fun/ppermute | solution.py:40
  122.7 6.4 %shard_map.39 = (bf16[2304,128]{1,0:T(8,128)(2,1)S(1)}, bf16[2304,128]{1,0:T(8,128)(2,1)S(1)}) custom-call(s32[1]{0:T(128)} %bitcast.15.most_ref, s32[865]{0:T(1024)S(1)} %copy-done, bf16[12288,128]{1,0:T(8,128)(2,1)} %all-gather.3.cloned.1.call-done.refs_0_, bf16[12288,128]{1,0:T(8,128)(2,1)S(1)} %collective-permute-done.24.refs_1_, ...), custom_call_target="tpu_custom_call" | custom-call | tf_op jit(solution)/shard_map/pallas_call | solution.py:263
  129.1 1.5 %collective-permute-start.28 = (bf16[2304,128]{1,0:T(8,128)(2,1)S(1)}, bf16[2304,128]{1,0:T(8,128)(2,1)S(1)}, u32[]{:S(2)}, u32[]{:S(2)}) collective-permute-start(bf16[2304,128]{1,0:T(8,128)(2,1)S(1)} %get-tuple-element.107), channel_id=1, source_target_pairs={{0,64},{1,65},{2,66},{3,67},{4,68},{5,69},{6,70},{7,71},{8,72},{9,... | collective-permute-start | bytes 1769480 | tf_op jit(solution)/shard_map/ppermute | solution.py:40
  130.6 1.6 %collective-permute-done.28 = bf16[2304,128]{1,0:T(8,128)(2,1)S(1)} collective-permute-done((bf16[2304,128]{1,0:T(8,128)(2,1)S(1)}, bf16[2304,128]{1,0:T(8,128)(2,1)S(1)}, u32[]{:S(2)}, u32[]{:S(2)}) %collective-permute-start.28) | collective-permute-done | bytes 589856 | tf_op jit(solution)/shard_map/ppermute | solution.py:40
  (72 shorter events, 19.1 us)
Async XLA Ops:
  6.5 63.6 %all-gather.3.cloned.1.call-start = ((), (), s32[]{:S(2)}) async-start(), calls=%async_computation | async-start | bytes 3538944 | tf_op jit(solution)/shard_map/all_gather | solution.py:349
  10.2 9.1 %collective-permute-start.6 = (bf16[1552,128]{1,0:T(8,128)(2,1)S(1)}, bf16[1552,128]{1,0:T(8,128)(2,1)S(1)}, u32[]{:S(2)}, u32[]{:S(2)}) collective-permute-start(bf16[1552,128]{1,0:T(8,128)(2,1)S(1)} %pad_maximum_fusion.1), channel_id=1, source_target_pairs={{0,1},{1,128},{2,3},{3,130},{4,5},{5,132},{6,7},{7,134},{8,9},{9,1... | collective-permute-start | bytes 1191944 | tf_op jit(solution)/shard_map/ppermute | solution.py:40
  12.4 10.5 %collective-permute-start.7 = (bf16[1552,128]{1,0:T(8,128)(2,1)S(1)}, bf16[1552,128]{1,0:T(8,128)(2,1)S(1)}, u32[]{:S(2)}, u32[]{:S(2)}) collective-permute-start(bf16[1552,128]{1,0:T(8,128)(2,1)S(1)} %pad_maximum_fusion.1), channel_id=1, source_target_pairs={{0,129},{1,0},{2,131},{3,2},{4,133},{5,4},{6,135},{7,6},{8,137},{9... | collective-permute-start | bytes 1191944 | tf_op jit(solution)/shard_map/ppermute | solution.py:40
  13.9 10.8 %collective-permute-start.8 = (bf16[1552,128]{1,0:T(8,128)(2,1)S(1)}, bf16[1552,128]{1,0:T(8,128)(2,1)S(1)}, u32[]{:S(2)}, u32[]{:S(2)}) collective-permute-start(bf16[1552,128]{1,0:T(8,128)(2,1)S(1)} %pad_maximum_fusion.1), channel_id=1, source_target_pairs={{0,128},{1,129},{2,130},{3,131},{4,132},{5,133},{6,134},{7,135},{8... | collective-permute-start | bytes 1191944 | tf_op jit(solution)/shard_map/ppermute | solution.py:40
  24.9 22.1 %collective-permute-start.10 = (bf16[6208,128]{1,0:T(8,128)(2,1)S(1)}, bf16[6208,128]{1,0:T(8,128)(2,1)S(1)}, u32[]{:S(2)}, u32[]{:S(2)}) collective-permute-start(bf16[6208,128]{1,0:T(8,128)(2,1)S(1)} %pad_maximum_fusion.refs_1_), channel_id=1, source_target_pairs={{0,6},{1,7},{2,0},{3,1},{4,2},{5,3},{6,4},{7,5},{8,14},{9,15},{10,... | collective-permute-start | bytes 4767752 | tf_op jit(solution)/shard_map/ppermute | solution.py:40
  27.5 21.1 %collective-permute-start.9 = (bf16[6208,128]{1,0:T(8,128)(2,1)S(1)}, bf16[6208,128]{1,0:T(8,128)(2,1)}, u32[]{:S(2)}, u32[]{:S(2)}) collective-permute-start(bf16[6208,128]{1,0:T(8,128)(2,1)S(1)} %pad_maximum_fusion.refs_1_), channel_id=1, source_target_pairs={{0,2},{1,3},{2,4},{3,5},{4,6},{5,7},{6,0},{7,1},{8,10},{9,11},{10,... | collective-permute-start | bytes 4767752 | tf_op jit(solution)/shard_map/ppermute | solution.py:40
  27.5 19.5 %collective-permute-start.11 = (s32[4,128]{1,0:T(4,128)S(1)}, s32[4,128]{1,0:T(4,128)S(1)}, u32[]{:S(2)}, u32[]{:S(2)}) collective-permute-start(s32[4,128]{1,0:T(4,128)S(1)} %fusion.8), channel_id=1, source_target_pairs={{0,4},{1,5},{2,6},{3,7},{4,0},{5,1},{6,2},{7,3},{8,12},{9,13},{10,... | collective-permute-start | bytes 6152 | tf_op jit(solution)/shard_map/ppermute | solution.py:40
  45.9 14.2 %copy-start.3 = (s32[8,1,128]{2,1,0:T(1,128)}, s32[8,1,128]{2,1,0:T(1,128)S(1)}, u32[]{:S(2)}) copy-start(s32[8,1,128]{2,1,0:T(1,128)S(1)} %all-gather) | copy-start | bytes 12292
  52.4 6.6 %collective-permute-start.15 = (s32[16,128]{1,0:T(8,128)S(1)}, s32[16,128]{1,0:T(8,128)S(1)}, u32[]{:S(2)}, u32[]{:S(2)}) collective-permute-start(s32[16,128]{1,0:T(8,128)S(1)} %pad_add_fusion), channel_id=1, source_target_pairs={{0,64},{1,65},{2,66},{3,67},{4,68},{5,69},{6,70},{7,71},{8,72},{9,... | collective-permute-start | bytes 24584 | tf_op jit(solution)/shard_map/ppermute | solution.py:40
  55.1 3.8 %collective-permute-start.14 = (s32[8,128]{1,0:T(8,128)S(1)}, s32[8,128]{1,0:T(8,128)S(1)}, u32[]{:S(2)}, u32[]{:S(2)}) collective-permute-start(s32[8,128]{1,0:T(8,128)S(1)} %bitcast.35), channel_id=1, source_target_pairs={{0,64},{1,65},{2,66},{3,67},{4,68},{5,69},{6,70},{7,71},{8,72},{9,... | collective-permute-start | bytes 12296 | tf_op jit(solution)/shard_map/ppermute | solution.py:40
  55.2 14.3 %collective-permute-start.12 = (bf16[3104,128]{1,0:T(8,128)(2,1)}, bf16[3104,128]{1,0:T(8,128)(2,1)}, u32[]{:S(2)}, u32[]{:S(2)}) collective-permute-start(bf16[3104,128]{1,0:T(8,128)(2,1)} %slice.43), channel_id=1, source_target_pairs={{0,2},{1,3},{2,4},{3,5},{4,6},{5,7},{6,0},{7,1},{8,10},{9,11},{10,... | collective-permute-start | bytes 2383880 | tf_op jit(solution)/shard_map/ppermute | solution.py:40
  56.4 13.2 %collective-permute-start.13 = (bf16[3104,128]{1,0:T(8,128)(2,1)}, bf16[3104,128]{1,0:T(8,128)(2,1)}, u32[]{:S(2)}, u32[]{:S(2)}) collective-permute-start(bf16[3104,128]{1,0:T(8,128)(2,1)} %slice.44), channel_id=1, source_target_pairs={{0,6},{1,7},{2,0},{3,1},{4,2},{5,3},{6,4},{7,5},{8,14},{9,15},{10,... | collective-permute-start | bytes 2383880 | tf_op jit(solution)/shard_map/ppermute | solution.py:40
  57.9 12.3 %collective-permute-start.16 = (bf16[6208,128]{1,0:T(8,128)(2,1)S(1)}, bf16[6208,128]{1,0:T(8,128)(2,1)}, u32[]{:S(2)}, u32[]{:S(2)}) collective-permute-start(bf16[6208,128]{1,0:T(8,128)(2,1)S(1)} %pad_maximum_fusion.refs_1_), channel_id=1, source_target_pairs={{0,64},{1,65},{2,66},{3,67},{4,68},{5,69},{6,70},{7,71},{8,72},{9,... | collective-permute-start | bytes 4767752 | tf_op jit(solution)/shard_map/ppermute | solution.py:40
  58.9 14.6 %collective-permute-start.17 = (bf16[6208,128]{1,0:T(8,128)(2,1)}, bf16[6208,128]{1,0:T(8,128)(2,1)}, u32[]{:S(2)}, u32[]{:S(2)}) collective-permute-start(bf16[6208,128]{1,0:T(8,128)(2,1)} %collective-permute-done.9.refs_2_), channel_id=1, source_target_pairs={{0,64},{1,65},{2,66},{3,67},{4,68},{5,69},{6,70},{7,71},{8,72},{9,... | collective-permute-start | bytes 4767752 | tf_op jit(solution)/shard_map/ppermute | solution.py:40
  59.0 14.5 %collective-permute-start.18 = (bf16[6208,128]{1,0:T(8,128)(2,1)S(1)}, bf16[6208,128]{1,0:T(8,128)(2,1)}, u32[]{:S(2)}, u32[]{:S(2)}) collective-permute-start(bf16[6208,128]{1,0:T(8,128)(2,1)S(1)} %collective-permute-done.10.refs_3_), channel_id=1, source_target_pairs={{0,64},{1,65},{2,66},{3,67},{4,68},{5,69},{6,70},{7,71},{8,72},{9,... | collective-permute-start | bytes 4767752 | tf_op jit(solution)/shard_map/ppermute | solution.py:40
  69.5 10.5 %copy-start.6 = (s32[6,2]{0,1:T(2,128)S(1)}, s32[6,2]{0,1:T(2,128)}, u32[]{:S(2)}) copy-start(s32[6,2]{0,1:T(2,128)} %param.6) | copy-start | bytes 148
  69.6 2.7 %collective-permute-start.19 = (bf16[3104,128]{1,0:T(8,128)(2,1)}, bf16[3104,128]{1,0:T(8,128)(2,1)}, u32[]{:S(2)}, u32[]{:S(2)}) collective-permute-start(bf16[3104,128]{1,0:T(8,128)(2,1)} %collective-permute-done.12.refs_4_), channel_id=1, source_target_pairs={{0,64},{1,65},{2,66},{3,67},{4,68},{5,69},{6,70},{7,71},{8,72},{9,... | collective-permute-start | bytes 2383880 | tf_op jit(solution)/shard_map/ppermute | solution.py:40
  69.7 3.8 %collective-permute-start.20 = (bf16[3104,128]{1,0:T(8,128)(2,1)}, bf16[3104,128]{1,0:T(8,128)(2,1)}, u32[]{:S(2)}, u32[]{:S(2)}) collective-permute-start(bf16[3104,128]{1,0:T(8,128)(2,1)} %collective-permute-done.13.refs_5_), channel_id=1, source_target_pairs={{0,64},{1,65},{2,66},{3,67},{4,68},{5,69},{6,70},{7,71},{8,72},{9,... | collective-permute-start | bytes 2383880 | tf_op jit(solution)/shard_map/ppermute | solution.py:40
  74.1 4.3 %copy-start.5 = (s32[4,128]{1,0:T(4,128)S(1)}, s32[4,128]{1,0:T(4,128)}, u32[]{:S(2)}) copy-start(s32[4,128]{1,0:T(4,128)} %get-tuple-element.96) | copy-start | bytes 6148
  78.3 44.4 %collective-permute-start.24 = (bf16[12288,128]{1,0:T(8,128)(2,1)}, bf16[12288,128]{1,0:T(8,128)(2,1)S(1)}, u32[]{:S(2)}, u32[]{:S(2)}) collective-permute-start(bf16[12288,128]{1,0:T(8,128)(2,1)} %all-gather.3.cloned.1.call-done.refs_0_), channel_id=1, source_target_pairs={{0,64},{1,65},{2,66},{3,67},{4,68},{5,69},{6,70},{7,71},{8,72},{9,... | collective-permute-start | bytes 9437192 | tf_op jit(solution)/shard_map/ppermute | solution.py:40
  78.4 4.5 %collective-permute-start.21 = (s32[1,128]{1,0:T(1,128)S(1)}, s32[1,128]{1,0:T(1,128)S(1)}, u32[]{:S(2)}, u32[]{:S(2)}) collective-permute-start(s32[1,128]{1,0:T(1,128)S(1)} %get-tuple-element.108), channel_id=1, source_target_pairs={{0,6},{1,7},{2,0},{3,1},{4,2},{5,3},{6,4},{7,5},{8,14},{9,15},{10,... | collective-permute-start | bytes 1544 | tf_op jit(solution)/shard_map/ppermute | solution.py:40
  80.2 4.9 %collective-permute-start.22 = (s32[1,128]{1,0:T(1,128)S(1)}, s32[1,128]{1,0:T(1,128)S(1)}, u32[]{:S(2)}, u32[]{:S(2)}) collective-permute-start(s32[1,128]{1,0:T(1,128)S(1)} %get-tuple-element.110), channel_id=1, source_target_pairs={{0,2},{1,3},{2,4},{3,5},{4,6},{5,7},{6,0},{7,1},{8,10},{9,11},{10,... | collective-permute-start | bytes 1544 | tf_op jit(solution)/shard_map/ppermute | solution.py:40
  80.2 10.6 %collective-permute-start.25 = (bf16[2304,128]{1,0:T(8,128)(2,1)}, bf16[2304,128]{1,0:T(8,128)(2,1)}, u32[]{:S(2)}, u32[]{:S(2)}) collective-permute-start(bf16[2304,128]{1,0:T(8,128)(2,1)} %shard_map.38.refs_2_), channel_id=1, source_target_pairs={{0,1},{1,128},{2,3},{3,130},{4,5},{5,132},{6,7},{7,134},{8,9},{9,1... | collective-permute-start | bytes 1769480 | tf_op jit(solution)/shard_map/ppermute | solution.py:40
  80.9 15.5 %collective-permute-start.26 = (bf16[2304,128]{1,0:T(8,128)(2,1)}, bf16[2304,128]{1,0:T(8,128)(2,1)}, u32[]{:S(2)}, u32[]{:S(2)}) collective-permute-start(bf16[2304,128]{1,0:T(8,128)(2,1)} %shard_map.38.refs_2_), channel_id=1, source_target_pairs={{0,129},{1,0},{2,131},{3,2},{4,133},{5,4},{6,135},{7,6},{8,137},{9... | collective-permute-start | bytes 1769480 | tf_op jit(solution)/shard_map/ppermute | solution.py:40
  83.0 15.3 %collective-permute-start.27 = (bf16[2304,128]{1,0:T(8,128)(2,1)}, bf16[2304,128]{1,0:T(8,128)(2,1)}, u32[]{:S(2)}, u32[]{:S(2)}) collective-permute-start(bf16[2304,128]{1,0:T(8,128)(2,1)} %shard_map.38.refs_2_), channel_id=1, source_target_pairs={{0,128},{1,129},{2,130},{3,131},{4,132},{5,133},{6,134},{7,135},{8... | collective-permute-start | bytes 1769480 | tf_op jit(solution)/shard_map/ppermute | solution.py:40
  85.1 4.1 %collective-permute-start.23 = (s32[1,128]{1,0:T(1,128)S(1)}, s32[1,128]{1,0:T(1,128)S(1)}, u32[]{:S(2)}, u32[]{:S(2)}) collective-permute-start(s32[1,128]{1,0:T(1,128)S(1)} %get-tuple-element.109), channel_id=1, source_target_pairs={{0,4},{1,5},{2,6},{3,7},{4,0},{5,1},{6,2},{7,3},{8,12},{9,13},{10,... | collective-permute-start | bytes 1544 | tf_op jit(solution)/shard_map/ppermute | solution.py:40
  98.2 24.5 %copy-start = (s32[865]{0:T(1024)S(1)}, s32[865]{0:T(1024)}, u32[]{:S(2)}) copy-start(s32[865]{0:T(1024)} %get-tuple-element.97.jobs_ref) | copy-start | bytes 10384
  101.9 12.0 %collective-permute-start = (bf16[2816,128]{1,0:T(8,128)(2,1)}, bf16[2816,128]{1,0:T(8,128)(2,1)}, u32[]{:S(2)}, u32[]{:S(2)}) collective-permute-start(bf16[2816,128]{1,0:T(8,128)(2,1)} %get-tuple-element.44), channel_id=1, source_target_pairs={{0,2},{1,3},{2,4},{3,5},{4,6},{5,7},{6,0},{7,1},{8,10},{9,11},{10,... | collective-permute-start | bytes 2162696 | tf_op jit(solution)/shard_map/cond/branch_1_fun/ppermute | solution.py:40
  102.3 18.7 %collective-permute-start.1 = (bf16[2816,128]{1,0:T(8,128)(2,1)}, bf16[2816,128]{1,0:T(8,128)(2,1)}, u32[]{:S(2)}, u32[]{:S(2)}) collective-permute-start(bf16[2816,128]{1,0:T(8,128)(2,1)} %get-tuple-element.45), channel_id=1, source_target_pairs={{0,6},{1,7},{2,0},{3,1},{4,2},{5,3},{6,4},{7,5},{8,14},{9,15},{10,... | collective-permute-start | bytes 2162696 | tf_op jit(solution)/shard_map/cond/branch_1_fun/ppermute | solution.py:40
  104.6 18.0 %collective-permute-start.2 = (bf16[2816,128]{1,0:T(8,128)(2,1)}, bf16[2816,128]{1,0:T(8,128)(2,1)}, u32[]{:S(2)}, u32[]{:S(2)}) collective-permute-start(bf16[2816,128]{1,0:T(8,128)(2,1)} %get-tuple-element.46), channel_id=1, source_target_pairs={{0,4},{1,5},{2,6},{3,7},{4,0},{5,1},{6,2},{7,3},{8,12},{9,13},{10,... | collective-permute-start | bytes 2162696 | tf_op jit(solution)/shard_map/cond/branch_1_fun/ppermute | solution.py:40
  122.7 9.5 %copy-start.2 = (f32[6,3,128,128]{3,2,1,0:T(8,128)S(1)}, f32[6,3,128,128]{3,2,1,0:T(8,128)}, u32[]{:S(2)}) copy-start(f32[6,3,128,128]{3,2,1,0:T(8,128)} %convert_multiply_fusion) | copy-start | bytes 3538948
  129.1 3.1 %collective-permute-start.28 = (bf16[2304,128]{1,0:T(8,128)(2,1)S(1)}, bf16[2304,128]{1,0:T(8,128)(2,1)S(1)}, u32[]{:S(2)}, u32[]{:S(2)}) collective-permute-start(bf16[2304,128]{1,0:T(8,128)(2,1)S(1)} %get-tuple-element.107), channel_id=1, source_target_pairs={{0,64},{1,65},{2,66},{3,67},{4,68},{5,69},{6,70},{7,71},{8,72},{9,... | collective-permute-start | bytes 1769480 | tf_op jit(solution)/shard_map/ppermute | solution.py:40
  (2 other events, 2.0 us)
Sparse Core Ops, SparseCore 0:
  9.1 48.5 all-gather.2

commit v7 on v6

--- a/solution.py
+++ b/solution.py
@@ -18,7 +18,7 @@
 COUNT, MOST = 32, 33
 PAY = LEFT * BLK + 16
 UNIT = 16
-SLOTS = 32
+SLOTS = 16
 JOBS = 2 * ROWS * 8 * KC
 ALL = ("row", "col", "depth")
 
@@ -271,7 +271,7 @@
             pltpu.VMEM((SLOTS, BLK, BLK), jnp.bfloat16),
             pltpu.SemaphoreType.DMA((2, SLOTS)),
         ],
-        compiler_params=pltpu.CompilerParams(vmem_limit_bytes=7 * 1024 * 1024),
+        compiler_params=pltpu.CompilerParams(vmem_limit_bytes=6 * 1024 * 1024),
     )(most, jobs, *lefts, *rights)
 
 

time: 142 us -> 142 us (level)
  Pallas kernels: 23.7 us -> 20.1 us
  starting transfers between devices: 29 us -> 31.8 us
    ppermute x26, starting transfers between devices: 29 us -> 31.8 us  [move(): return lax.ppermute(array, ALL, pairs)]
    pallas_call x2, Pallas kernels: 10.6 us -> 7.92 us  [product(): pl.pallas_call(functools.partial(product_kernel, len(lefts), len(rights))...]
where the time goes in v7:
time: 142 us; the launch traced here: 139 us
  waiting for transfers between devices  44.2 us (31%)
  starting transfers between devices  31.8 us (22%)
  Pallas kernels  20.1 us (14%)
  blocking collectives  16.9 us (12%)
  between operations  14.1 us (10%)
  other arithmetic  6.68 us (5%)
  local copies, waits for them, and re-layouts  5.59 us (4%)
    ppermute x26, waiting for transfers between devices, move(): return lax.ppermute(array, ALL, pairs)  43.5 us
    ppermute x26, starting transfers between devices, move(): return lax.ppermute(array, ALL, pairs)  31.8 us
    all_gather x1, blocking collectives, local(): row_marks = lax.all_gather(marks, 'col', axis=0, tiled=True)  16.9 us
    pallas_call x1, Pallas kernels, plan(): pl.pallas_call(plan_kernel, out_shape=(JOB_TABLE, JOB_TABLE, jax.ShapeDty...  8.48 us
    pallas_call x2, Pallas kernels, product(): pl.pallas_call(functools.partial(product_kernel, len(lefts), len(rights))...  7.92 us
    pallas_call x1, Pallas kernels, pack(): pl.pallas_call(pack_kernel, out_shape=(shape,) * 3, in_specs=[SMEM] * 4 +...  3.74 us
  transfers between devices with their start and end apart: 27, of which 15 were waited for; matrix products, arithmetic and copies ran while one was open for 8% of the time, Pallas kernels for 9%

profile of v7, /device:TPU:1, one launch (start us, length us, event | category | flops | bytes accessed | tf_op | source)
XLA Modules:
  0.0 139.4 jit_solution(15726627576547834128)
XLA Ops:
  10.2 2.2 %collective-permute-start.6 = (bf16[1552,128]{1,0:T(8,128)(2,1)S(1)}, bf16[1552,128]{1,0:T(8,128)(2,1)S(1)}, u32[]{:S(2)}, u32[]{:S(2)}) collective-permute-start(bf16[1552,128]{1,0:T(8,128)(2,1)S(1)} %pad_maximum_fusion.1), channel_id=1, source_target_pairs={{0,1},{1,128},{2,3},{3,130},{4,5},{5,132},{6,7},{7,134},{8,9},{9,1... | collective-permute-start | bytes 1191944 | tf_op jit(solution)/shard_map/ppermute | solution.py:40
  12.4 1.5 %collective-permute-start.7 = (bf16[1552,128]{1,0:T(8,128)(2,1)S(1)}, bf16[1552,128]{1,0:T(8,128)(2,1)S(1)}, u32[]{:S(2)}, u32[]{:S(2)}) collective-permute-start(bf16[1552,128]{1,0:T(8,128)(2,1)S(1)} %pad_maximum_fusion.1), channel_id=1, source_target_pairs={{0,129},{1,0},{2,131},{3,2},{4,133},{5,4},{6,135},{7,6},{8,137},{9... | collective-permute-start | bytes 1191944 | tf_op jit(solution)/shard_map/ppermute | solution.py:40
  13.9 1.6 %collective-permute-start.8 = (bf16[1552,128]{1,0:T(8,128)(2,1)S(1)}, bf16[1552,128]{1,0:T(8,128)(2,1)S(1)}, u32[]{:S(2)}, u32[]{:S(2)}) collective-permute-start(bf16[1552,128]{1,0:T(8,128)(2,1)S(1)} %pad_maximum_fusion.1), channel_id=1, source_target_pairs={{0,128},{1,129},{2,130},{3,131},{4,132},{5,133},{6,134},{7,135},{8... | collective-permute-start | bytes 1191944 | tf_op jit(solution)/shard_map/ppermute | solution.py:40
  15.5 3.9 %collective-permute-done.6 = bf16[1552,128]{1,0:T(8,128)(2,1)S(1)} collective-permute-done((bf16[1552,128]{1,0:T(8,128)(2,1)S(1)}, bf16[1552,128]{1,0:T(8,128)(2,1)S(1)}, u32[]{:S(2)}, u32[]{:S(2)}) %collective-permute-start.6) | collective-permute-done | bytes 397344 | tf_op jit(solution)/shard_map/ppermute | solution.py:40
  19.4 3.6 %collective-permute-done.7 = bf16[1552,128]{1,0:T(8,128)(2,1)S(1)} collective-permute-done((bf16[1552,128]{1,0:T(8,128)(2,1)S(1)}, bf16[1552,128]{1,0:T(8,128)(2,1)S(1)}, u32[]{:S(2)}, u32[]{:S(2)}) %collective-permute-start.7) | collective-permute-done | bytes 397344 | tf_op jit(solution)/shard_map/ppermute | solution.py:40
  23.0 1.8 %collective-permute-done.8 = bf16[1552,128]{1,0:T(8,128)(2,1)S(1)} collective-permute-done((bf16[1552,128]{1,0:T(8,128)(2,1)S(1)}, bf16[1552,128]{1,0:T(8,128)(2,1)S(1)}, u32[]{:S(2)}, u32[]{:S(2)}) %collective-permute-start.8) | collective-permute-done | bytes 397344 | tf_op jit(solution)/shard_map/ppermute | solution.py:40
  24.9 2.6 %collective-permute-start.10 = (bf16[6208,128]{1,0:T(8,128)(2,1)S(1)}, bf16[6208,128]{1,0:T(8,128)(2,1)S(1)}, u32[]{:S(2)}, u32[]{:S(2)}) collective-permute-start(bf16[6208,128]{1,0:T(8,128)(2,1)S(1)} %pad_maximum_fusion.refs_1_), channel_id=1, source_target_pairs={{0,6},{1,7},{2,0},{3,1},{4,2},{5,3},{6,4},{7,5},{8,14},{9,15},{10,... | collective-permute-start | bytes 4767752 | tf_op jit(solution)/shard_map/ppermute | solution.py:40
  27.5 1.5 %collective-permute-start.11 = (s32[4,128]{1,0:T(4,128)S(1)}, s32[4,128]{1,0:T(4,128)S(1)}, u32[]{:S(2)}, u32[]{:S(2)}) collective-permute-start(s32[4,128]{1,0:T(4,128)S(1)} %fusion.8), channel_id=1, source_target_pairs={{0,4},{1,5},{2,6},{3,7},{4,0},{5,1},{6,2},{7,3},{8,12},{9,13},{10,... | collective-permute-start | bytes 6152 | tf_op jit(solution)/shard_map/ppermute | solution.py:40
  29.0 16.9 %all-gather = s32[8,1,128]{2,1,0:T(1,128)S(1)} all-gather(s32[1,1,128]{2,1,0:T(1,128)S(1)} %bitcast.38), channel_id=1, replica_groups=mesh['row'=4,'col'=8,'depth'=8] {'col'}, dimensions={0}, use_global_device_ids=true | all-gather | bytes 4608 | tf_op jit(solution)/shard_map/all_gather | solution.py:356
  47.0 1.5 %collective-permute-done.9.refs_2_ = bf16[6208,128]{1,0:T(8,128)(2,1)} collective-permute-done((bf16[6208,128]{1,0:T(8,128)(2,1)S(1)}, bf16[6208,128]{1,0:T(8,128)(2,1)}, u32[]{:S(2)}, u32[]{:S(2)}) %collective-permute-start.9) | collective-permute-done | bytes 1589280 | tf_op jit(solution)/shard_map/ppermute | solution.py:40
  48.5 2.1 %slice.43 = bf16[3104,128]{1,0:T(8,128)(2,1)} slice(bf16[6208,128]{1,0:T(8,128)(2,1)} %collective-permute-done.9.refs_2_), slice={[0:3104], [0:128]} | slice | bytes 1589248 | tf_op jit(solution)/shard_map/slice | solution.py:360
  52.4 2.7 %collective-permute-start.15 = (s32[16,128]{1,0:T(8,128)S(1)}, s32[16,128]{1,0:T(8,128)S(1)}, u32[]{:S(2)}, u32[]{:S(2)}) collective-permute-start(s32[16,128]{1,0:T(8,128)S(1)} %pad_add_fusion), channel_id=1, source_target_pairs={{0,64},{1,65},{2,66},{3,67},{4,68},{5,69},{6,70},{7,71},{8,72},{9,... | collective-permute-start | bytes 24584 | tf_op jit(solution)/shard_map/ppermute | solution.py:40
  55.2 1.1 collective-permute-start.12
  56.4 1.5 %collective-permute-start.13 = (bf16[3104,128]{1,0:T(8,128)(2,1)}, bf16[3104,128]{1,0:T(8,128)(2,1)}, u32[]{:S(2)}, u32[]{:S(2)}) collective-permute-start(bf16[3104,128]{1,0:T(8,128)(2,1)} %slice.44), channel_id=1, source_target_pairs={{0,6},{1,7},{2,0},{3,1},{4,2},{5,3},{6,4},{7,5},{8,14},{9,15},{10,... | collective-permute-start | bytes 2383880 | tf_op jit(solution)/shard_map/ppermute | solution.py:40
  60.1 8.5 %shard_map.37 = (s32[865]{0:T(1024)}, s32[865]{0:T(1024)}, s32[4,128]{1,0:T(4,128)}) custom-call(s32[4]{0:T(128)S(1)} %pad_add_fusion.2.here_ref, s32[8,128]{1,0:T(8,128)} %bitcast.36, s32[8,128]{1,0:T(8,128)} %copy-done.4, s32[16,128]{1,0:T(8,128)} %pad_add_fusion.1.plane_ref), custom_call_target="tpu_custom_call" | custom-call | flops 1000 | bytes 1000 | tf_op jit(solution)/shard_map/pallas_call | solution.py:193
  69.5 2.1 %collective-permute-done.19.refs_9_ = bf16[3104,128]{1,0:T(8,128)(2,1)} collective-permute-done((bf16[3104,128]{1,0:T(8,128)(2,1)}, bf16[3104,128]{1,0:T(8,128)(2,1)}, u32[]{:S(2)}, u32[]{:S(2)}) %collective-permute-start.19) | collective-permute-done | bytes 794656 | tf_op jit(solution)/shard_map/ppermute | solution.py:40
  73.4 3.3 %shard_map.38.refs_2_ = bf16[2304,128]{1,0:T(8,128)(2,1)} custom-call(s32[1]{0:T(128)} %constant.52.clone.1.most_ref, s32[865]{0:T(1024)S(1)} %copy-done.1, bf16[12288,128]{1,0:T(8,128)(2,1)} %all-gather.3.cloned.1.call-done.refs_0_, bf16[6208,128]{1,0:T(8,128)(2,1)S(1)} %pad_maximum_fusion.refs_1_, bf16[6208,128]{1,0:T(8,128)(2,1)} %collective-permute-done.9.refs_2_, ...), custom_call_target="tpu_custom_call" | custom-call | tf_op jit(solution)/shard_map/pallas_call | solution.py:263
  77.3 3.6 %collective-permute-start.21 = (s32[1,128]{1,0:T(1,128)S(1)}, s32[1,128]{1,0:T(1,128)S(1)}, u32[]{:S(2)}, u32[]{:S(2)}) collective-permute-start(s32[1,128]{1,0:T(1,128)S(1)} %get-tuple-element.108), channel_id=1, source_target_pairs={{0,6},{1,7},{2,0},{3,1},{4,2},{5,3},{6,4},{7,5},{8,14},{9,15},{10,... | collective-permute-start | bytes 1544 | tf_op jit(solution)/shard_map/ppermute | solution.py:40
  81.1 2.7 %collective-permute-start.26 = (bf16[2304,128]{1,0:T(8,128)(2,1)}, bf16[2304,128]{1,0:T(8,128)(2,1)}, u32[]{:S(2)}, u32[]{:S(2)}) collective-permute-start(bf16[2304,128]{1,0:T(8,128)(2,1)} %shard_map.38.refs_2_), channel_id=1, source_target_pairs={{0,129},{1,0},{2,131},{3,2},{4,133},{5,4},{6,135},{7,6},{8,137},{9... | collective-permute-start | bytes 1769480 | tf_op jit(solution)/shard_map/ppermute | solution.py:40
  85.3 1.2 collective-permute-start.23
  87.6 1.7 %collective-permute-done.23 = s32[1,128]{1,0:T(1,128)S(1)} collective-permute-done((s32[1,128]{1,0:T(1,128)S(1)}, s32[1,128]{1,0:T(1,128)S(1)}, u32[]{:S(2)}, u32[]{:S(2)}) %collective-permute-start.23) | collective-permute-done | bytes 544 | tf_op jit(solution)/shard_map/ppermute | solution.py:40
  90.4 1.2 collective-permute-done.25.refs_3_
  91.6 5.6 %collective-permute-done.26.refs_4_ = bf16[2304,128]{1,0:T(8,128)(2,1)} collective-permute-done((bf16[2304,128]{1,0:T(8,128)(2,1)}, bf16[2304,128]{1,0:T(8,128)(2,1)}, u32[]{:S(2)}, u32[]{:S(2)}) %collective-permute-start.26) | collective-permute-done | bytes 589856 | tf_op jit(solution)/shard_map/ppermute | solution.py:40
  98.3 24.5 %conditional.1 = (bf16[2816,128]{1,0:T(8,128)(2,1)}, bf16[2816,128]{1,0:T(8,128)(2,1)}, bf16[2816,128]{1,0:T(8,128)(2,1)}, bf16[9216,128]{1,0:T(8,128)(2,1)}, bf...) conditional(s32[]{:T(128)} %bitcast.16, (bf16[2304,128]{1,0:T(8,128)(2,1)}, bf16[2304,128]{1,0:T(8,128)(2,1)}, ...), branch_computations={%region_0.1_spmd, %region_1.2_spmd} | conditional | bytes 33030312 | solution.py:334
  98.3 3.7 %branch_1_fun.2 = (bf16[2816,128]{1,0:T(8,128)(2,1)}, bf16[2816,128]{1,0:T(8,128)(2,1)}, bf16[2816,128]{1,0:T(8,128)(2,1)}) custom-call(s32[4]{0:T(128)S(1)} %get-tuple-element.36.here_ref, s32[1,128]{1,0:T(1,128)S(1)} %get-tuple-element.37.refs_0_, s32[1,128]{1,0:T(1,128)S(1)} %get-tuple-element.38.refs_1_, s32[1,128]{1,0:T(1,128)S(1)} %get-tuple-element.39.refs_2_, ...), custom_call_target="tpu_custom_call" | custom-call | tf_op jit(solution)/shard_map/cond/branch_1_fun/pallas_call | solution.py:309
  102.2 2.7 %collective-permute-start.1 = (bf16[2816,128]{1,0:T(8,128)(2,1)}, bf16[2816,128]{1,0:T(8,128)(2,1)}, u32[]{:S(2)}, u32[]{:S(2)}) collective-permute-start(bf16[2816,128]{1,0:T(8,128)(2,1)} %get-tuple-element.45), channel_id=1, source_target_pairs={{0,6},{1,7},{2,0},{3,1},{4,2},{5,3},{6,4},{7,5},{8,14},{9,15},{10,... | collective-permute-start | bytes 2162696 | tf_op jit(solution)/shard_map/cond/branch_1_fun/ppermute | solution.py:40
  105.8 8.3 %collective-permute-done = bf16[2816,128]{1,0:T(8,128)(2,1)} collective-permute-done((bf16[2816,128]{1,0:T(8,128)(2,1)}, bf16[2816,128]{1,0:T(8,128)(2,1)}, u32[]{:S(2)}, u32[]{:S(2)}) %collective-permute-start) | collective-permute-done | bytes 720928 | tf_op jit(solution)/shard_map/cond/branch_1_fun/ppermute | solution.py:40
  114.1 7.0 %collective-permute-done.1 = bf16[2816,128]{1,0:T(8,128)(2,1)} collective-permute-done((bf16[2816,128]{1,0:T(8,128)(2,1)}, bf16[2816,128]{1,0:T(8,128)(2,1)}, u32[]{:S(2)}, u32[]{:S(2)}) %collective-permute-start.1) | collective-permute-done | bytes 720928 | tf_op jit(solution)/shard_map/cond/branch_1_fun/ppermute | solution.py:40
  121.1 1.7 %collective-permute-done.2 = bf16[2816,128]{1,0:T(8,128)(2,1)} collective-permute-done((bf16[2816,128]{1,0:T(8,128)(2,1)}, bf16[2816,128]{1,0:T(8,128)(2,1)}, u32[]{:S(2)}, u32[]{:S(2)}) %collective-permute-start.2) | collective-permute-done | bytes 720928 | tf_op jit(solution)/shard_map/cond/branch_1_fun/ppermute | solution.py:40
  122.8 4.6 %shard_map.39 = (bf16[2304,128]{1,0:T(8,128)(2,1)S(1)}, bf16[2304,128]{1,0:T(8,128)(2,1)S(1)}) custom-call(s32[1]{0:T(128)} %bitcast.15.most_ref, s32[865]{0:T(1024)S(1)} %copy-done, bf16[12288,128]{1,0:T(8,128)(2,1)} %all-gather.3.cloned.1.call-done.refs_0_, bf16[12288,128]{1,0:T(8,128)(2,1)S(1)} %collective-permute-done.24.refs_1_, ...), custom_call_target="tpu_custom_call" | custom-call | tf_op jit(solution)/shard_map/pallas_call | solution.py:263
  127.4 2.4 %collective-permute-start.28 = (bf16[2304,128]{1,0:T(8,128)(2,1)S(1)}, bf16[2304,128]{1,0:T(8,128)(2,1)S(1)}, u32[]{:S(2)}, u32[]{:S(2)}) collective-permute-start(bf16[2304,128]{1,0:T(8,128)(2,1)S(1)} %get-tuple-element.107), channel_id=1, source_target_pairs={{0,64},{1,65},{2,66},{3,67},{4,68},{5,69},{6,70},{7,71},{8,72},{9,... | collective-permute-start | bytes 1769480 | tf_op jit(solution)/shard_map/ppermute | solution.py:40
  129.8 1.6 %collective-permute-done.28 = bf16[2304,128]{1,0:T(8,128)(2,1)S(1)} collective-permute-done((bf16[2304,128]{1,0:T(8,128)(2,1)S(1)}, bf16[2304,128]{1,0:T(8,128)(2,1)S(1)}, u32[]{:S(2)}, u32[]{:S(2)}) %collective-permute-start.28) | collective-permute-done | bytes 589856 | tf_op jit(solution)/shard_map/ppermute | solution.py:40
  (72 shorter events, 18.7 us)
Async XLA Ops:
  6.5 63.0 %all-gather.3.cloned.1.call-start = ((), (), s32[]{:S(2)}) async-start(), calls=%async_computation | async-start | bytes 3538944 | tf_op jit(solution)/shard_map/all_gather | solution.py:349
  10.2 9.1 %collective-permute-start.6 = (bf16[1552,128]{1,0:T(8,128)(2,1)S(1)}, bf16[1552,128]{1,0:T(8,128)(2,1)S(1)}, u32[]{:S(2)}, u32[]{:S(2)}) collective-permute-start(bf16[1552,128]{1,0:T(8,128)(2,1)S(1)} %pad_maximum_fusion.1), channel_id=1, source_target_pairs={{0,1},{1,128},{2,3},{3,130},{4,5},{5,132},{6,7},{7,134},{8,9},{9,1... | collective-permute-start | bytes 1191944 | tf_op jit(solution)/shard_map/ppermute | solution.py:40
  12.4 10.5 %collective-permute-start.7 = (bf16[1552,128]{1,0:T(8,128)(2,1)S(1)}, bf16[1552,128]{1,0:T(8,128)(2,1)S(1)}, u32[]{:S(2)}, u32[]{:S(2)}) collective-permute-start(bf16[1552,128]{1,0:T(8,128)(2,1)S(1)} %pad_maximum_fusion.1), channel_id=1, source_target_pairs={{0,129},{1,0},{2,131},{3,2},{4,133},{5,4},{6,135},{7,6},{8,137},{9... | collective-permute-start | bytes 1191944 | tf_op jit(solution)/shard_map/ppermute | solution.py:40
  13.9 10.8 %collective-permute-start.8 = (bf16[1552,128]{1,0:T(8,128)(2,1)S(1)}, bf16[1552,128]{1,0:T(8,128)(2,1)S(1)}, u32[]{:S(2)}, u32[]{:S(2)}) collective-permute-start(bf16[1552,128]{1,0:T(8,128)(2,1)S(1)} %pad_maximum_fusion.1), channel_id=1, source_target_pairs={{0,128},{1,129},{2,130},{3,131},{4,132},{5,133},{6,134},{7,135},{8... | collective-permute-start | bytes 1191944 | tf_op jit(solution)/shard_map/ppermute | solution.py:40
  24.9 22.1 %collective-permute-start.10 = (bf16[6208,128]{1,0:T(8,128)(2,1)S(1)}, bf16[6208,128]{1,0:T(8,128)(2,1)S(1)}, u32[]{:S(2)}, u32[]{:S(2)}) collective-permute-start(bf16[6208,128]{1,0:T(8,128)(2,1)S(1)} %pad_maximum_fusion.refs_1_), channel_id=1, source_target_pairs={{0,6},{1,7},{2,0},{3,1},{4,2},{5,3},{6,4},{7,5},{8,14},{9,15},{10,... | collective-permute-start | bytes 4767752 | tf_op jit(solution)/shard_map/ppermute | solution.py:40
  27.5 21.1 %collective-permute-start.9 = (bf16[6208,128]{1,0:T(8,128)(2,1)S(1)}, bf16[6208,128]{1,0:T(8,128)(2,1)}, u32[]{:S(2)}, u32[]{:S(2)}) collective-permute-start(bf16[6208,128]{1,0:T(8,128)(2,1)S(1)} %pad_maximum_fusion.refs_1_), channel_id=1, source_target_pairs={{0,2},{1,3},{2,4},{3,5},{4,6},{5,7},{6,0},{7,1},{8,10},{9,11},{10,... | collective-permute-start | bytes 4767752 | tf_op jit(solution)/shard_map/ppermute | solution.py:40
  27.5 19.5 %collective-permute-start.11 = (s32[4,128]{1,0:T(4,128)S(1)}, s32[4,128]{1,0:T(4,128)S(1)}, u32[]{:S(2)}, u32[]{:S(2)}) collective-permute-start(s32[4,128]{1,0:T(4,128)S(1)} %fusion.8), channel_id=1, source_target_pairs={{0,4},{1,5},{2,6},{3,7},{4,0},{5,1},{6,2},{7,3},{8,12},{9,13},{10,... | collective-permute-start | bytes 6152 | tf_op jit(solution)/shard_map/ppermute | solution.py:40
  45.9 14.2 %copy-start.3 = (s32[8,1,128]{2,1,0:T(1,128)}, s32[8,1,128]{2,1,0:T(1,128)S(1)}, u32[]{:S(2)}) copy-start(s32[8,1,128]{2,1,0:T(1,128)S(1)} %all-gather) | copy-start | bytes 12292
  52.4 6.6 %collective-permute-start.15 = (s32[16,128]{1,0:T(8,128)S(1)}, s32[16,128]{1,0:T(8,128)S(1)}, u32[]{:S(2)}, u32[]{:S(2)}) collective-permute-start(s32[16,128]{1,0:T(8,128)S(1)} %pad_add_fusion), channel_id=1, source_target_pairs={{0,64},{1,65},{2,66},{3,67},{4,68},{5,69},{6,70},{7,71},{8,72},{9,... | collective-permute-start | bytes 24584 | tf_op jit(solution)/shard_map/ppermute | solution.py:40
  55.1 3.8 %collective-permute-start.14 = (s32[8,128]{1,0:T(8,128)S(1)}, s32[8,128]{1,0:T(8,128)S(1)}, u32[]{:S(2)}, u32[]{:S(2)}) collective-permute-start(s32[8,128]{1,0:T(8,128)S(1)} %bitcast.35), channel_id=1, source_target_pairs={{0,64},{1,65},{2,66},{3,67},{4,68},{5,69},{6,70},{7,71},{8,72},{9,... | collective-permute-start | bytes 12296 | tf_op jit(solution)/shard_map/ppermute | solution.py:40
  55.2 13.4 %collective-permute-start.12 = (bf16[3104,128]{1,0:T(8,128)(2,1)}, bf16[3104,128]{1,0:T(8,128)(2,1)}, u32[]{:S(2)}, u32[]{:S(2)}) collective-permute-start(bf16[3104,128]{1,0:T(8,128)(2,1)} %slice.43), channel_id=1, source_target_pairs={{0,2},{1,3},{2,4},{3,5},{4,6},{5,7},{6,0},{7,1},{8,10},{9,11},{10,... | collective-permute-start | bytes 2383880 | tf_op jit(solution)/shard_map/ppermute | solution.py:40
  56.4 12.3 %collective-permute-start.13 = (bf16[3104,128]{1,0:T(8,128)(2,1)}, bf16[3104,128]{1,0:T(8,128)(2,1)}, u32[]{:S(2)}, u32[]{:S(2)}) collective-permute-start(bf16[3104,128]{1,0:T(8,128)(2,1)} %slice.44), channel_id=1, source_target_pairs={{0,6},{1,7},{2,0},{3,1},{4,2},{5,3},{6,4},{7,5},{8,14},{9,15},{10,... | collective-permute-start | bytes 2383880 | tf_op jit(solution)/shard_map/ppermute | solution.py:40
  57.9 11.6 %collective-permute-start.16 = (bf16[6208,128]{1,0:T(8,128)(2,1)S(1)}, bf16[6208,128]{1,0:T(8,128)(2,1)}, u32[]{:S(2)}, u32[]{:S(2)}) collective-permute-start(bf16[6208,128]{1,0:T(8,128)(2,1)S(1)} %pad_maximum_fusion.refs_1_), channel_id=1, source_target_pairs={{0,64},{1,65},{2,66},{3,67},{4,68},{5,69},{6,70},{7,71},{8,72},{9,... | collective-permute-start | bytes 4767752 | tf_op jit(solution)/shard_map/ppermute | solution.py:40
  58.9 13.9 %collective-permute-start.17 = (bf16[6208,128]{1,0:T(8,128)(2,1)}, bf16[6208,128]{1,0:T(8,128)(2,1)}, u32[]{:S(2)}, u32[]{:S(2)}) collective-permute-start(bf16[6208,128]{1,0:T(8,128)(2,1)} %collective-permute-done.9.refs_2_), channel_id=1, source_target_pairs={{0,64},{1,65},{2,66},{3,67},{4,68},{5,69},{6,70},{7,71},{8,72},{9,... | collective-permute-start | bytes 4767752 | tf_op jit(solution)/shard_map/ppermute | solution.py:40
  59.0 13.8 %collective-permute-start.18 = (bf16[6208,128]{1,0:T(8,128)(2,1)S(1)}, bf16[6208,128]{1,0:T(8,128)(2,1)}, u32[]{:S(2)}, u32[]{:S(2)}) collective-permute-start(bf16[6208,128]{1,0:T(8,128)(2,1)S(1)} %collective-permute-done.10.refs_3_), channel_id=1, source_target_pairs={{0,64},{1,65},{2,66},{3,67},{4,68},{5,69},{6,70},{7,71},{8,72},{9,... | collective-permute-start | bytes 4767752 | tf_op jit(solution)/shard_map/ppermute | solution.py:40
  68.7 12.2 %copy-start.6 = (s32[6,2]{0,1:T(2,128)S(1)}, s32[6,2]{0,1:T(2,128)}, u32[]{:S(2)}) copy-start(s32[6,2]{0,1:T(2,128)} %param.6) | copy-start | bytes 148
  68.7 2.9 %collective-permute-start.19 = (bf16[3104,128]{1,0:T(8,128)(2,1)}, bf16[3104,128]{1,0:T(8,128)(2,1)}, u32[]{:S(2)}, u32[]{:S(2)}) collective-permute-start(bf16[3104,128]{1,0:T(8,128)(2,1)} %collective-permute-done.12.refs_4_), channel_id=1, source_target_pairs={{0,64},{1,65},{2,66},{3,67},{4,68},{5,69},{6,70},{7,71},{8,72},{9,... | collective-permute-start | bytes 2383880 | tf_op jit(solution)/shard_map/ppermute | solution.py:40
  69.3 3.4 %collective-permute-start.20 = (bf16[3104,128]{1,0:T(8,128)(2,1)}, bf16[3104,128]{1,0:T(8,128)(2,1)}, u32[]{:S(2)}, u32[]{:S(2)}) collective-permute-start(bf16[3104,128]{1,0:T(8,128)(2,1)} %collective-permute-done.13.refs_5_), channel_id=1, source_target_pairs={{0,64},{1,65},{2,66},{3,67},{4,68},{5,69},{6,70},{7,71},{8,72},{9,... | collective-permute-start | bytes 2383880 | tf_op jit(solution)/shard_map/ppermute | solution.py:40
  73.4 3.9 %copy-start.5 = (s32[4,128]{1,0:T(4,128)S(1)}, s32[4,128]{1,0:T(4,128)}, u32[]{:S(2)}) copy-start(s32[4,128]{1,0:T(4,128)} %get-tuple-element.96) | copy-start | bytes 6148
  76.8 46.0 %collective-permute-start.24 = (bf16[12288,128]{1,0:T(8,128)(2,1)}, bf16[12288,128]{1,0:T(8,128)(2,1)S(1)}, u32[]{:S(2)}, u32[]{:S(2)}) collective-permute-start(bf16[12288,128]{1,0:T(8,128)(2,1)} %all-gather.3.cloned.1.call-done.refs_0_), channel_id=1, source_target_pairs={{0,64},{1,65},{2,66},{3,67},{4,68},{5,69},{6,70},{7,71},{8,72},{9,... | collective-permute-start | bytes 9437192 | tf_op jit(solution)/shard_map/ppermute | solution.py:40
  77.3 6.5 %collective-permute-start.21 = (s32[1,128]{1,0:T(1,128)S(1)}, s32[1,128]{1,0:T(1,128)S(1)}, u32[]{:S(2)}, u32[]{:S(2)}) collective-permute-start(s32[1,128]{1,0:T(1,128)S(1)} %get-tuple-element.108), channel_id=1, source_target_pairs={{0,6},{1,7},{2,0},{3,1},{4,2},{5,3},{6,4},{7,5},{8,14},{9,15},{10,... | collective-permute-start | bytes 1544 | tf_op jit(solution)/shard_map/ppermute | solution.py:40
  81.0 4.2 %collective-permute-start.22 = (s32[1,128]{1,0:T(1,128)S(1)}, s32[1,128]{1,0:T(1,128)S(1)}, u32[]{:S(2)}, u32[]{:S(2)}) collective-permute-start(s32[1,128]{1,0:T(1,128)S(1)} %get-tuple-element.110), channel_id=1, source_target_pairs={{0,2},{1,3},{2,4},{3,5},{4,6},{5,7},{6,0},{7,1},{8,10},{9,11},{10,... | collective-permute-start | bytes 1544 | tf_op jit(solution)/shard_map/ppermute | solution.py:40
  81.0 10.6 %collective-permute-start.25 = (bf16[2304,128]{1,0:T(8,128)(2,1)}, bf16[2304,128]{1,0:T(8,128)(2,1)}, u32[]{:S(2)}, u32[]{:S(2)}) collective-permute-start(bf16[2304,128]{1,0:T(8,128)(2,1)} %shard_map.38.refs_2_), channel_id=1, source_target_pairs={{0,1},{1,128},{2,3},{3,130},{4,5},{5,132},{6,7},{7,134},{8,9},{9,1... | collective-permute-start | bytes 1769480 | tf_op jit(solution)/shard_map/ppermute | solution.py:40
  81.1 16.1 %collective-permute-start.26 = (bf16[2304,128]{1,0:T(8,128)(2,1)}, bf16[2304,128]{1,0:T(8,128)(2,1)}, u32[]{:S(2)}, u32[]{:S(2)}) collective-permute-start(bf16[2304,128]{1,0:T(8,128)(2,1)} %shard_map.38.refs_2_), channel_id=1, source_target_pairs={{0,129},{1,0},{2,131},{3,2},{4,133},{5,4},{6,135},{7,6},{8,137},{9... | collective-permute-start | bytes 1769480 | tf_op jit(solution)/shard_map/ppermute | solution.py:40
  83.8 14.6 %collective-permute-start.27 = (bf16[2304,128]{1,0:T(8,128)(2,1)}, bf16[2304,128]{1,0:T(8,128)(2,1)}, u32[]{:S(2)}, u32[]{:S(2)}) collective-permute-start(bf16[2304,128]{1,0:T(8,128)(2,1)} %shard_map.38.refs_2_), channel_id=1, source_target_pairs={{0,128},{1,129},{2,130},{3,131},{4,132},{5,133},{6,134},{7,135},{8... | collective-permute-start | bytes 1769480 | tf_op jit(solution)/shard_map/ppermute | solution.py:40
  85.3 4.1 %collective-permute-start.23 = (s32[1,128]{1,0:T(1,128)S(1)}, s32[1,128]{1,0:T(1,128)S(1)}, u32[]{:S(2)}, u32[]{:S(2)}) collective-permute-start(s32[1,128]{1,0:T(1,128)S(1)} %get-tuple-element.109), channel_id=1, source_target_pairs={{0,4},{1,5},{2,6},{3,7},{4,0},{5,1},{6,2},{7,3},{8,12},{9,13},{10,... | collective-permute-start | bytes 1544 | tf_op jit(solution)/shard_map/ppermute | solution.py:40
  98.3 24.5 %copy-start = (s32[865]{0:T(1024)S(1)}, s32[865]{0:T(1024)}, u32[]{:S(2)}) copy-start(s32[865]{0:T(1024)} %get-tuple-element.97.jobs_ref) | copy-start | bytes 10384
  102.1 12.0 %collective-permute-start = (bf16[2816,128]{1,0:T(8,128)(2,1)}, bf16[2816,128]{1,0:T(8,128)(2,1)}, u32[]{:S(2)}, u32[]{:S(2)}) collective-permute-start(bf16[2816,128]{1,0:T(8,128)(2,1)} %get-tuple-element.44), channel_id=1, source_target_pairs={{0,2},{1,3},{2,4},{3,5},{4,6},{5,7},{6,0},{7,1},{8,10},{9,11},{10,... | collective-permute-start | bytes 2162696 | tf_op jit(solution)/shard_map/cond/branch_1_fun/ppermute | solution.py:40
  102.2 18.9 %collective-permute-start.1 = (bf16[2816,128]{1,0:T(8,128)(2,1)}, bf16[2816,128]{1,0:T(8,128)(2,1)}, u32[]{:S(2)}, u32[]{:S(2)}) collective-permute-start(bf16[2816,128]{1,0:T(8,128)(2,1)} %get-tuple-element.45), channel_id=1, source_target_pairs={{0,6},{1,7},{2,0},{3,1},{4,2},{5,3},{6,4},{7,5},{8,14},{9,15},{10,... | collective-permute-start | bytes 2162696 | tf_op jit(solution)/shard_map/cond/branch_1_fun/ppermute | solution.py:40
  104.9 18.0 %collective-permute-start.2 = (bf16[2816,128]{1,0:T(8,128)(2,1)}, bf16[2816,128]{1,0:T(8,128)(2,1)}, u32[]{:S(2)}, u32[]{:S(2)}) collective-permute-start(bf16[2816,128]{1,0:T(8,128)(2,1)} %get-tuple-element.46), channel_id=1, source_target_pairs={{0,4},{1,5},{2,6},{3,7},{4,0},{5,1},{6,2},{7,3},{8,12},{9,13},{10,... | collective-permute-start | bytes 2162696 | tf_op jit(solution)/shard_map/cond/branch_1_fun/ppermute | solution.py:40
  122.8 8.7 %copy-start.2 = (f32[6,3,128,128]{3,2,1,0:T(8,128)S(1)}, f32[6,3,128,128]{3,2,1,0:T(8,128)}, u32[]{:S(2)}) copy-start(f32[6,3,128,128]{3,2,1,0:T(8,128)} %convert_multiply_fusion) | copy-start | bytes 3538948
  127.4 4.1 %collective-permute-start.28 = (bf16[2304,128]{1,0:T(8,128)(2,1)S(1)}, bf16[2304,128]{1,0:T(8,128)(2,1)S(1)}, u32[]{:S(2)}, u32[]{:S(2)}) collective-permute-start(bf16[2304,128]{1,0:T(8,128)(2,1)S(1)} %get-tuple-element.107), channel_id=1, source_target_pairs={{0,64},{1,65},{2,66},{3,67},{4,68},{5,69},{6,70},{7,71},{8,72},{9,... | collective-permute-start | bytes 1769480 | tf_op jit(solution)/shard_map/ppermute | solution.py:40
  (2 other events, 2.0 us)
Sparse Core Ops, SparseCore 0:
  9.1 48.5 all-gather.2
